TPU v7x, 128 devices: a whole 4x4x4 slice. The times are simulated.
128 devices in a mesh: row: 8 (over z, core), col: 16 (over y, x).
Axes of the slice: x: 4, y: 4, z: 4, core: 2. Of those that a mesh axis runs over, the one named last changes fastest.
Arguments:
- normed: bfloat16 [512, 8192], P('row', 'col'), may hold values from -6 to 6
- w_in: bfloat16 [8192, 32768], P('col', 'row'), may hold values from -0.0625 to 0.0625
- w_out: bfloat16 [32768, 8192], P('row', 'col'), may hold values from -0.03125 to 0.03125
- d_out: bfloat16 [512, 8192], P('row', 'col'), may hold values from -6 to 6
Outputs:
- ffn_out: bfloat16 [512, 8192], P('row', 'col')
- d_normed: bfloat16 [512, 8192], P('row', 'col')
- grad_in: bfloat16 [8192, 32768], P('col', 'row')
- grad_out: bfloat16 [32768, 8192], P('row', 'col')
All inputs are finite; a program needn't handle non-finite values.
Results may differ from a plain program's by a relative error of at most 0.029.
Values may be sent and summed in bfloat16 or wider, within the bound.
No kernel may reach another device: no remote copies, remote signals or barrier semaphores. Data moves between devices by JAX's collectives and lax.ppermute only.
A program may use at most 128 MiB of HBM per device.

v0:
```python
import jax
import jax.numpy as jnp
from jax import lax
from jax.sharding import PartitionSpec as P


def gelu_tanh(value):
    inner = 0.7978845608 * (value + 0.044715 * value * value * value)
    return 0.5 * value * (1.0 + jnp.tanh(inner))


def gelu_slope(value):
    tangent = jnp.tanh(0.7978845608 * (value + 0.044715 * value * value * value))
    return 0.5 * (1.0 + tangent) + 0.5 * value * (1.0 - tangent * tangent) * 0.7978845608 * (
        1.0 + 3.0 * 0.044715 * value * value
    )


def shards(normed, w_in, w_out, d_out):
    inputs, cotangent = (
        lax.all_gather(normed, "row", axis=0, tiled=True),
        lax.all_gather(d_out, "row", axis=0, tiled=True),
    )
    window = inputs
    preact = lax.psum(
        jnp.dot(window, w_in, preferred_element_type=jnp.float32).astype(jnp.bfloat16), "col"
    ).astype(jnp.float32)
    act_all = gelu_tanh(preact).astype(jnp.bfloat16)
    window = cotangent
    d_act = lax.psum(
        lax.dot_general(
            window, w_out, (((1,), (1,)), ((), ())), preferred_element_type=jnp.float32
        ).astype(jnp.bfloat16),
        "col",
    ).astype(jnp.float32)
    d_pre = (d_act * gelu_slope(preact)).astype(jnp.bfloat16)
    window = act_all
    ffn_out = lax.psum_scatter(
        jnp.dot(window, w_out, preferred_element_type=jnp.float32).astype(jnp.bfloat16),
        "row",
        scatter_dimension=0,
        tiled=True,
    )
    grad_out = lax.dot_general(
        act_all, cotangent, (((0,), (0,)), ((), ())), preferred_element_type=jnp.float32
    ).astype(jnp.bfloat16)
    grad_in = lax.dot_general(
        inputs, d_pre, (((0,), (0,)), ((), ())), preferred_element_type=jnp.float32
    ).astype(jnp.bfloat16)
    window = d_pre
    d_normed = lax.psum_scatter(
        lax.dot_general(
            window, w_in, (((1,), (1,)), ((), ())), preferred_element_type=jnp.float32
        ).astype(jnp.bfloat16),
        "row",
        scatter_dimension=0,
        tiled=True,
    )
    return (ffn_out, d_normed, grad_in, grad_out)


def solution(mesh):
    return jax.shard_map(
        shards,
        mesh=mesh,
        in_specs=(P("row", "col"), P("col", "row"), P("row", "col"), P("row", "col")),
        out_specs=(P("row", "col"), P("row", "col"), P("col", "row"), P("row", "col")),
        check_vma=False,
    )
```

profile of v0, /device:TPU:1, one launch (start us, length us, event | category | flops | bytes accessed | tf_op | source)
XLA Modules:
  0.0 270.1 jit_solution(11021103015644143860)
XLA Ops:
  7.2 0.0 all-reduce.3.cloned.1.call-start
  7.2 15.9 %all_gather.6 = bf16[512,512]{1,0:T(8,128)(2,1)S(1)} all-gather(bf16[64,512]{1,0:T(8,128)(2,1)} %param.4), channel_id=1, replica_groups=mesh['row'=8,'col'=16] {'row'}, dimensions={0}, use_global_device_ids=true | all-gather | bytes 589824 | tf_op jit(solution)/shard_map/all_gather | solution.py:21
  23.1 13.3 %all_gather.7 = bf16[512,512]{1,0:T(8,128)(2,1)S(1)} all-gather(bf16[64,512]{1,0:T(8,128)(2,1)} %param.7), channel_id=1, replica_groups=mesh['row'=8,'col'=16] {'row'}, dimensions={0}, use_global_device_ids=true | all-gather | bytes 589824 | tf_op jit(solution)/shard_map/all_gather | solution.py:22
  36.4 0.0 copy-start.1
  36.4 6.7 %convolution_convert_fusion.2 = bf16[512,4096]{1,0:T(8,128)(2,1)} fusion(bf16[512,512]{1,0:T(8,128)(2,1)S(1)} %all_gather.7, bf16[4096,512]{1,0:T(8,128)(2,1)} %param.6), kind=kOutput, calls=%fused_computation.20 | convolution fusion | flops 2149580800 | bytes 8912896 | tf_op jit(solution)/shard_map/dot_general | solution.py:31
  43.1 0.0 copy-done.1
  43.1 4.4 %convolution_convert_fusion.3 = bf16[512,4096]{1,0:T(8,128)(2,1)} fusion(bf16[512,512]{1,0:T(8,128)(2,1)S(1)} %all_gather.6, bf16[512,4096]{1,0:T(8,128)(2,1)S(1)} %copy-done.1), kind=kOutput, calls=%fused_computation.21 | convolution fusion | flops 2149580800 | bytes 8912896 | tf_op jit(solution)/shard_map/dot_general | solution.py:26
  47.5 0.0 all-reduce.3.cloned.1.call-update
  47.6 0.0 reduce-scatter.5.cloned.1.call-start
  47.6 141.9 %all-reduce.3.cloned.1.call-done = (bf16[512,4096]{1,0:T(8,128)(2,1)}, bf16[512,4096]{1,0:T(8,128)(2,1)}) async-done(((bf16[512,4096]{1,0:T(8,128)(2,1)}, bf16[512,4096]{1,0:T(8,128)(2,1)}), (bf16[512,4096]{1,0:T(8,128)(2,1)}, bf16[512,4096]{1,0:T(8,128)(2,1)})) %all-reduce.3.cloned.1.call-update) | async-done | bytes 8388624 | tf_op jit(solution)/shard_map/psum | solution.py:25
  189.6 0.0 copy-start.2
  189.6 8.2 %fusion.7 = bf16[512,4096]{1,0:T(8,128)(2,1)S(1)} fusion(bf16[512,4096]{1,0:T(8,128)(2,1)} %get-tuple-element.8, bf16[512,4096]{1,0:T(8,128)(2,1)} %get-tuple-element.9), kind=kLoop, calls=%fused_computation.14 | loop fusion | flops 44040192 | bytes 12582912 | tf_op jit(solution)/shard_map/convert_element_type | solution.py:36
  197.8 0.0 copy-start
  197.8 2.0 copy-done
  199.8 0.0 copy-done.2
  199.8 3.2 %convolution_convert_fusion.4 = bf16[512,512]{1,0:T(8,128)(2,1)} fusion(bf16[512,4096]{1,0:T(8,128)(2,1)S(1)} %fusion.7, bf16[512,4096]{1,0:T(8,128)(2,1)S(1)} %copy-done.2), kind=kOutput, calls=%fused_computation.23 | convolution fusion | flops 2147745792 | bytes 8912896 | tf_op jit(solution)/shard_map/dot_general | solution.py:52
  203.0 0.0 reduce-scatter.5.cloned.1.call-update
  203.0 0.2 reduce-scatter.3.cloned.1.call-start
  203.3 7.4 %convolution_convert_fusion.5 = bf16[512,512]{1,0:T(8,128)(2,1)} fusion(bf16[4096,512]{1,0:T(8,128)(2,1)} %param.6, bf16[512,4096]{1,0:T(8,128)(2,1)} %get-tuple-element.8), kind=kOutput, calls=%fused_computation.24 | convolution fusion | flops 2168717312 | bytes 8912896 | tf_op jit(solution)/shard_map/dot_general | solution.py:39
  210.6 0.0 reduce-scatter.3.cloned.1.call-update
  210.7 6.6 %fusion.11 = bf16[512,4096]{0,1:T(8,128)(2,1)} fusion(bf16[512,4096]{1,0:T(8,128)(2,1)} %copy-done, bf16[512,512]{1,0:T(8,128)(2,1)S(1)} %all_gather.6), kind=kOutput, calls=%fused_computation.22 | convolution fusion | flops 2149580800 | bytes 8912896 | tf_op jit(solution)/shard_map/dot_general | solution.py:47
  217.3 6.3 %copy.8 = bf16[512,4096]{1,0:T(8,128)(2,1)} copy(bf16[512,4096]{0,1:T(8,128)(2,1)} %fusion.11) | data formatting | bytes 8388608
  223.6 8.8 %convolution_convert_fusion = bf16[4096,512]{1,0:T(8,128)(2,1)} fusion(bf16[512,512]{1,0:T(8,128)(2,1)S(1)} %all_gather.7, bf16[512,4096]{1,0:T(8,128)(2,1)} %get-tuple-element.8), kind=kOutput, calls=%fused_computation.18 | convolution fusion | flops 2170552320 | bytes 8912896 | tf_op jit(solution)/shard_map/dot_general | solution.py:44
  232.4 0.0 reduce-scatter.5.cloned.1.call-done
  232.4 31.2 %reduce-scatter.3.cloned.1.call-done = bf16[64,512]{1,0:T(8,128)(2,1)} async-done(((bf16[512,512]{1,0:T(8,128)(2,1)}), bf16[64,512]{1,0:T(8,128)(2,1)}) %reduce-scatter.3.cloned.1.call-update) | async-done | bytes 65552 | tf_op jit(solution)/shard_map/reduce_scatter | solution.py:38
Async XLA Ops:
  7.2 182.4 %all-reduce.3.cloned.1.call-start = ((), (), s32[]{:S(2)}) async-start(), calls=%async_computation.4 | async-start | bytes 16777216 | tf_op jit(solution)/shard_map/psum | solution.py:25
  36.4 6.7 %copy-start.1 = (bf16[512,4096]{1,0:T(8,128)(2,1)S(1)}, bf16[512,4096]{1,0:T(8,128)(2,1)}, u32[]{:S(2)}) copy-start(bf16[512,4096]{1,0:T(8,128)(2,1)} %param.5) | copy-start | bytes 12582916
  47.6 184.8 %reduce-scatter.5.cloned.1.call-start = ((), (), s32[]{:S(2)}) async-start(), calls=%async_computation.3 | async-start | bytes 589824 | tf_op jit(solution)/shard_map/reduce_scatter | solution.py:51
  189.6 10.3 %copy-start.2 = (bf16[512,4096]{1,0:T(8,128)(2,1)S(1)}, bf16[512,4096]{1,0:T(8,128)(2,1)}, u32[]{:S(2)}) copy-start(bf16[512,4096]{1,0:T(8,128)(2,1)} %param.5) | copy-start | bytes 12582916
  197.8 2.0 copy-start
  203.0 60.6 %reduce-scatter.3.cloned.1.call-start = ((), (), s32[]{:S(2)}) async-start(), calls=%async_computation.2 | async-start | bytes 589824 | tf_op jit(solution)/shard_map/reduce_scatter | solution.py:38
Sparse Core Ops, SparseCore 0:
  47.7 141.8 all-reduce.2
  203.1 27.6 reduce-scatter.4
  233.8 29.7 reduce-scatter.2
where the time goes:
time: 273 us; the launch traced here: 270 us
  waiting for transfers between devices  173 us (63%)
  matrix products  37.1 us (14%)
  blocking collectives  29.2 us (11%)
  between operations  13.8 us (5%)
  local copies, waits for them, and re-layouts  8.35 us (3%)
  other arithmetic  8.23 us (3%)
    psum x1, waiting for transfers between devices, shards(): lax.psum(jnp.dot(window, w_in, preferred_element_type=jnp.float32).astype...  142 us
    reduce_scatter x1, waiting for transfers between devices, shards(): lax.psum_scatter(jnp.dot(window, w_out, preferred_element_type=jnp.float3...  31.2 us
    all_gather x1, blocking collectives, shards(): lax.all_gather(normed, 'row', axis=0, tiled=True)  15.9 us
    all_gather x1, blocking collectives, shards(): lax.all_gather(d_out, 'row', axis=0, tiled=True)  13.3 us
    dot_general x1, matrix products, shards(): lax.dot_general(act_all, cotangent, (((0,), (0,)), ((), ())), preferred_e...  8.79 us
    unnamed x7, local copies, waits for them, and re-layouts  8.35 us
    convert_element_type x1, other arithmetic, shards(): d_pre = (d_act * gelu_slope(preact)).astype(jnp.bfloat16)  8.23 us
    dot_general x1, matrix products, shards(): jnp.dot(window, w_out, preferred_element_type=jnp.float32)  7.38 us
  transfers between devices with their start and end apart: 3, of which 2 were waited for; matrix products, arithmetic and copies ran while one was open for 11% of the time, Pallas kernels for 0%

commit v1 on v0

v1 whole, which is shorter than its diff:
```python
import functools

import jax
import jax.numpy as jnp
from jax import lax
from jax.experimental import pallas as pl
from jax.experimental.pallas import tpu as pltpu
from jax.sharding import PartitionSpec as P

BOTH = ("row", "col")
F32, BF16 = jnp.float32, jnp.bfloat16
WIDE = 256
LIMIT = 48 * 1024 * 1024


def gelu_tanh(value):
    inner = 0.7978845608 * (value + 0.044715 * value * value * value)
    return 0.5 * value * (1.0 + jnp.tanh(inner))


def gelu_slope(value):
    tangent = jnp.tanh(0.7978845608 * (value + 0.044715 * value * value * value))
    return 0.5 * (1.0 + tangent) + 0.5 * value * (1.0 - tangent * tangent) * 0.7978845608 * (
        1.0 + 3.0 * 0.044715 * value * value
    )


GRAY = (0, 1, 3, 2)
UNGRAY = (0, 1, 3, 2)


def pairs(move):
    listed = []
    for z in range(4):
        for core in range(2):
            for y in range(4):
                for x in range(4):
                    tz, tcore, ty, tx = move(z, core, y, x)
                    listed.append(
                        ((z * 2 + core) * 16 + y * 4 + x, (tz * 2 + tcore) * 16 + ty * 4 + tx)
                    )
    return listed


def flip(position, bit):
    return UNGRAY[GRAY[position] ^ (1 << bit)]


PRIMARY = [
    pairs(
        lambda z, core, y, x, bit=bit: (z, core, y, flip(x, bit))
        if core == 0
        else (z, core, flip(y, bit), x)
    )
    for bit in range(2)
]
SECONDARY = [
    pairs(lambda z, core, y, x, k=k: (z, core, y ^ k, x) if core == 0 else (z, core, y, x ^ k))
    for k in range(4)
]
ALONG_Z = [pairs(lambda z, core, y, x, k=k: (z ^ k, core, y, x)) for k in range(4)]
CORES = pairs(lambda z, core, y, x: (z, 1 - core, y, x))


def send(block, perm):
    return lax.ppermute(block, BOTH, perm)


def gray(position):
    return jnp.bitwise_xor(position, jnp.right_shift(position, 1))


def places():
    row, col = lax.axis_index("row"), lax.axis_index("col")
    core, y, x = row % 2, col // 4, col % 4
    primary = gray(jnp.where(core == 0, x, y))
    secondary = jnp.where(core == 0, y, x)
    low, high = primary % 2, primary // 2
    return jnp.stack([low * 8 + high * 4 + secondary, high * 8 + low * 4 + secondary]).astype(
        jnp.int32
    )


def weight_block(transposed, part, first, step, me):
    pair = jnp.bitwise_xor(first + step, jnp.right_shift(me[part], 1)) + 8 * part
    return (pair, 0) if transposed else (0, pair)


def weight_spec(transposed, depth, index):
    return pl.BlockSpec((WIDE, depth) if transposed else (depth, WIDE), index)


def produce_body(transposed, part_of, me, x_ref, w_ref, *outs):
    if transposed:
        term = lax.dot_general(
            x_ref[...], w_ref[...], (((1,), (1,)), ((), ())), preferred_element_type=F32
        )
    else:
        term = jnp.dot(x_ref[...], w_ref[...], preferred_element_type=F32)
    term = term.astype(BF16)

    def put(out, part):
        odd = me[part] % 2
        out[odd] = term[:, : WIDE // 2]
        out[1 - odd] = term[:, WIDE // 2 :]

    if part_of is not None:
        put(outs[0], part_of)
    else:
        for part in range(2):
            pl.when(pl.program_id(0) == part)(functools.partial(put, outs[part], part))


def produce(x, w, me, transposed, part, first):
    tokens, depth = x.shape
    shape = jax.ShapeDtypeStruct((8, tokens, WIDE // 2), BF16)
    block = (2, tokens, WIDE // 2)
    if part is not None:
        grid = (4,)
        w_index = lambda j, me: weight_block(transposed, part, first, j, me)
        x_index = lambda j, me: (0, 0)
        out_specs = [pl.BlockSpec(block, lambda j, me: (j, 0, 0))]
    else:
        grid = (2, 4)
        w_index = lambda i, j, me: weight_block(transposed, i, first, j, me)
        x_index = lambda i, j, me: (0, 0)
        out_specs = [
            pl.BlockSpec(block, lambda i, j, me: (jnp.where(i == 0, j, 3), 0, 0)),
            pl.BlockSpec(block, lambda i, j, me: (jnp.where(i == 0, 0, j), 0, 0)),
        ]
    count = len(out_specs)
    return pl.pallas_call(
        functools.partial(produce_body, transposed, part),
        out_shape=[shape] * count,
        grid_spec=pltpu.PrefetchScalarGridSpec(
            num_scalar_prefetch=1,
            grid=grid,
            in_specs=[
                pl.BlockSpec((tokens, depth), x_index),
                weight_spec(transposed, depth, w_index),
            ],
            out_specs=out_specs,
        ),
        compiler_params=pltpu.CompilerParams(vmem_limit_bytes=LIMIT),
        cost_estimate=pl.CostEstimate(
            flops=2 * tokens * depth * 4 * WIDE * count,
            bytes_accessed=2 * (tokens * depth + 4 * WIDE * (depth + tokens) * count),
            transcendentals=0,
        ),
    )(me, x, w)


def consume_body(transposed, has_total, me, a_ref, b_ref, w_ref, y_ref, *rest):
    if has_total:
        total_in, unused_grad, total, grad = rest
    else:
        total, grad = rest
    i, j = pl.program_id(0), pl.program_id(1)

    @pl.when((i == 0) & (j == 0))
    def start():
        total[...] = total_in[...] if has_total else jnp.zeros_like(total)

    def step(ref, part):
        odd = me[part] % 2
        block = jnp.concatenate([ref[odd], ref[1 - odd]], axis=1)
        if transposed:
            total[...] += jnp.dot(block, w_ref[...], preferred_element_type=F32)
            grad[...] = lax.dot_general(
                block, y_ref[...], (((0,), (0,)), ((), ())), preferred_element_type=F32
            ).astype(BF16)
        else:
            total[...] += lax.dot_general(
                block, w_ref[...], (((1,), (1,)), ((), ())), preferred_element_type=F32
            )
            grad[...] = jnp.dot(y_ref[...], block, preferred_element_type=F32).astype(BF16)

    for part, ref in enumerate((a_ref, b_ref)):
        pl.when(i == part)(functools.partial(step, ref, part))


def consume(a, b, w, y, me, transposed, first, before):
    tokens, depth = y.shape
    block = (2, tokens, WIDE // 2)
    w_index = lambda i, j, me: weight_block(transposed, i, first, j, me)
    whole = lambda i, j, me: (0, 0)
    in_specs = [
        pl.BlockSpec(block, lambda i, j, me: (jnp.where(i == 0, j, 3), 0, 0)),
        pl.BlockSpec(block, lambda i, j, me: (jnp.where(i == 0, 0, j), 0, 0)),
        weight_spec(transposed, depth, w_index),
        pl.BlockSpec(y.shape, whole),
    ]
    operands = [me, a, b, w, y]
    aliases = {}
    if before is not None:
        in_specs += [pl.BlockSpec((tokens, depth), whole), pl.BlockSpec(memory_space=pl.ANY)]
        operands += list(before)
        aliases = {5: 0, 6: 1}
    return pl.pallas_call(
        functools.partial(consume_body, transposed, before is not None),
        out_shape=[
            jax.ShapeDtypeStruct((tokens, depth), F32),
            jax.ShapeDtypeStruct(w.shape, BF16),
        ],
        grid_spec=pltpu.PrefetchScalarGridSpec(
            num_scalar_prefetch=1,
            grid=(2, 4),
            in_specs=in_specs,
            out_specs=[
                pl.BlockSpec((tokens, depth), whole),
                weight_spec(transposed, depth, w_index),
            ],
        ),
        input_output_aliases=aliases,
        compiler_params=pltpu.CompilerParams(vmem_limit_bytes=LIMIT),
        cost_estimate=pl.CostEstimate(
            flops=4 * tokens * depth * 8 * WIDE,
            bytes_accessed=2 * (3 * tokens * depth + 8 * WIDE * (2 * depth + tokens)),
            transcendentals=0,
        ),
    )(*operands)


def add(*terms):
    total = terms[0].astype(F32)
    for term in terms[1:]:
        total = total + term.astype(F32)
    return total


def gather_rows(block):
    along = jnp.concatenate([block] + [send(block, ALONG_Z[k]) for k in (1, 3, 2)], axis=0)
    return jnp.concatenate([along, send(along, CORES)], axis=0)


def scatter_rows(total):
    half = total.shape[0] // 2
    other = send(total[half:].astype(BF16), CORES)
    kept = add(total[:half], other)
    rows = half // 4
    sent = [kept[rows * n : rows * (n + 1)].astype(BF16) for n in range(1, 4)]
    got = [send(sent[n], ALONG_Z[k]) for n, k in enumerate((1, 3, 2))]
    return add(kept[:rows], *got).astype(BF16)


def reduce_hidden(x, w, me, transposed):
    (far_a,) = produce(x, w, me, transposed, 0, 4)
    got_a = send(far_a, PRIMARY[0])
    (far_b,) = produce(x, w, me, transposed, 1, 4)
    got_b = send(far_b, PRIMARY[1])
    near_a, near_b = produce(x, w, me, transposed, None, 0)
    next_a = send(add(near_a[4:], got_a[4:]).astype(BF16), PRIMARY[1])
    next_b = send(add(near_b[4:], got_b[4:]).astype(BF16), PRIMARY[0])
    four_a = add(near_a[:4], got_a[:4], next_a)
    four_b = add(near_b[:4], got_b[:4], next_b)
    own = jnp.stack([four_a[0], four_b[0]])
    last = [
        send(jnp.stack([four_a[k], four_b[k]]).astype(BF16), SECONDARY[k]) for k in (1, 3, 2)
    ]
    return add(own, *last)


def spread_hidden(own):
    one, three, two = (send(own, SECONDARY[k]) for k in (1, 3, 2))
    four = [jnp.stack([own[h], one[h], two[h], three[h]]) for h in range(2)]
    near = [
        jnp.concatenate([four[h], send(four[h], PRIMARY[1 - h])], axis=0) for h in range(2)
    ]
    far = [send(near[h], PRIMARY[h]) for h in range(2)]
    return near, far


def shards(normed, w_in, w_out, d_out):
    me = places()
    inputs = gather_rows(normed)
    cotangent = gather_rows(d_out)
    preact = reduce_hidden(inputs, w_in, me, False)
    act = gelu_tanh(preact).astype(BF16)
    d_act = reduce_hidden(cotangent, w_out, me, True)
    near, far = spread_hidden(act)
    d_pre = (d_act * gelu_slope(preact)).astype(BF16)
    d_near, d_far = spread_hidden(d_pre)
    first = consume(near[0], near[1], w_out, cotangent, me, True, 0, None)
    ffn_total, grad_out = consume(far[0], far[1], w_out, cotangent, me, True, 4, first)
    ffn_out = scatter_rows(ffn_total)
    turned = inputs.T
    first = consume(d_near[0], d_near[1], w_in, turned, me, False, 0, None)
    d_total, grad_in = consume(d_far[0], d_far[1], w_in, turned, me, False, 4, first)
    d_normed = scatter_rows(d_total)
    return (ffn_out, d_normed, grad_in, grad_out)


def solution(mesh):
    return jax.shard_map(
        shards,
        mesh=mesh,
        in_specs=(P("row", "col"), P("col", "row"), P("row", "col"), P("row", "col")),
        out_specs=(P("row", "col"), P("row", "col"), P("col", "row"), P("row", "col")),
        check_vma=False,
    )
```

time: 273 us -> 167 us (0.61)
  waiting for transfers between devices: 173 us -> 40.8 us
  starting transfers between devices: 0.3 us -> 55.5 us
  Pallas kernels: 0 us -> 52.4 us
  matrix products: 37.1 us -> 0 us
  blocking collectives: 29.2 us -> 0 us
  between operations: 13.8 us -> 1.09 us
    psum x1 -> x0, waiting for transfers between devices: 142 us -> none  [shards(): lax.psum(jnp.dot(window, w_in, preferred_element_type=jnp.float32).astype...]
    ppermute x0 -> x44, starting transfers between devices: none -> 55.5 us  [send(): return lax.ppermute(block, BOTH, perm)]
    pallas_call x0 -> x10, Pallas kernels: none -> 52.4 us  [the longest x4 32 us: consume(): pl.pallas_call(functools.partial(consume_body, transposed, before is not...]
    ppermute x0 -> x44, waiting for transfers between devices: none -> 40.8 us  [send(): return lax.ppermute(block, BOTH, perm)]
    dot_general x6 -> x0, matrix products: 37.1 us -> none  [the longest x1 8.79 us: shards(): lax.dot_general(act_all, cotangent, (((0,), (0,)), ((), ())), preferred_e...]
    reduce_scatter x2 -> x0, waiting for transfers between devices: 31.2 us -> none  [the longest x1 31.2 us: shards(): lax.psum_scatter(jnp.dot(window, w_out, preferred_element_type=jnp.float3...]
    all_gather x2 -> x0, blocking collectives: 29.2 us -> none  [the longest x1 15.9 us: shards(): lax.all_gather(normed, 'row', axis=0, tiled=True)]
    unnamed x7 -> x9, local copies, waits for them, and re-layouts: 8.35 us -> 4 us
  transfers between devices with their start and end apart: 3 -> 44, of which waited for: 2 -> 18; matrix products, arithmetic and copies ran while one was open for 11% -> 6% of each run, Pallas kernels for 0% -> 32%
where the time goes in v1:
time: 167 us; the launch traced here: 165 us
  starting transfers between devices  55.5 us (33%)
  Pallas kernels  52.4 us (31%)
  waiting for transfers between devices  40.8 us (24%)
  other arithmetic  9.2 us (6%)
  local copies, waits for them, and re-layouts  5.8 us (3%)
    ppermute x44, starting transfers between devices, send(): return lax.ppermute(block, BOTH, perm)  55.5 us
    ppermute x44, waiting for transfers between devices, send(): return lax.ppermute(block, BOTH, perm)  40.8 us
    pallas_call x4, Pallas kernels, consume(): pl.pallas_call(functools.partial(consume_body, transposed, before is not...  32 us
    pallas_call x6, Pallas kernels, produce(): pl.pallas_call(functools.partial(produce_body, transposed, part), out_sha...  20.4 us
    unnamed x9, local copies, waits for them, and re-layouts  4 us
  transfers between devices with their start and end apart: 44, of which 18 were waited for; matrix products, arithmetic and copies ran while one was open for 6% of the time, Pallas kernels for 32%

profile of v1, /device:TPU:1, one launch (start us, length us, event | category | flops | bytes accessed | tf_op | source)
XLA Modules:
  0.0 164.8 jit_solution(149440239724460958)
XLA Ops:
  1.6 2.5 %collective-permute-start = (bf16[64,512]{0,1:T(8,128)(2,1)S(1)}, bf16[64,512]{0,1:T(8,128)(2,1)S(1)}, u32[]{:S(2)}, u32[]{:S(2)}) collective-permute-start(bf16[64,512]{0,1:T(8,128)(2,1)S(1)} %copy.16), channel_id=1, source_target_pairs={{0,32},{1,33},{2,34},{3,35},{4,36},{5,37},{6,38},{7,39},{8,40},{9,... | collective-permute-start | bytes 196616 | tf_op jit(solution)/shard_map/ppermute | solution.py:66
  4.1 2.2 %collective-permute-start.1 = (bf16[64,512]{0,1:T(8,128)(2,1)S(1)}, bf16[64,512]{0,1:T(8,128)(2,1)S(1)}, u32[]{:S(2)}, u32[]{:S(2)}) collective-permute-start(bf16[64,512]{0,1:T(8,128)(2,1)S(1)} %copy.16), channel_id=1, source_target_pairs={{0,96},{1,97},{2,98},{3,99},{4,100},{5,101},{6,102},{7,103},{8,104... | collective-permute-start | bytes 196616 | tf_op jit(solution)/shard_map/ppermute | solution.py:66
  7.4 2.2 %collective-permute-start.19 = (bf16[64,512]{1,0:T(8,128)(2,1)}, bf16[64,512]{1,0:T(8,128)(2,1)S(1)}, u32[]{:S(2)}, u32[]{:S(2)}) collective-permute-start(bf16[64,512]{1,0:T(8,128)(2,1)} %param.7), channel_id=1, source_target_pairs={{0,96},{1,97},{2,98},{3,99},{4,100},{5,101},{6,102},{7,103},{8,104... | collective-permute-start | bytes 196616 | tf_op jit(solution)/shard_map/ppermute | solution.py:66
  10.7 2.7 %collective-permute-done.2 = bf16[64,512]{0,1:T(8,128)(2,1)S(1)} collective-permute-done((bf16[64,512]{0,1:T(8,128)(2,1)S(1)}, bf16[64,512]{0,1:T(8,128)(2,1)S(1)}, u32[]{:S(2)}, u32[]{:S(2)}) %collective-permute-start.2) | collective-permute-done | bytes 65568 | tf_op jit(solution)/shard_map/ppermute | solution.py:66
  13.6 2.4 %collective-permute-start.3 = (bf16[256,512]{0,1:T(8,128)(2,1)S(1)}, bf16[256,512]{0,1:T(8,128)(2,1)S(1)}, u32[]{:S(2)}, u32[]{:S(2)}) collective-permute-start(bf16[256,512]{0,1:T(8,128)(2,1)S(1)} %pad_maximum_fusion.4), channel_id=1, source_target_pairs={{0,16},{1,17},{2,18},{3,19},{4,20},{5,21},{6,22},{7,23},{8,24},{9,... | collective-permute-start | bytes 786440 | tf_op jit(solution)/shard_map/ppermute | solution.py:66
  19.2 2.2 %copy-done = bf16[512,4096]{1,0:T(8,128)(2,1)S(1)} copy-done((bf16[512,4096]{1,0:T(8,128)(2,1)S(1)}, bf16[512,4096]{1,0:T(8,128)(2,1)}, u32[]{:S(2)}) %copy-start) | copy-done | bytes 4194328
  21.4 2.0 %shard_map.76 = bf16[8,512,128]{2,1,0:T(8,128)(2,1)S(1)} custom-call(s32[2]{0:T(128)S(1)} %pad_add_fusion.me, bf16[512,512]{1,0:T(8,128)(2,1)S(1)} %copy.17.x_ref, bf16[512,4096]{1,0:T(8,128)(2,1)S(1)} %copy-done), custom_call_target="tpu_custom_call" | custom-call | flops 536870912 | bytes 2621440 | tf_op jit(solution)/shard_map/pallas_call | solution.py:132
  24.8 2.0 %shard_map.77 = bf16[8,512,128]{2,1,0:T(8,128)(2,1)S(1)} custom-call(s32[2]{0:T(128)S(1)} %pad_add_fusion.me, bf16[512,512]{1,0:T(8,128)(2,1)S(1)} %copy.17.x_ref, bf16[512,4096]{1,0:T(8,128)(2,1)S(1)} %copy-done), custom_call_target="tpu_custom_call" | custom-call | flops 536870912 | bytes 2621440 | tf_op jit(solution)/shard_map/pallas_call | solution.py:132
  26.8 2.0 %collective-permute-start.6 = (bf16[8,512,128]{2,1,0:T(8,128)(2,1)S(1)}, bf16[8,512,128]{2,1,0:T(8,128)(2,1)}, u32[]{:S(2)}, u32[]{:S(2)}) collective-permute-start(bf16[8,512,128]{2,1,0:T(8,128)(2,1)S(1)} %shard_map.77), channel_id=1, source_target_pairs={{0,3},{1,2},{2,1},{3,0},{4,7},{5,6},{6,5},{7,4},{8,11},{9,10},{10,... | collective-permute-start | bytes 3145736 | tf_op jit(solution)/shard_map/ppermute | solution.py:66
  34.0 6.2 %shard_map.75 = (bf16[8,512,128]{2,1,0:T(8,128)(2,1)S(1)}, bf16[8,512,128]{2,1,0:T(8,128)(2,1)S(1)}) custom-call(s32[2]{0:T(128)S(1)} %pad_add_fusion.me, bf16[512,512]{1,0:T(8,128)(2,1)S(1)} %copy.17.x_ref, bf16[512,4096]{1,0:T(8,128)(2,1)} %w_ref.19), custom_call_target="tpu_custom_call" | custom-call | flops 1073741824 | bytes 4718592 | tf_op jit(solution)/shard_map/pallas_call | solution.py:132
  40.1 6.3 %shard_map.80 = (bf16[8,512,128]{2,1,0:T(8,128)(2,1)S(1)}, bf16[8,512,128]{2,1,0:T(8,128)(2,1)S(1)}) custom-call(s32[2]{0:T(128)S(1)} %pad_add_fusion.me, bf16[512,512]{1,0:T(8,128)(2,1)S(1)} %constant_dynamic-update-slice_fusion.10.y_ref.x_ref, bf16[4096,512]{1,0:T(8,128)(2,1)} %w_ref.17), custom_call_target="tpu_custom_call" | custom-call | flops 1073741824 | bytes 4718592 | tf_op jit(solution)/shard_map/pallas_call | solution.py:132
  47.7 2.1 %collective-permute-start.5 = (bf16[4,512,128]{2,1,0:T(8,128)(2,1)S(1)}, bf16[4,512,128]{2,1,0:T(8,128)(2,1)S(1)}, u32[]{:S(2)}, u32[]{:S(2)}) collective-permute-start(bf16[4,512,128]{2,1,0:T(8,128)(2,1)S(1)} %add_convert_fusion.3), channel_id=1, source_target_pairs={{0,3},{1,2},{2,1},{3,0},{4,7},{5,6},{6,5},{7,4},{8,11},{9,10},{10,... | collective-permute-start | bytes 1572872 | tf_op jit(solution)/shard_map/ppermute | solution.py:66
  53.5 5.4 %collective-permute-done.5 = bf16[4,512,128]{2,1,0:T(8,128)(2,1)S(1)} collective-permute-done((bf16[4,512,128]{2,1,0:T(8,128)(2,1)S(1)}, bf16[4,512,128]{2,1,0:T(8,128)(2,1)S(1)}, u32[]{:S(2)}, u32[]{:S(2)}) %collective-permute-start.5) | collective-permute-done | bytes 524320 | tf_op jit(solution)/shard_map/ppermute | solution.py:66
  66.8 2.3 %collective-permute-start.31 = (bf16[2,512,128]{2,1,0:T(8,128)(2,1)S(1)}, bf16[2,512,128]{2,1,0:T(8,128)(2,1)S(1)}, u32[]{:S(2)}, u32[]{:S(2)}) collective-permute-start(bf16[2,512,128]{2,1,0:T(8,128)(2,1)S(1)} %pad_maximum_fusion.10), channel_id=1, source_target_pairs={{0,12},{1,13},{2,14},{3,15},{4,8},{5,9},{6,10},{7,11},{8,4},{9,5},... | collective-permute-start | bytes 786440 | tf_op jit(solution)/shard_map/ppermute | solution.py:66
  70.1 2.2 %collective-permute-done.10 = bf16[2,512,128]{2,1,0:T(8,128)(2,1)S(1)} collective-permute-done((bf16[2,512,128]{2,1,0:T(8,128)(2,1)S(1)}, bf16[2,512,128]{2,1,0:T(8,128)(2,1)S(1)}, u32[]{:S(2)}, u32[]{:S(2)}) %collective-permute-start.10) | collective-permute-done | bytes 262176 | tf_op jit(solution)/shard_map/ppermute | solution.py:66
  72.3 2.8 %collective-permute-done.30 = bf16[2,512,128]{2,1,0:T(8,128)(2,1)S(1)} collective-permute-done((bf16[2,512,128]{2,1,0:T(8,128)(2,1)S(1)}, bf16[2,512,128]{2,1,0:T(8,128)(2,1)S(1)}, u32[]{:S(2)}, u32[]{:S(2)}) %collective-permute-start.30) | collective-permute-done | bytes 262176 | tf_op jit(solution)/shard_map/ppermute | solution.py:66
  75.1 2.6 %collective-permute-done.32 = bf16[2,512,128]{2,1,0:T(8,128)(2,1)S(1)} collective-permute-done((bf16[2,512,128]{2,1,0:T(8,128)(2,1)S(1)}, bf16[2,512,128]{2,1,0:T(8,128)(2,1)S(1)}, u32[]{:S(2)}, u32[]{:S(2)}) %collective-permute-start.32) | collective-permute-done | bytes 262176 | tf_op jit(solution)/shard_map/ppermute | solution.py:66
  78.6 3.7 %collective-permute-start.34 = (bf16[2,512,128]{2,1,0:T(8,128)(2,1)S(1)}, bf16[2,512,128]{2,1,0:T(8,128)(2,1)S(1)}, u32[]{:S(2)}, u32[]{:S(2)}) collective-permute-start(bf16[2,512,128]{2,1,0:T(8,128)(2,1)S(1)} %get-tuple-element.40), channel_id=1, source_target_pairs={{0,8},{1,9},{2,10},{3,11},{4,12},{5,13},{6,14},{7,15},{8,0},{9,1},... | collective-permute-start | bytes 786440 | tf_op jit(solution)/shard_map/ppermute | solution.py:66
  82.5 3.8 %collective-permute-start.12 = (bf16[2,512,128]{2,1,0:T(8,128)(2,1)S(1)}, bf16[2,512,128]{2,1,0:T(8,128)(2,1)S(1)}, u32[]{:S(2)}, u32[]{:S(2)}) collective-permute-start(bf16[2,512,128]{2,1,0:T(8,128)(2,1)S(1)} %get-tuple-element.41), channel_id=1, source_target_pairs={{0,8},{1,9},{2,10},{3,11},{4,12},{5,13},{6,14},{7,15},{8,0},{9,1},... | collective-permute-start | bytes 786440 | tf_op jit(solution)/shard_map/ppermute | solution.py:66
  86.6 2.2 %collective-permute-done.34 = bf16[2,512,128]{2,1,0:T(8,128)(2,1)S(1)} collective-permute-done((bf16[2,512,128]{2,1,0:T(8,128)(2,1)S(1)}, bf16[2,512,128]{2,1,0:T(8,128)(2,1)S(1)}, u32[]{:S(2)}, u32[]{:S(2)}) %collective-permute-start.34) | collective-permute-done | bytes 262176 | tf_op jit(solution)/shard_map/ppermute | solution.py:66
  88.9 2.9 %collective-permute-done.35 = bf16[2,512,128]{2,1,0:T(8,128)(2,1)S(1)} collective-permute-done((bf16[2,512,128]{2,1,0:T(8,128)(2,1)S(1)}, bf16[2,512,128]{2,1,0:T(8,128)(2,1)S(1)}, u32[]{:S(2)}, u32[]{:S(2)}) %collective-permute-start.35) | collective-permute-done | bytes 262176 | tf_op jit(solution)/shard_map/ppermute | solution.py:66
  95.2 2.3 %collective-permute-done.13 = bf16[2,512,128]{2,1,0:T(8,128)(2,1)S(1)} collective-permute-done((bf16[2,512,128]{2,1,0:T(8,128)(2,1)S(1)}, bf16[2,512,128]{2,1,0:T(8,128)(2,1)S(1)}, u32[]{:S(2)}, u32[]{:S(2)}) %collective-permute-start.13) | collective-permute-done | bytes 262176 | tf_op jit(solution)/shard_map/ppermute | solution.py:66
  98.6 2.0 %collective-permute-start.14 = (bf16[4,512,128]{2,1,0:T(8,128)(2,1)S(1)}, bf16[4,512,128]{2,1,0:T(8,128)(2,1)S(1)}, u32[]{:S(2)}, u32[]{:S(2)}) collective-permute-start(bf16[4,512,128]{2,1,0:T(8,128)(2,1)S(1)} %pad_maximum_fusion), channel_id=1, source_target_pairs={{0,3},{1,2},{2,1},{3,0},{4,7},{5,6},{6,5},{7,4},{8,11},{9,10},{10,... | collective-permute-start | bytes 1572872 | tf_op jit(solution)/shard_map/ppermute | solution.py:66
  100.6 3.6 %collective-permute-done.38 = bf16[4,512,128]{2,1,0:T(8,128)(2,1)S(1)} collective-permute-done((bf16[4,512,128]{2,1,0:T(8,128)(2,1)S(1)}, bf16[4,512,128]{2,1,0:T(8,128)(2,1)S(1)}, u32[]{:S(2)}, u32[]{:S(2)}) %collective-permute-start.38) | collective-permute-done | bytes 524320 | tf_op jit(solution)/shard_map/ppermute | solution.py:66
  106.1 2.3 %collective-permute-done.36 = bf16[4,512,128]{2,1,0:T(8,128)(2,1)S(1)} collective-permute-done((bf16[4,512,128]{2,1,0:T(8,128)(2,1)S(1)}, bf16[4,512,128]{2,1,0:T(8,128)(2,1)S(1)}, u32[]{:S(2)}, u32[]{:S(2)}) %collective-permute-start.36) | collective-permute-done | bytes 524320 | tf_op jit(solution)/shard_map/ppermute | solution.py:66
  111.7 2.3 %collective-permute-done.14 = bf16[4,512,128]{2,1,0:T(8,128)(2,1)S(1)} collective-permute-done((bf16[4,512,128]{2,1,0:T(8,128)(2,1)S(1)}, bf16[4,512,128]{2,1,0:T(8,128)(2,1)S(1)}, u32[]{:S(2)}, u32[]{:S(2)}) %collective-permute-start.14) | collective-permute-done | bytes 524320 | tf_op jit(solution)/shard_map/ppermute | solution.py:66
  114.2 8.0 %shard_map.83 = (f32[512,512]{1,0:T(8,128)S(1)}, bf16[512,4096]{1,0:T(8,128)(2,1)}) custom-call(s32[2]{0:T(128)S(1)} %pad_add_fusion.me, bf16[8,512,128]{2,1,0:T(8,128)(2,1)S(1)} %constant_dynamic-update-slice_fusion.15.a_ref, bf16[8,512,128]{2,1,0:T(8,128)(2,1)S(1)} %constant_dynamic-update-slice_fusion.20.b_ref, bf16[512,4096]{1,0:T(8,128)(2,1)} %w_ref.19, ...), custom_call_target="tpu_custom_call" | custom-call | flops 2147483648 | bytes 7864320 | tf_op jit(solution)/shard_map/pallas_call | solution.py:199
  122.2 3.1 %collective-permute-done.39.b_ref = bf16[8,512,128]{2,1,0:T(8,128)(2,1)S(1)} collective-permute-done((bf16[8,512,128]{2,1,0:T(8,128)(2,1)S(1)}, bf16[8,512,128]{2,1,0:T(8,128)(2,1)S(1)}, u32[]{:S(2)}, u32[]{:S(2)}) %collective-permute-start.39) | collective-permute-done | bytes 1048608 | tf_op jit(solution)/shard_map/ppermute | solution.py:66
  125.2 8.1 %shard_map.84 = (f32[512,512]{1,0:T(8,128)S(1)}, bf16[512,4096]{1,0:T(8,128)(2,1)}) custom-call(s32[2]{0:T(128)S(1)} %pad_add_fusion.me, bf16[8,512,128]{2,1,0:T(8,128)(2,1)S(1)} %collective-permute-done.37.a_ref, bf16[8,512,128]{2,1,0:T(8,128)(2,1)S(1)} %collective-permute-done.39.b_ref, ...), custom_call_target="tpu_custom_call", output_to_operand_aliasing={{0}: (5, {}), {1}: (6, {})} | custom-call | flops 2147483648 | bytes 7864320 | tf_op jit(solution)/shard_map/pallas_call | solution.py:199
  133.3 3.4 %collective-permute-start.40 = (bf16[256,512]{1,0:T(8,128)(2,1)S(1)}, bf16[256,512]{1,0:T(8,128)(2,1)S(1)}, u32[]{:S(2)}, u32[]{:S(2)}) collective-permute-start(bf16[256,512]{1,0:T(8,128)(2,1)S(1)} %slice.360), channel_id=1, source_target_pairs={{0,16},{1,17},{2,18},{3,19},{4,20},{5,21},{6,22},{7,23},{8,24},{9,... | collective-permute-start | bytes 786440 | tf_op jit(solution)/shard_map/ppermute | solution.py:66
  136.7 7.9 %shard_map.78 = (f32[512,512]{1,0:T(8,128)S(1)}, bf16[4096,512]{1,0:T(8,128)(2,1)}) custom-call(s32[2]{0:T(128)S(1)} %pad_add_fusion.me, bf16[8,512,128]{2,1,0:T(8,128)(2,1)S(1)} %constant_dynamic-update-slice_fusion.a_ref, bf16[8,512,128]{2,1,0:T(8,128)(2,1)S(1)} %constant_dynamic-update-slice_fusion.5.b_ref, bf16[4096,512]{1,0:T(8,128)(2,1)} %w_ref.17, ...), custom_call_target="tpu_custom_call" | custom-call | flops 2147483648 | bytes 7864320 | tf_op jit(solution)/shard_map/pallas_call | solution.py:199
  144.6 8.0 %shard_map.79 = (f32[512,512]{1,0:T(8,128)S(1)}, bf16[4096,512]{1,0:T(8,128)(2,1)}) custom-call(s32[2]{0:T(128)S(1)} %pad_add_fusion.me, bf16[8,512,128]{2,1,0:T(8,128)(2,1)S(1)} %collective-permute-done.15.a_ref, bf16[8,512,128]{2,1,0:T(8,128)(2,1)S(1)} %collective-permute-done.17.b_ref, ...), custom_call_target="tpu_custom_call", output_to_operand_aliasing={{0}: (5, {}), {1}: (6, {})} | custom-call | flops 2147483648 | bytes 7864320 | tf_op jit(solution)/shard_map/pallas_call | solution.py:199
  (126 shorter events, 50.1 us)
Async XLA Ops:
  1.6 8.0 %collective-permute-start = (bf16[64,512]{0,1:T(8,128)(2,1)S(1)}, bf16[64,512]{0,1:T(8,128)(2,1)S(1)}, u32[]{:S(2)}, u32[]{:S(2)}) collective-permute-start(bf16[64,512]{0,1:T(8,128)(2,1)S(1)} %copy.16), channel_id=1, source_target_pairs={{0,32},{1,33},{2,34},{3,35},{4,36},{5,37},{6,38},{7,39},{8,40},{9,... | collective-permute-start | bytes 196616 | tf_op jit(solution)/shard_map/ppermute | solution.py:66
  7.4 9.4 %collective-permute-start.18 = (bf16[64,512]{1,0:T(8,128)(2,1)}, bf16[64,512]{1,0:T(8,128)(2,1)S(1)}, u32[]{:S(2)}, u32[]{:S(2)}) collective-permute-start(bf16[64,512]{1,0:T(8,128)(2,1)} %param.7), channel_id=1, source_target_pairs={{0,32},{1,33},{2,34},{3,35},{4,36},{5,37},{6,38},{7,39},{8,40},{9,... | collective-permute-start | bytes 196616 | tf_op jit(solution)/shard_map/ppermute | solution.py:66
  7.4 9.4 %collective-permute-start.19 = (bf16[64,512]{1,0:T(8,128)(2,1)}, bf16[64,512]{1,0:T(8,128)(2,1)S(1)}, u32[]{:S(2)}, u32[]{:S(2)}) collective-permute-start(bf16[64,512]{1,0:T(8,128)(2,1)} %param.7), channel_id=1, source_target_pairs={{0,96},{1,97},{2,98},{3,99},{4,100},{5,101},{6,102},{7,103},{8,104... | collective-permute-start | bytes 196616 | tf_op jit(solution)/shard_map/ppermute | solution.py:66
  17.7 11.1 %collective-permute-start.21 = (bf16[256,512]{1,0:T(8,128)(2,1)S(1)}, bf16[256,512]{1,0:T(8,128)(2,1)S(1)}, u32[]{:S(2)}, u32[]{:S(2)}) collective-permute-start(bf16[256,512]{1,0:T(8,128)(2,1)S(1)} %pad_maximum_fusion.8), channel_id=1, source_target_pairs={{0,16},{1,17},{2,18},{3,19},{4,20},{5,21},{6,22},{7,23},{8,24},{9,... | collective-permute-start | bytes 786440 | tf_op jit(solution)/shard_map/ppermute | solution.py:66
  23.4 23.1 %collective-permute-start.4 = (bf16[8,512,128]{2,1,0:T(8,128)(2,1)S(1)}, bf16[8,512,128]{2,1,0:T(8,128)(2,1)}, u32[]{:S(2)}, u32[]{:S(2)}) collective-permute-start(bf16[8,512,128]{2,1,0:T(8,128)(2,1)S(1)} %shard_map.76), channel_id=1, source_target_pairs={{0,1},{1,0},{2,3},{3,2},{4,5},{5,4},{6,7},{7,6},{8,9},{9,8},{10,11... | collective-permute-start | bytes 3145736 | tf_op jit(solution)/shard_map/ppermute | solution.py:66
  26.8 23.0 %collective-permute-start.6 = (bf16[8,512,128]{2,1,0:T(8,128)(2,1)S(1)}, bf16[8,512,128]{2,1,0:T(8,128)(2,1)}, u32[]{:S(2)}, u32[]{:S(2)}) collective-permute-start(bf16[8,512,128]{2,1,0:T(8,128)(2,1)S(1)} %shard_map.77), channel_id=1, source_target_pairs={{0,3},{1,2},{2,1},{3,0},{4,7},{5,6},{6,5},{7,4},{8,11},{9,10},{10,... | collective-permute-start | bytes 3145736 | tf_op jit(solution)/shard_map/ppermute | solution.py:66
  30.8 20.2 %collective-permute-start.26 = (bf16[8,512,128]{2,1,0:T(8,128)(2,1)S(1)}, bf16[8,512,128]{2,1,0:T(8,128)(2,1)S(1)}, u32[]{:S(2)}, u32[]{:S(2)}) collective-permute-start(bf16[8,512,128]{2,1,0:T(8,128)(2,1)S(1)} %shard_map.81), channel_id=1, source_target_pairs={{0,1},{1,0},{2,3},{3,2},{4,5},{5,4},{6,7},{7,6},{8,9},{9,8},{10,11... | collective-permute-start | bytes 3145736 | tf_op jit(solution)/shard_map/ppermute | solution.py:66
  33.2 20.0 %collective-permute-start.28 = (bf16[8,512,128]{2,1,0:T(8,128)(2,1)S(1)}, bf16[8,512,128]{2,1,0:T(8,128)(2,1)S(1)}, u32[]{:S(2)}, u32[]{:S(2)}) collective-permute-start(bf16[8,512,128]{2,1,0:T(8,128)(2,1)S(1)} %shard_map.82), channel_id=1, source_target_pairs={{0,3},{1,2},{2,1},{3,0},{4,7},{5,6},{6,5},{7,4},{8,11},{9,10},{10,... | collective-permute-start | bytes 3145736 | tf_op jit(solution)/shard_map/ppermute | solution.py:66
  47.7 11.2 %collective-permute-start.5 = (bf16[4,512,128]{2,1,0:T(8,128)(2,1)S(1)}, bf16[4,512,128]{2,1,0:T(8,128)(2,1)S(1)}, u32[]{:S(2)}, u32[]{:S(2)}) collective-permute-start(bf16[4,512,128]{2,1,0:T(8,128)(2,1)S(1)} %add_convert_fusion.3), channel_id=1, source_target_pairs={{0,3},{1,2},{2,1},{3,0},{4,7},{5,6},{6,5},{7,4},{8,11},{9,10},{10,... | collective-permute-start | bytes 1572872 | tf_op jit(solution)/shard_map/ppermute | solution.py:66
  51.0 9.2 %collective-permute-start.7 = (bf16[4,512,128]{2,1,0:T(8,128)(2,1)S(1)}, bf16[4,512,128]{2,1,0:T(8,128)(2,1)S(1)}, u32[]{:S(2)}, u32[]{:S(2)}) collective-permute-start(bf16[4,512,128]{2,1,0:T(8,128)(2,1)S(1)} %add_convert_fusion.2), channel_id=1, source_target_pairs={{0,1},{1,0},{2,3},{3,2},{4,5},{5,4},{6,7},{7,6},{8,9},{9,8},{10,11... | collective-permute-start | bytes 1572872 | tf_op jit(solution)/shard_map/ppermute | solution.py:66
  51.2 14.3 %collective-permute-start.27 = (bf16[4,512,128]{2,1,0:T(8,128)(2,1)S(1)}, bf16[4,512,128]{2,1,0:T(8,128)(2,1)S(1)}, u32[]{:S(2)}, u32[]{:S(2)}) collective-permute-start(bf16[4,512,128]{2,1,0:T(8,128)(2,1)S(1)} %add_convert_fusion.1), channel_id=1, source_target_pairs={{0,3},{1,2},{2,1},{3,0},{4,7},{5,6},{6,5},{7,4},{8,11},{9,10},{10,... | collective-permute-start | bytes 1572872 | tf_op jit(solution)/shard_map/ppermute | solution.py:66
  53.4 12.3 %collective-permute-start.29 = (bf16[4,512,128]{2,1,0:T(8,128)(2,1)S(1)}, bf16[4,512,128]{2,1,0:T(8,128)(2,1)S(1)}, u32[]{:S(2)}, u32[]{:S(2)}) collective-permute-start(bf16[4,512,128]{2,1,0:T(8,128)(2,1)S(1)} %add_convert_fusion), channel_id=1, source_target_pairs={{0,1},{1,0},{2,3},{3,2},{4,5},{5,4},{6,7},{7,6},{8,9},{9,8},{10,11... | collective-permute-start | bytes 1572872 | tf_op jit(solution)/shard_map/ppermute | solution.py:66
  61.5 7.9 %collective-permute-start.8 = (bf16[2,512,128]{2,1,0:T(8,128)(2,1)S(1)}, bf16[2,512,128]{2,1,0:T(8,128)(2,1)S(1)}, u32[]{:S(2)}, u32[]{:S(2)}) collective-permute-start(bf16[2,512,128]{2,1,0:T(8,128)(2,1)S(1)} %pad_maximum_fusion.5), channel_id=1, source_target_pairs={{0,4},{1,5},{2,6},{3,7},{4,0},{5,1},{6,2},{7,3},{8,12},{9,13},{10,... | collective-permute-start | bytes 786440 | tf_op jit(solution)/shard_map/ppermute | solution.py:66
  64.5 7.9 %collective-permute-start.10 = (bf16[2,512,128]{2,1,0:T(8,128)(2,1)S(1)}, bf16[2,512,128]{2,1,0:T(8,128)(2,1)S(1)}, u32[]{:S(2)}, u32[]{:S(2)}) collective-permute-start(bf16[2,512,128]{2,1,0:T(8,128)(2,1)S(1)} %pad_maximum_fusion.7), channel_id=1, source_target_pairs={{0,8},{1,9},{2,10},{3,11},{4,12},{5,13},{6,14},{7,15},{8,0},{9,1},... | collective-permute-start | bytes 786440 | tf_op jit(solution)/shard_map/ppermute | solution.py:66
  66.0 9.1 %collective-permute-start.30 = (bf16[2,512,128]{2,1,0:T(8,128)(2,1)S(1)}, bf16[2,512,128]{2,1,0:T(8,128)(2,1)S(1)}, u32[]{:S(2)}, u32[]{:S(2)}) collective-permute-start(bf16[2,512,128]{2,1,0:T(8,128)(2,1)S(1)} %pad_maximum_fusion.9), channel_id=1, source_target_pairs={{0,4},{1,5},{2,6},{3,7},{4,0},{5,1},{6,2},{7,3},{8,12},{9,13},{10,... | collective-permute-start | bytes 786440 | tf_op jit(solution)/shard_map/ppermute | solution.py:66
  66.8 8.3 %collective-permute-start.31 = (bf16[2,512,128]{2,1,0:T(8,128)(2,1)S(1)}, bf16[2,512,128]{2,1,0:T(8,128)(2,1)S(1)}, u32[]{:S(2)}, u32[]{:S(2)}) collective-permute-start(bf16[2,512,128]{2,1,0:T(8,128)(2,1)S(1)} %pad_maximum_fusion.10), channel_id=1, source_target_pairs={{0,12},{1,13},{2,14},{3,15},{4,8},{5,9},{6,10},{7,11},{8,4},{9,5},... | collective-permute-start | bytes 786440 | tf_op jit(solution)/shard_map/ppermute | solution.py:66
  69.5 8.2 %collective-permute-start.32 = (bf16[2,512,128]{2,1,0:T(8,128)(2,1)S(1)}, bf16[2,512,128]{2,1,0:T(8,128)(2,1)S(1)}, u32[]{:S(2)}, u32[]{:S(2)}) collective-permute-start(bf16[2,512,128]{2,1,0:T(8,128)(2,1)S(1)} %pad_maximum_fusion.11), channel_id=1, source_target_pairs={{0,8},{1,9},{2,10},{3,11},{4,12},{5,13},{6,14},{7,15},{8,0},{9,1},... | collective-permute-start | bytes 786440 | tf_op jit(solution)/shard_map/ppermute | solution.py:66
  78.2 8.1 %collective-permute-start.33 = (bf16[2,512,128]{2,1,0:T(8,128)(2,1)S(1)}, bf16[2,512,128]{2,1,0:T(8,128)(2,1)S(1)}, u32[]{:S(2)}, u32[]{:S(2)}) collective-permute-start(bf16[2,512,128]{2,1,0:T(8,128)(2,1)S(1)} %get-tuple-element.40), channel_id=1, source_target_pairs={{0,4},{1,5},{2,6},{3,7},{4,0},{5,1},{6,2},{7,3},{8,12},{9,13},{10,... | collective-permute-start | bytes 786440 | tf_op jit(solution)/shard_map/ppermute | solution.py:66
  78.6 10.2 %collective-permute-start.34 = (bf16[2,512,128]{2,1,0:T(8,128)(2,1)S(1)}, bf16[2,512,128]{2,1,0:T(8,128)(2,1)S(1)}, u32[]{:S(2)}, u32[]{:S(2)}) collective-permute-start(bf16[2,512,128]{2,1,0:T(8,128)(2,1)S(1)} %get-tuple-element.40), channel_id=1, source_target_pairs={{0,8},{1,9},{2,10},{3,11},{4,12},{5,13},{6,14},{7,15},{8,0},{9,1},... | collective-permute-start | bytes 786440 | tf_op jit(solution)/shard_map/ppermute | solution.py:66
  82.3 9.5 %collective-permute-start.35 = (bf16[2,512,128]{2,1,0:T(8,128)(2,1)S(1)}, bf16[2,512,128]{2,1,0:T(8,128)(2,1)S(1)}, u32[]{:S(2)}, u32[]{:S(2)}) collective-permute-start(bf16[2,512,128]{2,1,0:T(8,128)(2,1)S(1)} %get-tuple-element.40), channel_id=1, source_target_pairs={{0,12},{1,13},{2,14},{3,15},{4,8},{5,9},{6,10},{7,11},{8,4},{9,5},... | collective-permute-start | bytes 786440 | tf_op jit(solution)/shard_map/ppermute | solution.py:66
  82.4 12.6 %collective-permute-start.11 = (bf16[2,512,128]{2,1,0:T(8,128)(2,1)S(1)}, bf16[2,512,128]{2,1,0:T(8,128)(2,1)S(1)}, u32[]{:S(2)}, u32[]{:S(2)}) collective-permute-start(bf16[2,512,128]{2,1,0:T(8,128)(2,1)S(1)} %get-tuple-element.41), channel_id=1, source_target_pairs={{0,4},{1,5},{2,6},{3,7},{4,0},{5,1},{6,2},{7,3},{8,12},{9,13},{10,... | collective-permute-start | bytes 786440 | tf_op jit(solution)/shard_map/ppermute | solution.py:66
  82.5 12.6 %collective-permute-start.12 = (bf16[2,512,128]{2,1,0:T(8,128)(2,1)S(1)}, bf16[2,512,128]{2,1,0:T(8,128)(2,1)S(1)}, u32[]{:S(2)}, u32[]{:S(2)}) collective-permute-start(bf16[2,512,128]{2,1,0:T(8,128)(2,1)S(1)} %get-tuple-element.41), channel_id=1, source_target_pairs={{0,8},{1,9},{2,10},{3,11},{4,12},{5,13},{6,14},{7,15},{8,0},{9,1},... | collective-permute-start | bytes 786440 | tf_op jit(solution)/shard_map/ppermute | solution.py:66
  86.3 11.1 %collective-permute-start.13 = (bf16[2,512,128]{2,1,0:T(8,128)(2,1)S(1)}, bf16[2,512,128]{2,1,0:T(8,128)(2,1)S(1)}, u32[]{:S(2)}, u32[]{:S(2)}) collective-permute-start(bf16[2,512,128]{2,1,0:T(8,128)(2,1)S(1)} %get-tuple-element.41), channel_id=1, source_target_pairs={{0,12},{1,13},{2,14},{3,15},{4,8},{5,9},{6,10},{7,11},{8,4},{9,5},... | collective-permute-start | bytes 786440 | tf_op jit(solution)/shard_map/ppermute | solution.py:66
  92.0 12.2 %collective-permute-start.38 = (bf16[4,512,128]{2,1,0:T(8,128)(2,1)S(1)}, bf16[4,512,128]{2,1,0:T(8,128)(2,1)S(1)}, u32[]{:S(2)}, u32[]{:S(2)}) collective-permute-start(bf16[4,512,128]{2,1,0:T(8,128)(2,1)S(1)} %pad_maximum_fusion.3), channel_id=1, source_target_pairs={{0,1},{1,0},{2,3},{3,2},{4,5},{5,4},{6,7},{7,6},{8,9},{9,8},{10,11... | collective-permute-start | bytes 1572872 | tf_op jit(solution)/shard_map/ppermute | solution.py:66
  93.0 15.4 %collective-permute-start.36 = (bf16[4,512,128]{2,1,0:T(8,128)(2,1)S(1)}, bf16[4,512,128]{2,1,0:T(8,128)(2,1)S(1)}, u32[]{:S(2)}, u32[]{:S(2)}) collective-permute-start(bf16[4,512,128]{2,1,0:T(8,128)(2,1)S(1)} %pad_maximum_fusion.2), channel_id=1, source_target_pairs={{0,3},{1,2},{2,1},{3,0},{4,7},{5,6},{6,5},{7,4},{8,11},{9,10},{10,... | collective-permute-start | bytes 1572872 | tf_op jit(solution)/shard_map/ppermute | solution.py:66
  97.6 12.2 %collective-permute-start.16 = (bf16[4,512,128]{2,1,0:T(8,128)(2,1)S(1)}, bf16[4,512,128]{2,1,0:T(8,128)(2,1)S(1)}, u32[]{:S(2)}, u32[]{:S(2)}) collective-permute-start(bf16[4,512,128]{2,1,0:T(8,128)(2,1)S(1)} %pad_maximum_fusion.1), channel_id=1, source_target_pairs={{0,1},{1,0},{2,3},{3,2},{4,5},{5,4},{6,7},{7,6},{8,9},{9,8},{10,11... | collective-permute-start | bytes 1572872 | tf_op jit(solution)/shard_map/ppermute | solution.py:66
  98.6 15.4 %collective-permute-start.14 = (bf16[4,512,128]{2,1,0:T(8,128)(2,1)S(1)}, bf16[4,512,128]{2,1,0:T(8,128)(2,1)S(1)}, u32[]{:S(2)}, u32[]{:S(2)}) collective-permute-start(bf16[4,512,128]{2,1,0:T(8,128)(2,1)S(1)} %pad_maximum_fusion), channel_id=1, source_target_pairs={{0,3},{1,2},{2,1},{3,0},{4,7},{5,6},{6,5},{7,4},{8,11},{9,10},{10,... | collective-permute-start | bytes 1572872 | tf_op jit(solution)/shard_map/ppermute | solution.py:66
  104.2 21.0 %collective-permute-start.39 = (bf16[8,512,128]{2,1,0:T(8,128)(2,1)S(1)}, bf16[8,512,128]{2,1,0:T(8,128)(2,1)S(1)}, u32[]{:S(2)}, u32[]{:S(2)}) collective-permute-start(bf16[8,512,128]{2,1,0:T(8,128)(2,1)S(1)} %constant_dynamic-update-slice_fusion.20.b_ref), channel_id=1, source_target_pairs={{0,3},{1,2},{2,1},{3,0},{4,7},{5,6},{6,5},{7,4},{8,11},{9,10},{10,... | collective-permute-start | bytes 3145736 | tf_op jit(solution)/shard_map/ppermute | solution.py:66
  108.5 16.8 %collective-permute-start.37 = (bf16[8,512,128]{2,1,0:T(8,128)(2,1)S(1)}, bf16[8,512,128]{2,1,0:T(8,128)(2,1)S(1)}, u32[]{:S(2)}, u32[]{:S(2)}) collective-permute-start(bf16[8,512,128]{2,1,0:T(8,128)(2,1)S(1)} %constant_dynamic-update-slice_fusion.15.a_ref), channel_id=1, source_target_pairs={{0,1},{1,0},{2,3},{3,2},{4,5},{5,4},{6,7},{7,6},{8,9},{9,8},{10,11... | collective-permute-start | bytes 3145736 | tf_op jit(solution)/shard_map/ppermute | solution.py:66
  109.9 34.8 %collective-permute-start.17 = (bf16[8,512,128]{2,1,0:T(8,128)(2,1)S(1)}, bf16[8,512,128]{2,1,0:T(8,128)(2,1)S(1)}, u32[]{:S(2)}, u32[]{:S(2)}) collective-permute-start(bf16[8,512,128]{2,1,0:T(8,128)(2,1)S(1)} %constant_dynamic-update-slice_fusion.5.b_ref), channel_id=1, source_target_pairs={{0,3},{1,2},{2,1},{3,0},{4,7},{5,6},{6,5},{7,4},{8,11},{9,10},{10,... | collective-permute-start | bytes 3145736 | tf_op jit(solution)/shard_map/ppermute | solution.py:66
  114.1 30.6 %collective-permute-start.15 = (bf16[8,512,128]{2,1,0:T(8,128)(2,1)S(1)}, bf16[8,512,128]{2,1,0:T(8,128)(2,1)S(1)}, u32[]{:S(2)}, u32[]{:S(2)}) collective-permute-start(bf16[8,512,128]{2,1,0:T(8,128)(2,1)S(1)} %constant_dynamic-update-slice_fusion.a_ref), channel_id=1, source_target_pairs={{0,1},{1,0},{2,3},{3,2},{4,5},{5,4},{6,7},{7,6},{8,9},{9,8},{10,11... | collective-permute-start | bytes 3145736 | tf_op jit(solution)/shard_map/ppermute | solution.py:66
  133.3 19.5 %collective-permute-start.40 = (bf16[256,512]{1,0:T(8,128)(2,1)S(1)}, bf16[256,512]{1,0:T(8,128)(2,1)S(1)}, u32[]{:S(2)}, u32[]{:S(2)}) collective-permute-start(bf16[256,512]{1,0:T(8,128)(2,1)S(1)} %slice.360), channel_id=1, source_target_pairs={{0,16},{1,17},{2,18},{3,19},{4,20},{5,21},{6,22},{7,23},{8,24},{9,... | collective-permute-start | bytes 786440 | tf_op jit(solution)/shard_map/ppermute | solution.py:66
  (14 other events, 76.2 us)

commit v2 on v1

v2 whole, which is shorter than its diff:
```python
import functools

import jax
import jax.numpy as jnp
from jax import lax
from jax.experimental import pallas as pl
from jax.experimental.pallas import tpu as pltpu
from jax.sharding import PartitionSpec as P

BOTH = ("row", "col")
F32, BF16 = jnp.float32, jnp.bfloat16
CHUNK = 128
EIGHT = 8
LIMIT = 20 * 1024 * 1024


def gelu_tanh(value):
    inner = 0.7978845608 * (value + 0.044715 * value * value * value)
    return 0.5 * value * (1.0 + jnp.tanh(inner))


def gelu_slope(value):
    tangent = jnp.tanh(0.7978845608 * (value + 0.044715 * value * value * value))
    return 0.5 * (1.0 + tangent) + 0.5 * value * (1.0 - tangent * tangent) * 0.7978845608 * (
        1.0 + 3.0 * 0.044715 * value * value
    )


GRAY = (0, 1, 3, 2)
UNGRAY = (0, 1, 3, 2)


def pairs(move):
    listed = []
    for z in range(4):
        for core in range(2):
            for y in range(4):
                for x in range(4):
                    tz, tcore, ty, tx = move(z, core, y, x)
                    listed.append(
                        ((z * 2 + core) * 16 + y * 4 + x, (tz * 2 + tcore) * 16 + ty * 4 + tx)
                    )
    return listed


def flip(position, bit):
    return UNGRAY[GRAY[position] ^ (1 << bit)]


PRIMARY = [
    pairs(
        lambda z, core, y, x, bit=bit: (z, core, y, flip(x, bit))
        if core == 0
        else (z, core, flip(y, bit), x)
    )
    for bit in range(2)
]
SECONDARY = [
    pairs(lambda z, core, y, x, k=k: (z, core, y ^ k, x) if core == 0 else (z, core, y, x ^ k))
    for k in range(4)
]
FIRST_Z, SECOND_Z = (
    pairs(lambda z, core, y, x, turn=turn: (flip(z, core ^ turn), core, y, x)) for turn in range(2)
)
ACROSS_Z = pairs(lambda z, core, y, x: (z ^ 2, core, y, x))
CORES = pairs(lambda z, core, y, x: (z, 1 - core, y, x))


def send(block, perm):
    return lax.ppermute(block, BOTH, perm)


def gray(position):
    return jnp.bitwise_xor(position, jnp.right_shift(position, 1))


def places():
    row, col = lax.axis_index("row"), lax.axis_index("col")
    core, y, x = row % 2, col // 4, col % 4
    primary = gray(jnp.where(core == 0, x, y))
    secondary = jnp.where(core == 0, y, x)
    low, high = primary % 2, primary // 2
    return jnp.stack([low * 8 + high * 4 + secondary, high * 8 + low * 4 + secondary]).astype(
        jnp.int32
    )


def order(me, part, count):
    return [jnp.bitwise_xor(chunk, me[part] % count) for chunk in range(count)]


def weight_spec(transposed, depth, first, part_of):
    def index(i, me):
        part = part_of(i)
        group = jnp.bitwise_xor(first, jnp.right_shift(me[part], 3)) + 2 * part
        return (group, 0) if transposed else (0, group)

    wide = EIGHT * CHUNK
    return pl.BlockSpec((wide, depth) if transposed else (depth, wide), index)


def produce_body(transposed, parts, me, x_ref, w_ref, *outs):
    if transposed:
        term = lax.dot_general(
            x_ref[...], w_ref[...], (((1,), (1,)), ((), ())), preferred_element_type=F32
        )
    else:
        term = jnp.dot(x_ref[...], w_ref[...], preferred_element_type=F32)
    term = term.astype(BF16)

    def put(out, part):
        for chunk, place in enumerate(order(me, part, EIGHT)):
            out[place] = term[:, CHUNK * chunk : CHUNK * (chunk + 1)]

    if len(parts) == 1:
        put(outs[0], parts[0])
    else:
        for n, part in enumerate(parts):
            pl.when(pl.program_id(0) == n)(functools.partial(put, outs[n], part))


def produce(x, w, me, transposed, parts, first):
    tokens, depth = x.shape
    count = len(parts)
    part_of = (lambda i: parts[0]) if count == 1 else (lambda i: i)
    block = (EIGHT, tokens, CHUNK)
    return pl.pallas_call(
        functools.partial(produce_body, transposed, parts),
        out_shape=[jax.ShapeDtypeStruct(block, BF16)] * count,
        grid_spec=pltpu.PrefetchScalarGridSpec(
            num_scalar_prefetch=1,
            grid=(count,),
            in_specs=[
                pl.BlockSpec((tokens, depth), lambda i, me: (0, 0)),
                weight_spec(transposed, depth, first, part_of),
            ],
            out_specs=[pl.BlockSpec(block, lambda i, me: (0, 0, 0))] * count,
        ),
        compiler_params=pltpu.CompilerParams(vmem_limit_bytes=LIMIT),
        cost_estimate=pl.CostEstimate(
            flops=tokens * depth * CHUNK * count,
            bytes_accessed=tokens * depth,
            transcendentals=0,
        ),
    )(me, x, w)


def consume_body(transposed, has_total, has_grad, wants, me, a_ref, b_ref, *rest):
    rest = list(rest)
    w_ref = rest.pop(0) if "total" in wants else None
    y_ref = rest.pop(0) if "grad" in wants else None
    total_in = rest.pop(0) if has_total else None
    if has_grad:
        rest.pop(0)
    total = rest.pop(0) if "total" in wants else None
    grad = rest.pop(0) if "grad" in wants else None

    def step(ref, part):
        block = jnp.concatenate([ref[place] for place in order(me, part, EIGHT)], axis=1)
        if grad is not None and transposed:
            grad[...] = lax.dot_general(
                block, y_ref[...], (((0,), (0,)), ((), ())), preferred_element_type=F32
            ).astype(BF16)
        elif grad is not None:
            grad[...] = jnp.dot(y_ref[...], block, preferred_element_type=F32).astype(BF16)
        if total is not None:
            dims = ((1,), (0,)) if transposed else ((1,), (1,))
            added = lax.dot_general(block, w_ref[...], (dims, ((), ())), preferred_element_type=F32)
            if part == 1:
                total[...] += added
            elif has_total:
                total[...] = total_in[...] + added
            else:
                total[...] = added

    for part, ref in enumerate((a_ref, b_ref)):
        pl.when(pl.program_id(0) == part)(functools.partial(step, ref, part))


def consume(a, b, w, y, me, transposed, first, total=None, grad=None, wants=("total", "grad")):
    tokens, depth = y.shape
    block = (EIGHT, tokens, CHUNK)
    whole = lambda i, me: (0, 0)
    chunks = pl.BlockSpec(block, lambda i, me: (0, 0, 0))
    weights = weight_spec(transposed, depth, first, lambda i: i)
    in_specs, operands = [chunks, chunks], [me, a, b]
    out_specs, out_shape, aliases = [], [], {}
    if "total" in wants:
        in_specs.append(weights)
        operands.append(w)
        out_specs.append(pl.BlockSpec((tokens, depth), whole))
        out_shape.append(jax.ShapeDtypeStruct((tokens, depth), F32))
    if "grad" in wants:
        in_specs.append(pl.BlockSpec(y.shape, whole))
        operands.append(y)
        out_specs.append(weights)
        out_shape.append(jax.ShapeDtypeStruct(w.shape, BF16))
    if total is not None:
        aliases[len(operands)] = 0
        in_specs.append(pl.BlockSpec((tokens, depth), whole))
        operands.append(total)
    if grad is not None:
        aliases[len(operands)] = len(out_shape) - 1
        in_specs.append(pl.BlockSpec(memory_space=pl.ANY))
        operands.append(grad)
    return pl.pallas_call(
        functools.partial(consume_body, transposed, total is not None, grad is not None, wants),
        out_shape=out_shape,
        grid_spec=pltpu.PrefetchScalarGridSpec(
            num_scalar_prefetch=1, grid=(2,), in_specs=in_specs, out_specs=out_specs
        ),
        input_output_aliases=aliases,
        compiler_params=pltpu.CompilerParams(vmem_limit_bytes=LIMIT),
        cost_estimate=pl.CostEstimate(
            flops=4 * tokens * depth * CHUNK,
            bytes_accessed=tokens * depth,
            transcendentals=0,
        ),
    )(*operands)


def add(*terms):
    total = terms[0].astype(F32)
    for term in terms[1:]:
        total = total + term.astype(F32)
    return total


def after(value, *others):
    return lax.optimization_barrier((value,) + others)[0]


def join(block, got):
    return jnp.concatenate([block, got], axis=0)


def gather_rows(normed, d_out):
    normed = join(normed, send(normed, FIRST_Z))
    d_out = join(d_out, send(d_out, FIRST_Z))
    normed = join(normed, send(normed, SECOND_Z))
    d_out = join(d_out, send(after(d_out, normed), SECOND_Z))
    normed = join(normed, send(normed, CORES))
    d_out = join(d_out, send(d_out, CORES))
    return normed, d_out


def scatter_rows(total):
    half = total.shape[0] // 2
    total = add(total[:half], send(total[half:].astype(BF16), CORES))
    rows = half // 4
    parts = [total[rows * n : rows * (n + 1)] for n in range(4)]
    got = [send(parts[n].astype(BF16), perm) for n, perm in ((1, FIRST_Z), (2, SECOND_Z), (3, ACROSS_Z))]
    return add(parts[0], *got).astype(BF16)


def halve_first(x, w, me, transposed):
    far = [produce(x, w, me, transposed, (h,), 1)[0] for h in range(2)]
    got = [send(far[h], PRIMARY[h]) for h in range(2)]
    near = produce(x, w, me, transposed, (0, 1), 0)
    return near, got


def halve_second(near, got):
    out = [send(add(near[h][4:], got[h][4:]).astype(BF16), PRIMARY[1 - h]) for h in range(2)]
    return [add(near[h][:4], got[h][:4], out[h]) for h in range(2)]


def exchange(four):
    own = jnp.stack([four[0][0], four[1][0]])
    last = [
        send(jnp.stack([four[0][k], four[1][k]]).astype(BF16), SECONDARY[k]) for k in (1, 3, 2)
    ]
    return add(own, *last)


def spread_first(own):
    one, three, two = (send(own, SECONDARY[k]) for k in (1, 3, 2))
    return [jnp.stack([own[h], one[h], two[h], three[h]]) for h in range(2)]


def spread_second(four):
    return [
        jnp.concatenate([four[h], send(four[h], PRIMARY[1 - h])], axis=0) for h in range(2)
    ]


def spread_third(near):
    return [send(near[h], PRIMARY[h]) for h in range(2)]


def shards(normed, w_in, w_out, d_out):
    me = places()
    inputs, cotangent = gather_rows(normed, d_out)
    turned = inputs.T
    p_near, p_got = halve_first(inputs, w_in, me, False)
    d_near, d_got = halve_first(cotangent, w_out, me, True)
    p_four = halve_second(p_near, p_got)
    d_four = halve_second(d_near, d_got)
    preact = exchange(p_four)
    d_act = exchange(d_four)
    act = gelu_tanh(preact).astype(BF16)
    act, preact = lax.optimization_barrier((act, preact))
    p_four = spread_first(act)
    d_pre = (d_act * gelu_slope(preact)).astype(BF16)
    p_near = spread_second(p_four)
    d_four = spread_first(after(d_pre, *p_four))
    p_far = spread_third(p_near)
    d_near = spread_second([after(d_four[h], p_near[h]) for h in range(2)])
    total, grad = consume(p_near[0], p_near[1], w_out, cotangent, me, True, 0)
    d_far = spread_third([after(d_near[h], total) for h in range(2)])
    d_total, d_grad = consume(d_near[0], d_near[1], w_in, turned, me, False, 0)
    p_far[0] = after(p_far[0], d_total)
    total, grad_out = consume(p_far[0], p_far[1], w_out, cotangent, me, True, 1, total, grad)
    ffn_out = scatter_rows(total)
    (d_total,) = consume(d_far[0], d_far[1], w_in, turned, me, False, 1, d_total, None, ("total",))
    d_normed = scatter_rows(d_total)
    (grad_in,) = consume(
        after(d_far[0], d_total), d_far[1], w_in, turned, me, False, 1, None, d_grad, ("grad",)
    )
    return (ffn_out, d_normed, grad_in, grad_out)


def solution(mesh):
    return jax.shard_map(
        shards,
        mesh=mesh,
        in_specs=(P("row", "col"), P("col", "row"), P("row", "col"), P("row", "col")),
        out_specs=(P("row", "col"), P("row", "col"), P("col", "row"), P("row", "col")),
        check_vma=False,
    )
```

time: 167 us -> 154 us (0.922); the launches traced: 165 us -> 154 us
  Pallas kernels: 52.4 us -> 28.1 us
  waiting for transfers between devices: 40.8 us -> 53.3 us
  starting transfers between devices: 55.5 us -> 61.1 us
  other arithmetic: 9.2 us -> 5.61 us
    pallas_call x10 -> x11, Pallas kernels: 52.4 us -> 28.1 us  [the longest x5 17.9 us: consume(): pl.pallas_call(functools.partial(consume_body, transposed, total is not N...]
    ppermute x44 -> x42, waiting for transfers between devices: 40.8 us -> 53.3 us  [send(): return lax.ppermute(block, BOTH, perm)]
    ppermute x44 -> x42, starting transfers between devices: 55.5 us -> 61.1 us  [send(): return lax.ppermute(block, BOTH, perm)]
    another operation x16, other arithmetic: 3.52 us -> 1.45 us
    convert_element_type x6 -> x7, other arithmetic: 3.96 us -> 2.17 us  [the longest x2 1.33 us: scatter_rows(): return add(parts[0], *got).astype(BF16)]
    unnamed x9 -> x18, local copies, waits for them, and re-layouts: 4 us -> 3.57 us
  transfers between devices with their start and end apart: 44 -> 42, of which waited for: 18 -> 21; matrix products, arithmetic and copies ran while one was open for 6% -> 4% of each run, Pallas kernels for 32% -> 18%
where the time goes in v2:
time: 154 us
  starting transfers between devices  61.1 us (40%)
  waiting for transfers between devices  53.3 us (35%)
  Pallas kernels  28.1 us (18%)
  other arithmetic  5.61 us (4%)
  local copies, waits for them, and re-layouts  4.43 us (3%)
    ppermute x42, starting transfers between devices, send(): return lax.ppermute(block, BOTH, perm)  61.1 us
    ppermute x42, waiting for transfers between devices, send(): return lax.ppermute(block, BOTH, perm)  53.3 us
    pallas_call x5, Pallas kernels, consume(): pl.pallas_call(functools.partial(consume_body, transposed, total is not N...  17.9 us
    pallas_call x6, Pallas kernels, produce(): pl.pallas_call(functools.partial(produce_body, transposed, parts), out_sh...  10.2 us
    unnamed x18, local copies, waits for them, and re-layouts  3.57 us
  transfers between devices with their start and end apart: 42, of which 21 were waited for; matrix products, arithmetic and copies ran while one was open for 4% of the time, Pallas kernels for 18%

profile of v2, /device:TPU:1, one launch (start us, length us, event | category | flops | bytes accessed | tf_op | source)
XLA Modules:
  0.0 153.7 jit_solution(15921843651357006013)
XLA Ops:
  1.6 4.7 %collective-permute-start = (bf16[64,512]{0,1:T(8,128)(2,1)S(1)}, bf16[64,512]{0,1:T(8,128)(2,1)S(1)}, u32[]{:S(2)}, u32[]{:S(2)}) collective-permute-start(bf16[64,512]{0,1:T(8,128)(2,1)S(1)} %copy.15), channel_id=1, source_target_pairs={{0,32},{1,33},{2,34},{3,35},{4,36},{5,37},{6,38},{7,39},{8,40},{9,... | collective-permute-start | bytes 196616 | tf_op jit(solution)/shard_map/ppermute | solution.py:70
  6.3 2.4 %collective-permute-done = bf16[64,512]{0,1:T(8,128)(2,1)S(1)} collective-permute-done((bf16[64,512]{0,1:T(8,128)(2,1)S(1)}, bf16[64,512]{0,1:T(8,128)(2,1)S(1)}, u32[]{:S(2)}, u32[]{:S(2)}) %collective-permute-start) | collective-permute-done | bytes 65568 | tf_op jit(solution)/shard_map/ppermute | solution.py:70
  8.8 2.7 %collective-permute-start.15 = (bf16[64,512]{1,0:T(8,128)(2,1)}, bf16[64,512]{1,0:T(8,128)(2,1)S(1)}, u32[]{:S(2)}, u32[]{:S(2)}) collective-permute-start(bf16[64,512]{1,0:T(8,128)(2,1)} %param.7), channel_id=1, source_target_pairs={{0,32},{1,33},{2,34},{3,35},{4,36},{5,37},{6,38},{7,39},{8,40},{9,... | collective-permute-start | bytes 196616 | tf_op jit(solution)/shard_map/ppermute | solution.py:70
  12.8 3.0 %collective-permute-start.2 = (bf16[256,512]{0,1:T(8,128)(2,1)S(1)}, bf16[256,512]{0,1:T(8,128)(2,1)S(1)}, u32[]{:S(2)}, u32[]{:S(2)}) collective-permute-start(bf16[256,512]{0,1:T(8,128)(2,1)S(1)} %pad_maximum_fusion.5), channel_id=1, source_target_pairs={{0,16},{1,17},{2,18},{3,19},{4,20},{5,21},{6,22},{7,23},{8,24},{9,... | collective-permute-start | bytes 786440 | tf_op jit(solution)/shard_map/ppermute | solution.py:70
  20.9 2.8 %collective-permute-start.5 = (bf16[8,512,128]{2,1,0:T(8,128)(2,1)S(1)}, bf16[8,512,128]{2,1,0:T(8,128)(2,1)S(1)}, u32[]{:S(2)}, u32[]{:S(2)}) collective-permute-start(bf16[8,512,128]{2,1,0:T(8,128)(2,1)S(1)} %shard_map.77), channel_id=1, source_target_pairs={{0,3},{1,2},{2,1},{3,0},{4,7},{5,6},{6,5},{7,4},{8,11},{9,10},{10,... | collective-permute-start | bytes 3145736 | tf_op jit(solution)/shard_map/ppermute | solution.py:70
  23.7 3.0 %collective-permute-start.17 = (bf16[256,512]{1,0:T(8,128)(2,1)S(1)}, bf16[256,512]{1,0:T(8,128)(2,1)S(1)}, u32[]{:S(2)}, u32[]{:S(2)}) collective-permute-start(bf16[256,512]{1,0:T(8,128)(2,1)S(1)} %pad_maximum_fusion.9), channel_id=1, source_target_pairs={{0,16},{1,17},{2,18},{3,19},{4,20},{5,21},{6,22},{7,23},{8,24},{9,... | collective-permute-start | bytes 786440 | tf_op jit(solution)/shard_map/ppermute | solution.py:70
  32.5 2.8 %collective-permute-start.20 = (bf16[8,512,128]{2,1,0:T(8,128)(2,1)S(1)}, bf16[8,512,128]{2,1,0:T(8,128)(2,1)S(1)}, u32[]{:S(2)}, u32[]{:S(2)}) collective-permute-start(bf16[8,512,128]{2,1,0:T(8,128)(2,1)S(1)} %shard_map.80), channel_id=1, source_target_pairs={{0,3},{1,2},{2,1},{3,0},{4,7},{5,6},{6,5},{7,4},{8,11},{9,10},{10,... | collective-permute-start | bytes 3145736 | tf_op jit(solution)/shard_map/ppermute | solution.py:70
  35.3 2.5 %shard_map.75 = (bf16[8,512,128]{2,1,0:T(8,128)(2,1)S(1)}, bf16[8,512,128]{2,1,0:T(8,128)(2,1)S(1)}) custom-call(s32[2]{0:T(128)S(1)} %pad_add_fusion.me, bf16[512,512]{1,0:T(8,128)(2,1)S(1)} %copy.16.x_ref, bf16[512,4096]{1,0:T(8,128)(2,1)S(1)} %copy-done.2), custom_call_target="tpu_custom_call" | custom-call | flops 67108864 | bytes 262144 | tf_op jit(solution)/shard_map/pallas_call | solution.py:127
  37.8 2.4 %shard_map.78 = (bf16[8,512,128]{2,1,0:T(8,128)(2,1)S(1)}, bf16[8,512,128]{2,1,0:T(8,128)(2,1)S(1)}) custom-call(s32[2]{0:T(128)S(1)} %pad_add_fusion.me, bf16[512,512]{1,0:T(8,128)(2,1)S(1)} %constant_dynamic-update-slice_fusion.5.x_ref.rest_1_, bf16[4096,512]{1,0:T(8,128)(2,1)S(1)} %copy-done), custom_call_target="tpu_custom_call" | custom-call | flops 67108864 | bytes 262144 | tf_op jit(solution)/shard_map/pallas_call | solution.py:127
  42.3 2.8 %collective-permute-start.4 = (bf16[4,512,128]{2,1,0:T(8,128)(2,1)S(1)}, bf16[4,512,128]{2,1,0:T(8,128)(2,1)S(1)}, u32[]{:S(2)}, u32[]{:S(2)}) collective-permute-start(bf16[4,512,128]{2,1,0:T(8,128)(2,1)S(1)} %add_convert_fusion.3), channel_id=1, source_target_pairs={{0,3},{1,2},{2,1},{3,0},{4,7},{5,6},{6,5},{7,4},{8,11},{9,10},{10,... | collective-permute-start | bytes 1572872 | tf_op jit(solution)/shard_map/ppermute | solution.py:70
  45.1 8.3 %collective-permute-done.18 = bf16[8,512,128]{2,1,0:T(8,128)(2,1)S(1)} collective-permute-done((bf16[8,512,128]{2,1,0:T(8,128)(2,1)S(1)}, bf16[8,512,128]{2,1,0:T(8,128)(2,1)S(1)}, u32[]{:S(2)}, u32[]{:S(2)}) %collective-permute-start.18) | collective-permute-done | bytes 1048608 | tf_op jit(solution)/shard_map/ppermute | solution.py:70
  53.5 2.8 %collective-permute-start.19 = (bf16[4,512,128]{2,1,0:T(8,128)(2,1)S(1)}, bf16[4,512,128]{2,1,0:T(8,128)(2,1)S(1)}, u32[]{:S(2)}, u32[]{:S(2)}) collective-permute-start(bf16[4,512,128]{2,1,0:T(8,128)(2,1)S(1)} %add_convert_fusion.1), channel_id=1, source_target_pairs={{0,3},{1,2},{2,1},{3,0},{4,7},{5,6},{6,5},{7,4},{8,11},{9,10},{10,... | collective-permute-start | bytes 1572872 | tf_op jit(solution)/shard_map/ppermute | solution.py:70
  56.5 2.4 %collective-permute-done.6 = bf16[4,512,128]{2,1,0:T(8,128)(2,1)S(1)} collective-permute-done((bf16[4,512,128]{2,1,0:T(8,128)(2,1)S(1)}, bf16[4,512,128]{2,1,0:T(8,128)(2,1)S(1)}, u32[]{:S(2)}, u32[]{:S(2)}) %collective-permute-start.6) | collective-permute-done | bytes 524320 | tf_op jit(solution)/shard_map/ppermute | solution.py:70
  60.5 2.5 %collective-permute-start.9 = (bf16[2,512,128]{2,1,0:T(8,128)(2,1)S(1)}, bf16[2,512,128]{2,1,0:T(8,128)(2,1)S(1)}, u32[]{:S(2)}, u32[]{:S(2)}) collective-permute-start(bf16[2,512,128]{2,1,0:T(8,128)(2,1)S(1)} %pad_maximum_fusion.8), channel_id=1, source_target_pairs={{0,8},{1,9},{2,10},{3,11},{4,12},{5,13},{6,14},{7,15},{8,0},{9,1},... | collective-permute-start | bytes 786440 | tf_op jit(solution)/shard_map/ppermute | solution.py:70
  63.4 2.6 %collective-permute-done.21 = bf16[4,512,128]{2,1,0:T(8,128)(2,1)S(1)} collective-permute-done((bf16[4,512,128]{2,1,0:T(8,128)(2,1)S(1)}, bf16[4,512,128]{2,1,0:T(8,128)(2,1)S(1)}, u32[]{:S(2)}, u32[]{:S(2)}) %collective-permute-start.21) | collective-permute-done | bytes 524320 | tf_op jit(solution)/shard_map/ppermute | solution.py:70
  72.1 2.3 %collective-permute-start.11 = (bf16[2,512,128]{2,1,0:T(8,128)(2,1)S(1)}, bf16[2,512,128]{2,1,0:T(8,128)(2,1)S(1)}, u32[]{:S(2)}, u32[]{:S(2)}) collective-permute-start(bf16[2,512,128]{2,1,0:T(8,128)(2,1)S(1)} %get-tuple-element.26), channel_id=1, source_target_pairs={{0,8},{1,9},{2,10},{3,11},{4,12},{5,13},{6,14},{7,15},{8,0},{9,1},... | collective-permute-start | bytes 786440 | tf_op jit(solution)/shard_map/ppermute | solution.py:70
  79.2 3.6 %collective-permute-done.11 = bf16[2,512,128]{2,1,0:T(8,128)(2,1)S(1)} collective-permute-done((bf16[2,512,128]{2,1,0:T(8,128)(2,1)S(1)}, bf16[2,512,128]{2,1,0:T(8,128)(2,1)S(1)}, u32[]{:S(2)}, u32[]{:S(2)}) %collective-permute-start.11) | collective-permute-done | bytes 262176 | tf_op jit(solution)/shard_map/ppermute | solution.py:70
  84.5 2.7 %collective-permute-start.26 = (bf16[2,512,128]{2,1,0:T(8,128)(2,1)S(1)}, bf16[2,512,128]{2,1,0:T(8,128)(2,1)S(1)}, u32[]{:S(2)}, u32[]{:S(2)}) collective-permute-start(bf16[2,512,128]{2,1,0:T(8,128)(2,1)S(1)} %fusion.11), channel_id=1, source_target_pairs={{0,8},{1,9},{2,10},{3,11},{4,12},{5,13},{6,14},{7,15},{8,0},{9,1},... | collective-permute-start | bytes 786440 | tf_op jit(solution)/shard_map/ppermute | solution.py:70
  88.3 2.8 %collective-permute-start.13 = (bf16[4,512,128]{2,1,0:T(8,128)(2,1)S(1)}, bf16[4,512,128]{2,1,0:T(8,128)(2,1)S(1)}, u32[]{:S(2)}, u32[]{:S(2)}) collective-permute-start(bf16[4,512,128]{2,1,0:T(8,128)(2,1)S(1)} %pad_maximum_fusion.1), channel_id=1, source_target_pairs={{0,3},{1,2},{2,1},{3,0},{4,7},{5,6},{6,5},{7,4},{8,11},{9,10},{10,... | collective-permute-start | bytes 1572872 | tf_op jit(solution)/shard_map/ppermute | solution.py:70
  91.2 2.7 %collective-permute-done.26 = bf16[2,512,128]{2,1,0:T(8,128)(2,1)S(1)} collective-permute-done((bf16[2,512,128]{2,1,0:T(8,128)(2,1)S(1)}, bf16[2,512,128]{2,1,0:T(8,128)(2,1)S(1)}, u32[]{:S(2)}, u32[]{:S(2)}) %collective-permute-start.26) | collective-permute-done | bytes 262176 | tf_op jit(solution)/shard_map/ppermute | solution.py:70
  93.9 2.8 %collective-permute-done.27 = bf16[2,512,128]{2,1,0:T(8,128)(2,1)S(1)} collective-permute-done((bf16[2,512,128]{2,1,0:T(8,128)(2,1)S(1)}, bf16[2,512,128]{2,1,0:T(8,128)(2,1)S(1)}, u32[]{:S(2)}, u32[]{:S(2)}) %collective-permute-start.27) | collective-permute-done | bytes 262176 | tf_op jit(solution)/shard_map/ppermute | solution.py:70
  96.9 6.6 %collective-permute-done.13 = bf16[4,512,128]{2,1,0:T(8,128)(2,1)S(1)} collective-permute-done((bf16[4,512,128]{2,1,0:T(8,128)(2,1)S(1)}, bf16[4,512,128]{2,1,0:T(8,128)(2,1)S(1)}, u32[]{:S(2)}, u32[]{:S(2)}) %collective-permute-start.13) | collective-permute-done | bytes 524320 | tf_op jit(solution)/shard_map/ppermute | solution.py:70
  103.5 2.7 %collective-permute-start.28 = (bf16[4,512,128]{2,1,0:T(8,128)(2,1)S(1)}, bf16[4,512,128]{2,1,0:T(8,128)(2,1)S(1)}, u32[]{:S(2)}, u32[]{:S(2)}) collective-permute-start(bf16[4,512,128]{2,1,0:T(8,128)(2,1)S(1)} %pad_maximum_fusion.3), channel_id=1, source_target_pairs={{0,3},{1,2},{2,1},{3,0},{4,7},{5,6},{6,5},{7,4},{8,11},{9,10},{10,... | collective-permute-start | bytes 1572872 | tf_op jit(solution)/shard_map/ppermute | solution.py:70
  108.0 4.2 %shard_map.82 = (f32[512,512]{1,0:T(8,128)S(1)}, bf16[4096,512]{1,0:T(8,128)(2,1)}) custom-call(s32[2]{0:T(128)S(1)} %pad_add_fusion.me, bf16[8,512,128]{2,1,0:T(8,128)(2,1)S(1)} %constant_dynamic-update-slice_fusion.a_ref, bf16[8,512,128]{2,1,0:T(8,128)(2,1)S(1)} %constant_dynamic-update-slice_fusion.11.b_ref, bf16[4096,512]{1,0:T(8,128)(2,1)S(1)} %copy-done, ...), custom_call_target="tpu_custom_call" | custom-call | flops 134217728 | bytes 262144 | tf_op jit(solution)/shard_map/pallas_call | solution.py:206
  116.3 4.3 %shard_map.81 = (f32[512,512]{1,0:T(8,128)S(1)}, bf16[512,4096]{1,0:T(8,128)(2,1)}) custom-call(s32[2]{0:T(128)S(1)} %pad_add_fusion.me, bf16[8,512,128]{2,1,0:T(8,128)(2,1)S(1)} %constant_dynamic-update-slice_fusion.9.a_ref, bf16[8,512,128]{2,1,0:T(8,128)(2,1)S(1)} %constant_dynamic-update-slice_fusion.16.b_ref, bf16[512,4096]{1,0:T(8,128)(2,1)S(1)} %copy-done.2, ...), custom_call_target="tpu_custom_call" | custom-call | flops 134217728 | bytes 262144 | tf_op jit(solution)/shard_map/pallas_call | solution.py:206
  120.6 5.4 %collective-permute-done.14.a_ref = bf16[8,512,128]{2,1,0:T(8,128)(2,1)S(1)} collective-permute-done((bf16[8,512,128]{2,1,0:T(8,128)(2,1)S(1)}, bf16[8,512,128]{2,1,0:T(8,128)(2,1)S(1)}, u32[]{:S(2)}, u32[]{:S(2)}) %collective-permute-start.14) | collective-permute-done | bytes 1048608 | tf_op jit(solution)/shard_map/ppermute | solution.py:70
  126.0 4.2 %shard_map.83 = (f32[512,512]{1,0:T(8,128)S(1)}, bf16[4096,512]{1,0:T(8,128)(2,1)}) custom-call(s32[2]{0:T(128)S(1)} %pad_add_fusion.me, bf16[8,512,128]{2,1,0:T(8,128)(2,1)S(1)} %collective-permute-done.14.a_ref, bf16[8,512,128]{2,1,0:T(8,128)(2,1)S(1)} %collective-permute-done.31.b_ref, ...), custom_call_target="tpu_custom_call", output_to_operand_aliasing={{0}: (5, {}), {1}: (6, {})} | custom-call | flops 134217728 | bytes 262144 | tf_op jit(solution)/shard_map/pallas_call | solution.py:206
  132.0 5.2 %collective-permute-done.36.a_ref = bf16[8,512,128]{2,1,0:T(8,128)(2,1)S(1)} collective-permute-done((bf16[8,512,128]{2,1,0:T(8,128)(2,1)S(1)}, bf16[8,512,128]{2,1,0:T(8,128)(2,1)S(1)}, u32[]{:S(2)}, u32[]{:S(2)}) %collective-permute-start.36) | collective-permute-done | bytes 1048608 | tf_op jit(solution)/shard_map/ppermute | solution.py:70
  137.2 2.3 %shard_map.84 = f32[512,512]{1,0:T(8,128)S(1)} custom-call(s32[2]{0:T(128)S(1)} %pad_add_fusion.me, bf16[8,512,128]{2,1,0:T(8,128)(2,1)S(1)} %collective-permute-done.36.a_ref, bf16[8,512,128]{2,1,0:T(8,128)(2,1)S(1)} %collective-permute-done.37.b_ref, bf16[512,4096]{1,0:T(8,128)(2,1)S(1)} %copy-done.2, ...), custom_call_target="tpu_custom_call", output_to_operand_aliasing={{}: (4, {})} | custom-call | flops 134217728 | bytes 262144 | tf_op jit(solution)/shard_map/pallas_call | solution.py:206
  142.8 2.5 %collective-permute-start.35 = (bf16[64,512]{1,0:T(8,128)(2,1)S(1)}, bf16[64,512]{1,0:T(8,128)(2,1)S(1)}, u32[]{:S(2)}, u32[]{:S(2)}) collective-permute-start(bf16[64,512]{1,0:T(8,128)(2,1)S(1)} %get-tuple-element.74), channel_id=1, source_target_pairs={{0,64},{1,65},{2,66},{3,67},{4,68},{5,69},{6,70},{7,71},{8,72},{9,... | collective-permute-start | bytes 196616 | tf_op jit(solution)/shard_map/ppermute | solution.py:70
  146.2 3.2 %collective-permute-start.41 = (bf16[64,512]{1,0:T(8,128)(2,1)S(1)}, bf16[64,512]{1,0:T(8,128)(2,1)S(1)}, u32[]{:S(2)}, u32[]{:S(2)}) collective-permute-start(bf16[64,512]{1,0:T(8,128)(2,1)S(1)} %get-tuple-element.71), channel_id=1, source_target_pairs={{0,64},{1,65},{2,66},{3,67},{4,68},{5,69},{6,70},{7,71},{8,72},{9,... | collective-permute-start | bytes 196616 | tf_op jit(solution)/shard_map/ppermute | solution.py:70
  150.0 3.0 %shard_map.85 = bf16[512,4096]{1,0:T(8,128)(2,1)} custom-call(s32[2]{0:T(128)S(1)} %pad_add_fusion.me, bf16[8,512,128]{2,1,0:T(8,128)(2,1)S(1)} %collective-permute-done.36.a_ref, bf16[8,512,128]{2,1,0:T(8,128)(2,1)S(1)} %collective-permute-done.37.b_ref, bf16[512,512]{1,0:T(8,128)(2,1)S(1)} %fusion.39.rest_1_.rest_0_, ...), custom_call_target="tpu_custom_call", output_to_operand_aliasing={{}: (4, {})} | custom-call | flops 134217728 | bytes 262144 | tf_op jit(solution)/shard_map/pallas_call | solution.py:206
  (132 shorter events, 44.4 us)
Async XLA Ops:
  1.6 7.0 %collective-permute-start = (bf16[64,512]{0,1:T(8,128)(2,1)S(1)}, bf16[64,512]{0,1:T(8,128)(2,1)S(1)}, u32[]{:S(2)}, u32[]{:S(2)}) collective-permute-start(bf16[64,512]{0,1:T(8,128)(2,1)S(1)} %copy.15), channel_id=1, source_target_pairs={{0,32},{1,33},{2,34},{3,35},{4,36},{5,37},{6,38},{7,39},{8,40},{9,... | collective-permute-start | bytes 196616 | tf_op jit(solution)/shard_map/ppermute | solution.py:70
  20.9 19.3 %collective-permute-start.5 = (bf16[8,512,128]{2,1,0:T(8,128)(2,1)S(1)}, bf16[8,512,128]{2,1,0:T(8,128)(2,1)S(1)}, u32[]{:S(2)}, u32[]{:S(2)}) collective-permute-start(bf16[8,512,128]{2,1,0:T(8,128)(2,1)S(1)} %shard_map.77), channel_id=1, source_target_pairs={{0,3},{1,2},{2,1},{3,0},{4,7},{5,6},{6,5},{7,4},{8,11},{9,10},{10,... | collective-permute-start | bytes 3145736 | tf_op jit(solution)/shard_map/ppermute | solution.py:70
  28.1 14.0 %collective-permute-start.3 = (bf16[8,512,128]{2,1,0:T(8,128)(2,1)S(1)}, bf16[8,512,128]{2,1,0:T(8,128)(2,1)S(1)}, u32[]{:S(2)}, u32[]{:S(2)}) collective-permute-start(bf16[8,512,128]{2,1,0:T(8,128)(2,1)S(1)} %shard_map.76), channel_id=1, source_target_pairs={{0,1},{1,0},{2,3},{3,2},{4,5},{5,4},{6,7},{7,6},{8,9},{9,8},{10,11... | collective-permute-start | bytes 3145736 | tf_op jit(solution)/shard_map/ppermute | solution.py:70
  30.9 22.4 %collective-permute-start.18 = (bf16[8,512,128]{2,1,0:T(8,128)(2,1)S(1)}, bf16[8,512,128]{2,1,0:T(8,128)(2,1)S(1)}, u32[]{:S(2)}, u32[]{:S(2)}) collective-permute-start(bf16[8,512,128]{2,1,0:T(8,128)(2,1)S(1)} %shard_map.79), channel_id=1, source_target_pairs={{0,1},{1,0},{2,3},{3,2},{4,5},{5,4},{6,7},{7,6},{8,9},{9,8},{10,11... | collective-permute-start | bytes 3145736 | tf_op jit(solution)/shard_map/ppermute | solution.py:70
  32.5 23.8 %collective-permute-start.20 = (bf16[8,512,128]{2,1,0:T(8,128)(2,1)S(1)}, bf16[8,512,128]{2,1,0:T(8,128)(2,1)S(1)}, u32[]{:S(2)}, u32[]{:S(2)}) collective-permute-start(bf16[8,512,128]{2,1,0:T(8,128)(2,1)S(1)} %shard_map.80), channel_id=1, source_target_pairs={{0,3},{1,2},{2,1},{3,0},{4,7},{5,6},{6,5},{7,4},{8,11},{9,10},{10,... | collective-permute-start | bytes 3145736 | tf_op jit(solution)/shard_map/ppermute | solution.py:70
  40.3 18.6 %collective-permute-start.6 = (bf16[4,512,128]{2,1,0:T(8,128)(2,1)S(1)}, bf16[4,512,128]{2,1,0:T(8,128)(2,1)S(1)}, u32[]{:S(2)}, u32[]{:S(2)}) collective-permute-start(bf16[4,512,128]{2,1,0:T(8,128)(2,1)S(1)} %add_convert_fusion.2), channel_id=1, source_target_pairs={{0,1},{1,0},{2,3},{3,2},{4,5},{5,4},{6,7},{7,6},{8,9},{9,8},{10,11... | collective-permute-start | bytes 1572872 | tf_op jit(solution)/shard_map/ppermute | solution.py:70
  42.3 16.9 %collective-permute-start.4 = (bf16[4,512,128]{2,1,0:T(8,128)(2,1)S(1)}, bf16[4,512,128]{2,1,0:T(8,128)(2,1)S(1)}, u32[]{:S(2)}, u32[]{:S(2)}) collective-permute-start(bf16[4,512,128]{2,1,0:T(8,128)(2,1)S(1)} %add_convert_fusion.3), channel_id=1, source_target_pairs={{0,3},{1,2},{2,1},{3,0},{4,7},{5,6},{6,5},{7,4},{8,11},{9,10},{10,... | collective-permute-start | bytes 1572872 | tf_op jit(solution)/shard_map/ppermute | solution.py:70
  53.5 9.7 %collective-permute-start.19 = (bf16[4,512,128]{2,1,0:T(8,128)(2,1)S(1)}, bf16[4,512,128]{2,1,0:T(8,128)(2,1)S(1)}, u32[]{:S(2)}, u32[]{:S(2)}) collective-permute-start(bf16[4,512,128]{2,1,0:T(8,128)(2,1)S(1)} %add_convert_fusion.1), channel_id=1, source_target_pairs={{0,3},{1,2},{2,1},{3,0},{4,7},{5,6},{6,5},{7,4},{8,11},{9,10},{10,... | collective-permute-start | bytes 1572872 | tf_op jit(solution)/shard_map/ppermute | solution.py:70
  56.4 9.6 %collective-permute-start.21 = (bf16[4,512,128]{2,1,0:T(8,128)(2,1)S(1)}, bf16[4,512,128]{2,1,0:T(8,128)(2,1)S(1)}, u32[]{:S(2)}, u32[]{:S(2)}) collective-permute-start(bf16[4,512,128]{2,1,0:T(8,128)(2,1)S(1)} %add_convert_fusion), channel_id=1, source_target_pairs={{0,1},{1,0},{2,3},{3,2},{4,5},{5,4},{6,7},{7,6},{8,9},{9,8},{10,11... | collective-permute-start | bytes 1572872 | tf_op jit(solution)/shard_map/ppermute | solution.py:70
  59.5 8.4 %collective-permute-start.7 = (bf16[2,512,128]{2,1,0:T(8,128)(2,1)S(1)}, bf16[2,512,128]{2,1,0:T(8,128)(2,1)S(1)}, u32[]{:S(2)}, u32[]{:S(2)}) collective-permute-start(bf16[2,512,128]{2,1,0:T(8,128)(2,1)S(1)} %pad_maximum_fusion.6), channel_id=1, source_target_pairs={{0,4},{1,5},{2,6},{3,7},{4,0},{5,1},{6,2},{7,3},{8,12},{9,13},{10,... | collective-permute-start | bytes 786440 | tf_op jit(solution)/shard_map/ppermute | solution.py:70
  59.6 10.5 %collective-permute-start.8 = (bf16[2,512,128]{2,1,0:T(8,128)(2,1)S(1)}, bf16[2,512,128]{2,1,0:T(8,128)(2,1)S(1)}, u32[]{:S(2)}, u32[]{:S(2)}) collective-permute-start(bf16[2,512,128]{2,1,0:T(8,128)(2,1)S(1)} %pad_maximum_fusion.7), channel_id=1, source_target_pairs={{0,12},{1,13},{2,14},{3,15},{4,8},{5,9},{6,10},{7,11},{8,4},{9,5},... | collective-permute-start | bytes 786440 | tf_op jit(solution)/shard_map/ppermute | solution.py:70
  60.5 11.2 %collective-permute-start.9 = (bf16[2,512,128]{2,1,0:T(8,128)(2,1)S(1)}, bf16[2,512,128]{2,1,0:T(8,128)(2,1)S(1)}, u32[]{:S(2)}, u32[]{:S(2)}) collective-permute-start(bf16[2,512,128]{2,1,0:T(8,128)(2,1)S(1)} %pad_maximum_fusion.8), channel_id=1, source_target_pairs={{0,8},{1,9},{2,10},{3,11},{4,12},{5,13},{6,14},{7,15},{8,0},{9,1},... | collective-permute-start | bytes 786440 | tf_op jit(solution)/shard_map/ppermute | solution.py:70
  66.3 8.2 %collective-permute-start.22 = (bf16[2,512,128]{2,1,0:T(8,128)(2,1)S(1)}, bf16[2,512,128]{2,1,0:T(8,128)(2,1)S(1)}, u32[]{:S(2)}, u32[]{:S(2)}) collective-permute-start(bf16[2,512,128]{2,1,0:T(8,128)(2,1)S(1)} %pad_maximum_fusion.10), channel_id=1, source_target_pairs={{0,4},{1,5},{2,6},{3,7},{4,0},{5,1},{6,2},{7,3},{8,12},{9,13},{10,... | collective-permute-start | bytes 786440 | tf_op jit(solution)/shard_map/ppermute | solution.py:70
  66.5 9.7 %collective-permute-start.23 = (bf16[2,512,128]{2,1,0:T(8,128)(2,1)S(1)}, bf16[2,512,128]{2,1,0:T(8,128)(2,1)S(1)}, u32[]{:S(2)}, u32[]{:S(2)}) collective-permute-start(bf16[2,512,128]{2,1,0:T(8,128)(2,1)S(1)} %pad_maximum_fusion.11), channel_id=1, source_target_pairs={{0,12},{1,13},{2,14},{3,15},{4,8},{5,9},{6,10},{7,11},{8,4},{9,5},... | collective-permute-start | bytes 786440 | tf_op jit(solution)/shard_map/ppermute | solution.py:70
  67.9 9.2 %collective-permute-start.24 = (bf16[2,512,128]{2,1,0:T(8,128)(2,1)S(1)}, bf16[2,512,128]{2,1,0:T(8,128)(2,1)S(1)}, u32[]{:S(2)}, u32[]{:S(2)}) collective-permute-start(bf16[2,512,128]{2,1,0:T(8,128)(2,1)S(1)} %pad_maximum_fusion.12), channel_id=1, source_target_pairs={{0,8},{1,9},{2,10},{3,11},{4,12},{5,13},{6,14},{7,15},{8,0},{9,1},... | collective-permute-start | bytes 786440 | tf_op jit(solution)/shard_map/ppermute | solution.py:70
  72.0 7.1 %collective-permute-start.10 = (bf16[2,512,128]{2,1,0:T(8,128)(2,1)S(1)}, bf16[2,512,128]{2,1,0:T(8,128)(2,1)S(1)}, u32[]{:S(2)}, u32[]{:S(2)}) collective-permute-start(bf16[2,512,128]{2,1,0:T(8,128)(2,1)S(1)} %get-tuple-element.26), channel_id=1, source_target_pairs={{0,4},{1,5},{2,6},{3,7},{4,0},{5,1},{6,2},{7,3},{8,12},{9,13},{10,... | collective-permute-start | bytes 786440 | tf_op jit(solution)/shard_map/ppermute | solution.py:70
  72.1 10.7 %collective-permute-start.11 = (bf16[2,512,128]{2,1,0:T(8,128)(2,1)S(1)}, bf16[2,512,128]{2,1,0:T(8,128)(2,1)S(1)}, u32[]{:S(2)}, u32[]{:S(2)}) collective-permute-start(bf16[2,512,128]{2,1,0:T(8,128)(2,1)S(1)} %get-tuple-element.26), channel_id=1, source_target_pairs={{0,8},{1,9},{2,10},{3,11},{4,12},{5,13},{6,14},{7,15},{8,0},{9,1},... | collective-permute-start | bytes 786440 | tf_op jit(solution)/shard_map/ppermute | solution.py:70
  74.5 9.6 %collective-permute-start.12 = (bf16[2,512,128]{2,1,0:T(8,128)(2,1)S(1)}, bf16[2,512,128]{2,1,0:T(8,128)(2,1)S(1)}, u32[]{:S(2)}, u32[]{:S(2)}) collective-permute-start(bf16[2,512,128]{2,1,0:T(8,128)(2,1)S(1)} %get-tuple-element.26), channel_id=1, source_target_pairs={{0,12},{1,13},{2,14},{3,15},{4,8},{5,9},{6,10},{7,11},{8,4},{9,5},... | collective-permute-start | bytes 786440 | tf_op jit(solution)/shard_map/ppermute | solution.py:70
  84.5 9.4 %collective-permute-start.26 = (bf16[2,512,128]{2,1,0:T(8,128)(2,1)S(1)}, bf16[2,512,128]{2,1,0:T(8,128)(2,1)S(1)}, u32[]{:S(2)}, u32[]{:S(2)}) collective-permute-start(bf16[2,512,128]{2,1,0:T(8,128)(2,1)S(1)} %fusion.11), channel_id=1, source_target_pairs={{0,8},{1,9},{2,10},{3,11},{4,12},{5,13},{6,14},{7,15},{8,0},{9,1},... | collective-permute-start | bytes 786440 | tf_op jit(solution)/shard_map/ppermute | solution.py:70
  87.2 9.5 %collective-permute-start.27 = (bf16[2,512,128]{2,1,0:T(8,128)(2,1)S(1)}, bf16[2,512,128]{2,1,0:T(8,128)(2,1)S(1)}, u32[]{:S(2)}, u32[]{:S(2)}) collective-permute-start(bf16[2,512,128]{2,1,0:T(8,128)(2,1)S(1)} %fusion.11), channel_id=1, source_target_pairs={{0,12},{1,13},{2,14},{3,15},{4,8},{5,9},{6,10},{7,11},{8,4},{9,5},... | collective-permute-start | bytes 786440 | tf_op jit(solution)/shard_map/ppermute | solution.py:70
  88.3 15.1 %collective-permute-start.13 = (bf16[4,512,128]{2,1,0:T(8,128)(2,1)S(1)}, bf16[4,512,128]{2,1,0:T(8,128)(2,1)S(1)}, u32[]{:S(2)}, u32[]{:S(2)}) collective-permute-start(bf16[4,512,128]{2,1,0:T(8,128)(2,1)S(1)} %pad_maximum_fusion.1), channel_id=1, source_target_pairs={{0,3},{1,2},{2,1},{3,0},{4,7},{5,6},{6,5},{7,4},{8,11},{9,10},{10,... | collective-permute-start | bytes 1572872 | tf_op jit(solution)/shard_map/ppermute | solution.py:70
  91.1 15.1 %collective-permute-start.29 = (bf16[4,512,128]{2,1,0:T(8,128)(2,1)S(1)}, bf16[4,512,128]{2,1,0:T(8,128)(2,1)S(1)}, u32[]{:S(2)}, u32[]{:S(2)}) collective-permute-start(bf16[4,512,128]{2,1,0:T(8,128)(2,1)S(1)} %pad_maximum_fusion.2), channel_id=1, source_target_pairs={{0,1},{1,0},{2,3},{3,2},{4,5},{5,4},{6,7},{7,6},{8,9},{9,8},{10,11... | collective-permute-start | bytes 1572872 | tf_op jit(solution)/shard_map/ppermute | solution.py:70
  103.5 9.6 %collective-permute-start.28 = (bf16[4,512,128]{2,1,0:T(8,128)(2,1)S(1)}, bf16[4,512,128]{2,1,0:T(8,128)(2,1)S(1)}, u32[]{:S(2)}, u32[]{:S(2)}) collective-permute-start(bf16[4,512,128]{2,1,0:T(8,128)(2,1)S(1)} %pad_maximum_fusion.3), channel_id=1, source_target_pairs={{0,3},{1,2},{2,1},{3,0},{4,7},{5,6},{6,5},{7,4},{8,11},{9,10},{10,... | collective-permute-start | bytes 1572872 | tf_op jit(solution)/shard_map/ppermute | solution.py:70
  106.3 8.4 %collective-permute-start.30 = (bf16[4,512,128]{2,1,0:T(8,128)(2,1)S(1)}, bf16[4,512,128]{2,1,0:T(8,128)(2,1)S(1)}, u32[]{:S(2)}, u32[]{:S(2)}) collective-permute-start(bf16[4,512,128]{2,1,0:T(8,128)(2,1)S(1)} %pad_maximum_fusion.4), channel_id=1, source_target_pairs={{0,1},{1,0},{2,3},{3,2},{4,5},{5,4},{6,7},{7,6},{8,9},{9,8},{10,11... | collective-permute-start | bytes 1572872 | tf_op jit(solution)/shard_map/ppermute | solution.py:70
  106.4 19.5 %collective-permute-start.14 = (bf16[8,512,128]{2,1,0:T(8,128)(2,1)S(1)}, bf16[8,512,128]{2,1,0:T(8,128)(2,1)S(1)}, u32[]{:S(2)}, u32[]{:S(2)}) collective-permute-start(bf16[8,512,128]{2,1,0:T(8,128)(2,1)S(1)} %constant_dynamic-update-slice_fusion.a_ref), channel_id=1, source_target_pairs={{0,1},{1,0},{2,3},{3,2},{4,5},{5,4},{6,7},{7,6},{8,9},{9,8},{10,11... | collective-permute-start | bytes 3145736 | tf_op jit(solution)/shard_map/ppermute | solution.py:70
  107.9 18.1 %collective-permute-start.31 = (bf16[8,512,128]{2,1,0:T(8,128)(2,1)S(1)}, bf16[8,512,128]{2,1,0:T(8,128)(2,1)S(1)}, u32[]{:S(2)}, u32[]{:S(2)}) collective-permute-start(bf16[8,512,128]{2,1,0:T(8,128)(2,1)S(1)} %constant_dynamic-update-slice_fusion.11.b_ref), channel_id=1, source_target_pairs={{0,3},{1,2},{2,1},{3,0},{4,7},{5,6},{6,5},{7,4},{8,11},{9,10},{10,... | collective-permute-start | bytes 3145736 | tf_op jit(solution)/shard_map/ppermute | solution.py:70
  113.2 24.0 %collective-permute-start.36 = (bf16[8,512,128]{2,1,0:T(8,128)(2,1)S(1)}, bf16[8,512,128]{2,1,0:T(8,128)(2,1)S(1)}, u32[]{:S(2)}, u32[]{:S(2)}) collective-permute-start(bf16[8,512,128]{2,1,0:T(8,128)(2,1)S(1)} %constant_dynamic-update-slice_fusion.9.a_ref), channel_id=1, source_target_pairs={{0,1},{1,0},{2,3},{3,2},{4,5},{5,4},{6,7},{7,6},{8,9},{9,8},{10,11... | collective-permute-start | bytes 3145736 | tf_op jit(solution)/shard_map/ppermute | solution.py:70
  114.8 22.4 %collective-permute-start.37 = (bf16[8,512,128]{2,1,0:T(8,128)(2,1)S(1)}, bf16[8,512,128]{2,1,0:T(8,128)(2,1)S(1)}, u32[]{:S(2)}, u32[]{:S(2)}) collective-permute-start(bf16[8,512,128]{2,1,0:T(8,128)(2,1)S(1)} %constant_dynamic-update-slice_fusion.16.b_ref), channel_id=1, source_target_pairs={{0,3},{1,2},{2,1},{3,0},{4,7},{5,6},{6,5},{7,4},{8,11},{9,10},{10,... | collective-permute-start | bytes 3145736 | tf_op jit(solution)/shard_map/ppermute | solution.py:70
  130.2 11.0 %collective-permute-start.32 = (bf16[256,512]{1,0:T(8,128)(2,1)S(1)}, bf16[256,512]{1,0:T(8,128)(2,1)S(1)}, u32[]{:S(2)}, u32[]{:S(2)}) collective-permute-start(bf16[256,512]{1,0:T(8,128)(2,1)S(1)} %slice.350), channel_id=1, source_target_pairs={{0,16},{1,17},{2,18},{3,19},{4,20},{5,21},{6,22},{7,23},{8,24},{9,... | collective-permute-start | bytes 786440 | tf_op jit(solution)/shard_map/ppermute | solution.py:70
  141.9 7.4 %collective-permute-start.34 = (bf16[64,512]{1,0:T(8,128)(2,1)S(1)}, bf16[64,512]{1,0:T(8,128)(2,1)S(1)}, u32[]{:S(2)}, u32[]{:S(2)}) collective-permute-start(bf16[64,512]{1,0:T(8,128)(2,1)S(1)} %get-tuple-element.75), channel_id=1, source_target_pairs={{0,96},{1,97},{2,98},{3,99},{4,100},{5,101},{6,102},{7,103},{8,104... | collective-permute-start | bytes 196616 | tf_op jit(solution)/shard_map/ppermute | solution.py:70
  145.4 7.6 %collective-permute-start.39 = (bf16[64,512]{1,0:T(8,128)(2,1)S(1)}, bf16[64,512]{1,0:T(8,128)(2,1)S(1)}, u32[]{:S(2)}, u32[]{:S(2)}) collective-permute-start(bf16[64,512]{1,0:T(8,128)(2,1)S(1)} %get-tuple-element.70), channel_id=1, source_target_pairs={{0,32},{1,33},{2,34},{3,35},{4,36},{5,37},{6,38},{7,39},{8,40},{9,... | collective-permute-start | bytes 196616 | tf_op jit(solution)/shard_map/ppermute | solution.py:70
  146.0 7.0 %collective-permute-start.40 = (bf16[64,512]{1,0:T(8,128)(2,1)S(1)}, bf16[64,512]{1,0:T(8,128)(2,1)S(1)}, u32[]{:S(2)}, u32[]{:S(2)}) collective-permute-start(bf16[64,512]{1,0:T(8,128)(2,1)S(1)} %get-tuple-element.72), channel_id=1, source_target_pairs={{0,96},{1,97},{2,98},{3,99},{4,100},{5,101},{6,102},{7,103},{8,104... | collective-permute-start | bytes 196616 | tf_op jit(solution)/shard_map/ppermute | solution.py:70
  (14 other events, 81.7 us)

commit v3 on v2

--- a/solution.py
+++ b/solution.py
@@ -162,7 +162,9 @@
                 block, y_ref[...], (((0,), (0,)), ((), ())), preferred_element_type=F32
             ).astype(BF16)
         elif grad is not None:
-            grad[...] = jnp.dot(y_ref[...], block, preferred_element_type=F32).astype(BF16)
+            grad[...] = lax.dot_general(
+                y_ref[...], block, (((0,), (0,)), ((), ())), preferred_element_type=F32
+            ).astype(BF16)
         if total is not None:
             dims = ((1,), (0,)) if transposed else ((1,), (1,))
             added = lax.dot_general(block, w_ref[...], (dims, ((), ())), preferred_element_type=F32)
@@ -238,19 +240,38 @@
     normed = join(normed, send(normed, FIRST_Z))
     d_out = join(d_out, send(d_out, FIRST_Z))
     normed = join(normed, send(normed, SECOND_Z))
-    d_out = join(d_out, send(after(d_out, normed), SECOND_Z))
+    got = send(after(d_out, normed), SECOND_Z)
     normed = join(normed, send(normed, CORES))
-    d_out = join(d_out, send(d_out, CORES))
-    return normed, d_out
-
-
-def scatter_rows(total):
-    half = total.shape[0] // 2
-    total = add(total[:half], send(total[half:].astype(BF16), CORES))
+    return normed, (d_out, got)
+
+
+def stage(values, *earlier):
+    values, unused = lax.optimization_barrier((values, earlier))
+    return values
+
+
+def fuse(blocks):
+    blocks = [block.astype(BF16) for block in blocks]
+    return blocks[0] if len(blocks) == 1 else jnp.stack(blocks)
+
+
+def split(block, count):
+    return [block] if count == 1 else [block[n] for n in range(count)]
+
+
+def scatter_rows(totals):
+    count = len(totals)
+    half = totals[0].shape[0] // 2
+    got = split(send(fuse([total[half:] for total in totals]), CORES), count)
+    totals = [add(total[:half], other) for total, other in zip(totals, got)]
     rows = half // 4
-    parts = [total[rows * n : rows * (n + 1)] for n in range(4)]
-    got = [send(parts[n].astype(BF16), perm) for n, perm in ((1, FIRST_Z), (2, SECOND_Z), (3, ACROSS_Z))]
-    return add(parts[0], *got).astype(BF16)
+    kept = [total[:rows] for total in totals]
+    sent = [fuse([total[rows * n : rows * (n + 1)] for total in totals]) for n in range(1, 4)]
+    got = [
+        split(send(block, perm), count)
+        for block, perm in zip(sent, (FIRST_Z, SECOND_Z, ACROSS_Z))
+    ]
+    return [add(kept[n], *[g[n] for g in got]).astype(BF16) for n in range(count)], sent
 
 
 def halve_first(x, w, me, transposed):
@@ -290,9 +311,13 @@
 
 def shards(normed, w_in, w_out, d_out):
     me = places()
-    inputs, cotangent = gather_rows(normed, d_out)
-    turned = inputs.T
-    p_near, p_got = halve_first(inputs, w_in, me, False)
+    inputs, rows = gather_rows(normed, d_out)
+    p_out = [produce(inputs, w_in, me, False, (0,), 1)[0]]
+    cotangent = join(*rows)
+    cotangent = join(cotangent, send(cotangent, CORES))
+    p_out.append(produce(inputs, w_in, me, False, (1,), 1)[0])
+    p_got = [send(p_out[h], PRIMARY[h]) for h in range(2)]
+    p_near = produce(inputs, w_in, me, False, (0, 1), 0)
     d_near, d_got = halve_first(cotangent, w_out, me, True)
     p_four = halve_second(p_near, p_got)
     d_four = halve_second(d_near, d_got)
@@ -303,20 +328,18 @@
     p_four = spread_first(act)
     d_pre = (d_act * gelu_slope(preact)).astype(BF16)
     p_near = spread_second(p_four)
-    d_four = spread_first(after(d_pre, *p_four))
+    d_four = spread_first(d_pre)
     p_far = spread_third(p_near)
     d_near = spread_second([after(d_four[h], p_near[h]) for h in range(2)])
     total, grad = consume(p_near[0], p_near[1], w_out, cotangent, me, True, 0)
     d_far = spread_third([after(d_near[h], total) for h in range(2)])
-    d_total, d_grad = consume(d_near[0], d_near[1], w_in, turned, me, False, 0)
+    d_total, d_grad = consume(d_near[0], d_near[1], w_in, inputs, me, False, 0)
     p_far[0] = after(p_far[0], d_total)
     total, grad_out = consume(p_far[0], p_far[1], w_out, cotangent, me, True, 1, total, grad)
-    ffn_out = scatter_rows(total)
-    (d_total,) = consume(d_far[0], d_far[1], w_in, turned, me, False, 1, d_total, None, ("total",))
-    d_normed = scatter_rows(d_total)
-    (grad_in,) = consume(
-        after(d_far[0], d_total), d_far[1], w_in, turned, me, False, 1, None, d_grad, ("grad",)
-    )
+    (d_total,) = consume(d_far[0], d_far[1], w_in, inputs, me, False, 1, d_total, None, ("total",))
+    (ffn_out, d_normed), sent = scatter_rows([total, d_total])
+    d_far = stage(d_far, d_total, sent)
+    (grad_in,) = consume(d_far[0], d_far[1], w_in, inputs, me, False, 1, None, d_grad, ("grad",))
     return (ffn_out, d_normed, grad_in, grad_out)
 
 

time: 154 us -> 146 us (0.948)
  starting transfers between devices: 61.1 us -> 48.8 us
  waiting for transfers between devices: 53.3 us -> 57.9 us
    ppermute x42 -> x38, starting transfers between devices: 61.1 us -> 48.8 us  [send(): return lax.ppermute(block, BOTH, perm)]
    ppermute x42 -> x38, waiting for transfers between devices: 53.3 us -> 57.9 us  [send(): return lax.ppermute(block, BOTH, perm)]
    unnamed x18 -> x15, local copies, waits for them, and re-layouts: 3.57 us -> 3.15 us
  transfers between devices with their start and end apart: 42 -> 38, of which waited for: 21 -> 24; matrix products, arithmetic and copies ran while one was open for 4% -> 4% of each run, Pallas kernels for 18% -> 18%
where the time goes in v3:
time: 146 us
  waiting for transfers between devices  57.9 us (40%)
  starting transfers between devices  48.8 us (33%)
  Pallas kernels  28.2 us (19%)
  other arithmetic  5.37 us (4%)
  local copies, waits for them, and re-layouts  4.17 us (3%)
    ppermute x38, waiting for transfers between devices, send(): return lax.ppermute(block, BOTH, perm)  57.9 us
    ppermute x38, starting transfers between devices, send(): return lax.ppermute(block, BOTH, perm)  48.8 us
    pallas_call x5, Pallas kernels, consume(): pl.pallas_call(functools.partial(consume_body, transposed, total is not N...  18 us
    pallas_call x6, Pallas kernels, produce(): pl.pallas_call(functools.partial(produce_body, transposed, parts), out_sh...  10.2 us
    unnamed x15, local copies, waits for them, and re-layouts  3.15 us
  transfers between devices with their start and end apart: 38, of which 24 were waited for; matrix products, arithmetic and copies ran while one was open for 4% of the time, Pallas kernels for 18%

profile of v3, /device:TPU:1, one launch (start us, length us, event | category | flops | bytes accessed | tf_op | source)
XLA Modules:
  0.0 145.6 jit_solution(3356825121514553669)
XLA Ops:
  0.6 4.7 %collective-permute-start = (bf16[64,512]{1,0:T(8,128)(2,1)}, bf16[64,512]{1,0:T(8,128)(2,1)S(1)}, u32[]{:S(2)}, u32[]{:S(2)}) collective-permute-start(bf16[64,512]{1,0:T(8,128)(2,1)} %param.4), channel_id=1, source_target_pairs={{0,32},{1,33},{2,34},{3,35},{4,36},{5,37},{6,38},{7,39},{8,40},{9,... | collective-permute-start | bytes 196616 | tf_op jit(solution)/shard_map/ppermute | solution.py:70
  9.0 2.9 %collective-permute-done.1 = bf16[128,512]{1,0:T(8,128)(2,1)S(1)} collective-permute-done((bf16[128,512]{1,0:T(8,128)(2,1)S(1)}, bf16[128,512]{1,0:T(8,128)(2,1)S(1)}, u32[]{:S(2)}, u32[]{:S(2)}) %collective-permute-start.1) | collective-permute-done | bytes 131104 | tf_op jit(solution)/shard_map/ppermute | solution.py:70
  12.0 2.8 %collective-permute-start.2 = (bf16[256,512]{1,0:T(8,128)(2,1)S(1)}, bf16[256,512]{1,0:T(8,128)(2,1)S(1)}, u32[]{:S(2)}, u32[]{:S(2)}) collective-permute-start(bf16[256,512]{1,0:T(8,128)(2,1)S(1)} %get-tuple-element.104), channel_id=1, source_target_pairs={{0,16},{1,17},{2,18},{3,19},{4,20},{5,21},{6,22},{7,23},{8,24},{9,... | collective-permute-start | bytes 786440 | tf_op jit(solution)/shard_map/ppermute | solution.py:70
  15.9 2.2 %copy-done.1 = bf16[512,4096]{1,0:T(8,128)(2,1)S(1)} copy-done((bf16[512,4096]{1,0:T(8,128)(2,1)S(1)}, bf16[512,4096]{1,0:T(8,128)(2,1)}, u32[]{:S(2)}) %copy-start.1) | copy-done | bytes 4194328
  19.4 2.8 %collective-permute-start.5 = (bf16[8,512,128]{2,1,0:T(8,128)(2,1)S(1)}, bf16[8,512,128]{2,1,0:T(8,128)(2,1)S(1)}, u32[]{:S(2)}, u32[]{:S(2)}) collective-permute-start(bf16[8,512,128]{2,1,0:T(8,128)(2,1)S(1)} %shard_map.77), channel_id=1, source_target_pairs={{0,3},{1,2},{2,1},{3,0},{4,7},{5,6},{6,5},{7,4},{8,11},{9,10},{10,... | collective-permute-start | bytes 3145736 | tf_op jit(solution)/shard_map/ppermute | solution.py:70
  22.3 3.3 %collective-permute-start.17 = (bf16[256,512]{1,0:T(8,128)(2,1)S(1)}, bf16[256,512]{1,0:T(8,128)(2,1)S(1)}, u32[]{:S(2)}, u32[]{:S(2)}) collective-permute-start(bf16[256,512]{1,0:T(8,128)(2,1)S(1)} %pad_maximum_fusion.8), channel_id=1, source_target_pairs={{0,16},{1,17},{2,18},{3,19},{4,20},{5,21},{6,22},{7,23},{8,24},{9,... | collective-permute-start | bytes 786440 | tf_op jit(solution)/shard_map/ppermute | solution.py:70
  29.7 2.0 %collective-permute-start.20 = (bf16[8,512,128]{2,1,0:T(8,128)(2,1)S(1)}, bf16[8,512,128]{2,1,0:T(8,128)(2,1)S(1)}, u32[]{:S(2)}, u32[]{:S(2)}) collective-permute-start(bf16[8,512,128]{2,1,0:T(8,128)(2,1)S(1)} %shard_map.80), channel_id=1, source_target_pairs={{0,3},{1,2},{2,1},{3,0},{4,7},{5,6},{6,5},{7,4},{8,11},{9,10},{10,... | collective-permute-start | bytes 3145736 | tf_op jit(solution)/shard_map/ppermute | solution.py:70
  33.5 2.5 %shard_map.75 = (bf16[8,512,128]{2,1,0:T(8,128)(2,1)S(1)}, bf16[8,512,128]{2,1,0:T(8,128)(2,1)S(1)}) custom-call(s32[2]{0:T(128)S(1)} %pad_add_fusion.me, bf16[512,512]{1,0:T(8,128)(2,1)S(1)} %constant_dynamic-update-slice_fusion.3.x_ref.rest_1_.rest_0_, bf16[512,4096]{1,0:T(8,128)(2,1)S(1)} %copy-done.1), custom_call_target="tpu_custom_call" | custom-call | flops 67108864 | bytes 262144 | tf_op jit(solution)/shard_map/pallas_call | solution.py:127
  36.0 2.4 %shard_map.78 = (bf16[8,512,128]{2,1,0:T(8,128)(2,1)S(1)}, bf16[8,512,128]{2,1,0:T(8,128)(2,1)S(1)}) custom-call(s32[2]{0:T(128)S(1)} %pad_add_fusion.me, bf16[512,512]{1,0:T(8,128)(2,1)S(1)} %constant_dynamic-update-slice_fusion.12.x_ref.rest_1_, bf16[4096,512]{1,0:T(8,128)(2,1)S(1)} %copy-done), custom_call_target="tpu_custom_call" | custom-call | flops 67108864 | bytes 262144 | tf_op jit(solution)/shard_map/pallas_call | solution.py:127
  41.1 2.8 %collective-permute-start.4 = (bf16[4,512,128]{2,1,0:T(8,128)(2,1)S(1)}, bf16[4,512,128]{2,1,0:T(8,128)(2,1)S(1)}, u32[]{:S(2)}, u32[]{:S(2)}) collective-permute-start(bf16[4,512,128]{2,1,0:T(8,128)(2,1)S(1)} %add_convert_fusion.3), channel_id=1, source_target_pairs={{0,3},{1,2},{2,1},{3,0},{4,7},{5,6},{6,5},{7,4},{8,11},{9,10},{10,... | collective-permute-start | bytes 1572872 | tf_op jit(solution)/shard_map/ppermute | solution.py:70
  43.9 2.1 %collective-permute-done.20 = bf16[8,512,128]{2,1,0:T(8,128)(2,1)S(1)} collective-permute-done((bf16[8,512,128]{2,1,0:T(8,128)(2,1)S(1)}, bf16[8,512,128]{2,1,0:T(8,128)(2,1)S(1)}, u32[]{:S(2)}, u32[]{:S(2)}) %collective-permute-start.20) | collective-permute-done | bytes 1048608 | tf_op jit(solution)/shard_map/ppermute | solution.py:70
  46.2 5.9 %collective-permute-done.18 = bf16[8,512,128]{2,1,0:T(8,128)(2,1)S(1)} collective-permute-done((bf16[8,512,128]{2,1,0:T(8,128)(2,1)S(1)}, bf16[8,512,128]{2,1,0:T(8,128)(2,1)S(1)}, u32[]{:S(2)}, u32[]{:S(2)}) %collective-permute-start.18) | collective-permute-done | bytes 1048608 | tf_op jit(solution)/shard_map/ppermute | solution.py:70
  52.3 2.8 %collective-permute-start.19 = (bf16[4,512,128]{2,1,0:T(8,128)(2,1)S(1)}, bf16[4,512,128]{2,1,0:T(8,128)(2,1)S(1)}, u32[]{:S(2)}, u32[]{:S(2)}) collective-permute-start(bf16[4,512,128]{2,1,0:T(8,128)(2,1)S(1)} %add_convert_fusion.1), channel_id=1, source_target_pairs={{0,3},{1,2},{2,1},{3,0},{4,7},{5,6},{6,5},{7,4},{8,11},{9,10},{10,... | collective-permute-start | bytes 1572872 | tf_op jit(solution)/shard_map/ppermute | solution.py:70
  55.1 2.7 %collective-permute-done.6 = bf16[4,512,128]{2,1,0:T(8,128)(2,1)S(1)} collective-permute-done((bf16[4,512,128]{2,1,0:T(8,128)(2,1)S(1)}, bf16[4,512,128]{2,1,0:T(8,128)(2,1)S(1)}, u32[]{:S(2)}, u32[]{:S(2)}) %collective-permute-start.6) | collective-permute-done | bytes 524320 | tf_op jit(solution)/shard_map/ppermute | solution.py:70
  65.9 2.9 %collective-permute-done.8 = bf16[2,512,128]{2,1,0:T(8,128)(2,1)S(1)} collective-permute-done((bf16[2,512,128]{2,1,0:T(8,128)(2,1)S(1)}, bf16[2,512,128]{2,1,0:T(8,128)(2,1)S(1)}, u32[]{:S(2)}, u32[]{:S(2)}) %collective-permute-start.8) | collective-permute-done | bytes 262176 | tf_op jit(solution)/shard_map/ppermute | solution.py:70
  70.3 2.4 %collective-permute-start.11 = (bf16[2,512,128]{2,1,0:T(8,128)(2,1)S(1)}, bf16[2,512,128]{2,1,0:T(8,128)(2,1)S(1)}, u32[]{:S(2)}, u32[]{:S(2)}) collective-permute-start(bf16[2,512,128]{2,1,0:T(8,128)(2,1)S(1)} %get-tuple-element.26), channel_id=1, source_target_pairs={{0,8},{1,9},{2,10},{3,11},{4,12},{5,13},{6,14},{7,15},{8,0},{9,1},... | collective-permute-start | bytes 786440 | tf_op jit(solution)/shard_map/ppermute | solution.py:70
  76.0 2.3 %collective-permute-start.26 = (bf16[2,512,128]{2,1,0:T(8,128)(2,1)S(1)}, bf16[2,512,128]{2,1,0:T(8,128)(2,1)S(1)}, u32[]{:S(2)}, u32[]{:S(2)}) collective-permute-start(bf16[2,512,128]{2,1,0:T(8,128)(2,1)S(1)} %fusion.11), channel_id=1, source_target_pairs={{0,8},{1,9},{2,10},{3,11},{4,12},{5,13},{6,14},{7,15},{8,0},{9,1},... | collective-permute-start | bytes 786440 | tf_op jit(solution)/shard_map/ppermute | solution.py:70
  78.3 2.4 %collective-permute-done.10 = bf16[2,512,128]{2,1,0:T(8,128)(2,1)S(1)} collective-permute-done((bf16[2,512,128]{2,1,0:T(8,128)(2,1)S(1)}, bf16[2,512,128]{2,1,0:T(8,128)(2,1)S(1)}, u32[]{:S(2)}, u32[]{:S(2)}) %collective-permute-start.10) | collective-permute-done | bytes 262176 | tf_op jit(solution)/shard_map/ppermute | solution.py:70
  81.4 2.8 %collective-permute-start.13 = (bf16[4,512,128]{2,1,0:T(8,128)(2,1)S(1)}, bf16[4,512,128]{2,1,0:T(8,128)(2,1)S(1)}, u32[]{:S(2)}, u32[]{:S(2)}) collective-permute-start(bf16[4,512,128]{2,1,0:T(8,128)(2,1)S(1)} %pad_maximum_fusion), channel_id=1, source_target_pairs={{0,3},{1,2},{2,1},{3,0},{4,7},{5,6},{6,5},{7,4},{8,11},{9,10},{10,... | collective-permute-start | bytes 1572872 | tf_op jit(solution)/shard_map/ppermute | solution.py:70
  86.5 9.7 %collective-permute-done.29 = bf16[4,512,128]{2,1,0:T(8,128)(2,1)S(1)} collective-permute-done((bf16[4,512,128]{2,1,0:T(8,128)(2,1)S(1)}, bf16[4,512,128]{2,1,0:T(8,128)(2,1)S(1)}, u32[]{:S(2)}, u32[]{:S(2)}) %collective-permute-start.29) | collective-permute-done | bytes 524320 | tf_op jit(solution)/shard_map/ppermute | solution.py:70
  100.2 4.2 %shard_map.82 = (f32[512,512]{1,0:T(8,128)S(1)}, bf16[4096,512]{1,0:T(8,128)(2,1)}) custom-call(s32[2]{0:T(128)S(1)} %pad_add_fusion.me, bf16[8,512,128]{2,1,0:T(8,128)(2,1)S(1)} %constant_dynamic-update-slice_fusion.7.a_ref, bf16[8,512,128]{2,1,0:T(8,128)(2,1)S(1)} %constant_dynamic-update-slice_fusion.18.b_ref, bf16[4096,512]{1,0:T(8,128)(2,1)S(1)} %copy-done, ...), custom_call_target="tpu_custom_call" | custom-call | flops 134217728 | bytes 262144 | tf_op jit(solution)/shard_map/pallas_call | solution.py:208
  104.7 2.3 %collective-permute-done.28 = bf16[4,512,128]{2,1,0:T(8,128)(2,1)S(1)} collective-permute-done((bf16[4,512,128]{2,1,0:T(8,128)(2,1)S(1)}, bf16[4,512,128]{2,1,0:T(8,128)(2,1)S(1)}, u32[]{:S(2)}, u32[]{:S(2)}) %collective-permute-start.28) | collective-permute-done | bytes 524320 | tf_op jit(solution)/shard_map/ppermute | solution.py:70
  108.2 4.3 %shard_map.81 = (f32[512,512]{1,0:T(8,128)S(1)}, bf16[512,4096]{1,0:T(8,128)(2,1)}) custom-call(s32[2]{0:T(128)S(1)} %pad_add_fusion.me, bf16[8,512,128]{2,1,0:T(8,128)(2,1)S(1)} %constant_dynamic-update-slice_fusion.16.a_ref, bf16[8,512,128]{2,1,0:T(8,128)(2,1)S(1)} %constant_dynamic-update-slice_fusion.23.b_ref, bf16[512,4096]{1,0:T(8,128)(2,1)S(1)} %copy-done.1, ...), custom_call_target="tpu_custom_call" | custom-call | flops 134217728 | bytes 262144 | tf_op jit(solution)/shard_map/pallas_call | solution.py:208
  112.5 3.4 %collective-permute-done.14.a_ref = bf16[8,512,128]{2,1,0:T(8,128)(2,1)S(1)} collective-permute-done((bf16[8,512,128]{2,1,0:T(8,128)(2,1)S(1)}, bf16[8,512,128]{2,1,0:T(8,128)(2,1)S(1)}, u32[]{:S(2)}, u32[]{:S(2)}) %collective-permute-start.14) | collective-permute-done | bytes 1048608 | tf_op jit(solution)/shard_map/ppermute | solution.py:70
  115.9 2.3 %collective-permute-done.31.b_ref = bf16[8,512,128]{2,1,0:T(8,128)(2,1)S(1)} collective-permute-done((bf16[8,512,128]{2,1,0:T(8,128)(2,1)S(1)}, bf16[8,512,128]{2,1,0:T(8,128)(2,1)S(1)}, u32[]{:S(2)}, u32[]{:S(2)}) %collective-permute-start.31) | collective-permute-done | bytes 1048608 | tf_op jit(solution)/shard_map/ppermute | solution.py:70
  118.2 4.2 %shard_map.83 = (f32[512,512]{1,0:T(8,128)S(1)}, bf16[4096,512]{1,0:T(8,128)(2,1)}) custom-call(s32[2]{0:T(128)S(1)} %pad_add_fusion.me, bf16[8,512,128]{2,1,0:T(8,128)(2,1)S(1)} %collective-permute-done.14.a_ref, bf16[8,512,128]{2,1,0:T(8,128)(2,1)S(1)} %collective-permute-done.31.b_ref, ...), custom_call_target="tpu_custom_call", output_to_operand_aliasing={{0}: (5, {}), {1}: (6, {})} | custom-call | flops 134217728 | bytes 262144 | tf_op jit(solution)/shard_map/pallas_call | solution.py:208
  122.4 4.7 %collective-permute-done.32.a_ref = bf16[8,512,128]{2,1,0:T(8,128)(2,1)S(1)} collective-permute-done((bf16[8,512,128]{2,1,0:T(8,128)(2,1)S(1)}, bf16[8,512,128]{2,1,0:T(8,128)(2,1)S(1)}, u32[]{:S(2)}, u32[]{:S(2)}) %collective-permute-start.32) | collective-permute-done | bytes 1048608 | tf_op jit(solution)/shard_map/ppermute | solution.py:70
  127.1 2.3 %collective-permute-done.33.b_ref = bf16[8,512,128]{2,1,0:T(8,128)(2,1)S(1)} collective-permute-done((bf16[8,512,128]{2,1,0:T(8,128)(2,1)S(1)}, bf16[8,512,128]{2,1,0:T(8,128)(2,1)S(1)}, u32[]{:S(2)}, u32[]{:S(2)}) %collective-permute-start.33) | collective-permute-done | bytes 1048608 | tf_op jit(solution)/shard_map/ppermute | solution.py:70
  129.5 2.3 %shard_map.84 = f32[512,512]{1,0:T(8,128)S(1)} custom-call(s32[2]{0:T(128)S(1)} %pad_add_fusion.me, bf16[8,512,128]{2,1,0:T(8,128)(2,1)S(1)} %collective-permute-done.32.a_ref, bf16[8,512,128]{2,1,0:T(8,128)(2,1)S(1)} %collective-permute-done.33.b_ref, bf16[512,4096]{1,0:T(8,128)(2,1)S(1)} %copy-done.2, ...), custom_call_target="tpu_custom_call", output_to_operand_aliasing={{}: (4, {})} | custom-call | flops 134217728 | bytes 262144 | tf_op jit(solution)/shard_map/pallas_call | solution.py:208
  134.6 2.2 %collective-permute-start.37 = (bf16[2,64,512]{2,1,0:T(8,128)(2,1)S(1)}, bf16[2,64,512]{2,1,0:T(8,128)(2,1)S(1)}, u32[]{:S(2)}, u32[]{:S(2)}) collective-permute-start(bf16[2,64,512]{2,1,0:T(8,128)(2,1)S(1)} %pad_maximum_fusion.16), channel_id=1, source_target_pairs={{0,64},{1,65},{2,66},{3,67},{4,68},{5,69},{6,70},{7,71},{8,72},{9,... | collective-permute-start | bytes 393224 | tf_op jit(solution)/shard_map/ppermute | solution.py:70
  138.7 3.0 %shard_map.85 = bf16[512,4096]{1,0:T(8,128)(2,1)} custom-call(s32[2]{0:T(128)S(1)} %pad_add_fusion.me, bf16[8,512,128]{2,1,0:T(8,128)(2,1)S(1)} %collective-permute-done.32.a_ref, bf16[8,512,128]{2,1,0:T(8,128)(2,1)S(1)} %collective-permute-done.33.b_ref, ...), custom_call_target="tpu_custom_call", output_to_operand_aliasing={{}: (4, {})} | custom-call | flops 134217728 | bytes 262144 | tf_op jit(solution)/shard_map/pallas_call | solution.py:208
  141.7 3.2 %collective-permute-done.35 = bf16[2,64,512]{2,1,0:T(8,128)(2,1)S(1)} collective-permute-done((bf16[2,64,512]{2,1,0:T(8,128)(2,1)S(1)}, bf16[2,64,512]{2,1,0:T(8,128)(2,1)S(1)}, u32[]{:S(2)}, u32[]{:S(2)}) %collective-permute-start.35) | collective-permute-done | bytes 131104 | tf_op jit(solution)/shard_map/ppermute | solution.py:70
  (125 shorter events, 41.8 us)
Async XLA Ops:
  0.6 6.5 %collective-permute-start = (bf16[64,512]{1,0:T(8,128)(2,1)}, bf16[64,512]{1,0:T(8,128)(2,1)S(1)}, u32[]{:S(2)}, u32[]{:S(2)}) collective-permute-start(bf16[64,512]{1,0:T(8,128)(2,1)} %param.4), channel_id=1, source_target_pairs={{0,32},{1,33},{2,34},{3,35},{4,36},{5,37},{6,38},{7,39},{8,40},{9,... | collective-permute-start | bytes 196616 | tf_op jit(solution)/shard_map/ppermute | solution.py:70
  5.3 9.4 %collective-permute-start.15 = (bf16[64,512]{1,0:T(8,128)(2,1)}, bf16[64,512]{1,0:T(8,128)(2,1)S(1)}, u32[]{:S(2)}, u32[]{:S(2)}) collective-permute-start(bf16[64,512]{1,0:T(8,128)(2,1)} %param.7), channel_id=1, source_target_pairs={{0,32},{1,33},{2,34},{3,35},{4,36},{5,37},{6,38},{7,39},{8,40},{9,... | collective-permute-start | bytes 196616 | tf_op jit(solution)/shard_map/ppermute | solution.py:70
  15.6 6.7 %collective-permute-start.16 = (bf16[128,512]{1,0:T(8,128)(2,1)S(1)}, bf16[128,512]{1,0:T(8,128)(2,1)S(1)}, u32[]{:S(2)}, u32[]{:S(2)}) collective-permute-start(bf16[128,512]{1,0:T(8,128)(2,1)S(1)} %pad_maximum_fusion.13), channel_id=1, source_target_pairs={{0,96},{1,97},{2,98},{3,99},{4,100},{5,101},{6,102},{7,103},{8,104... | collective-permute-start | bytes 393224 | tf_op jit(solution)/shard_map/ppermute | solution.py:70
  19.4 18.9 %collective-permute-start.5 = (bf16[8,512,128]{2,1,0:T(8,128)(2,1)S(1)}, bf16[8,512,128]{2,1,0:T(8,128)(2,1)S(1)}, u32[]{:S(2)}, u32[]{:S(2)}) collective-permute-start(bf16[8,512,128]{2,1,0:T(8,128)(2,1)S(1)} %shard_map.77), channel_id=1, source_target_pairs={{0,3},{1,2},{2,1},{3,0},{4,7},{5,6},{6,5},{7,4},{8,11},{9,10},{10,... | collective-permute-start | bytes 3145736 | tf_op jit(solution)/shard_map/ppermute | solution.py:70
  26.9 14.0 %collective-permute-start.3 = (bf16[8,512,128]{2,1,0:T(8,128)(2,1)S(1)}, bf16[8,512,128]{2,1,0:T(8,128)(2,1)S(1)}, u32[]{:S(2)}, u32[]{:S(2)}) collective-permute-start(bf16[8,512,128]{2,1,0:T(8,128)(2,1)S(1)} %shard_map.76), channel_id=1, source_target_pairs={{0,1},{1,0},{2,3},{3,2},{4,5},{5,4},{6,7},{7,6},{8,9},{9,8},{10,11... | collective-permute-start | bytes 3145736 | tf_op jit(solution)/shard_map/ppermute | solution.py:70
  29.7 16.3 %collective-permute-start.20 = (bf16[8,512,128]{2,1,0:T(8,128)(2,1)S(1)}, bf16[8,512,128]{2,1,0:T(8,128)(2,1)S(1)}, u32[]{:S(2)}, u32[]{:S(2)}) collective-permute-start(bf16[8,512,128]{2,1,0:T(8,128)(2,1)S(1)} %shard_map.80), channel_id=1, source_target_pairs={{0,3},{1,2},{2,1},{3,0},{4,7},{5,6},{6,5},{7,4},{8,11},{9,10},{10,... | collective-permute-start | bytes 3145736 | tf_op jit(solution)/shard_map/ppermute | solution.py:70
  33.0 19.1 %collective-permute-start.18 = (bf16[8,512,128]{2,1,0:T(8,128)(2,1)S(1)}, bf16[8,512,128]{2,1,0:T(8,128)(2,1)S(1)}, u32[]{:S(2)}, u32[]{:S(2)}) collective-permute-start(bf16[8,512,128]{2,1,0:T(8,128)(2,1)S(1)} %shard_map.79), channel_id=1, source_target_pairs={{0,1},{1,0},{2,3},{3,2},{4,5},{5,4},{6,7},{7,6},{8,9},{9,8},{10,11... | collective-permute-start | bytes 3145736 | tf_op jit(solution)/shard_map/ppermute | solution.py:70
  38.5 19.2 %collective-permute-start.6 = (bf16[4,512,128]{2,1,0:T(8,128)(2,1)S(1)}, bf16[4,512,128]{2,1,0:T(8,128)(2,1)S(1)}, u32[]{:S(2)}, u32[]{:S(2)}) collective-permute-start(bf16[4,512,128]{2,1,0:T(8,128)(2,1)S(1)} %add_convert_fusion.2), channel_id=1, source_target_pairs={{0,1},{1,0},{2,3},{3,2},{4,5},{5,4},{6,7},{7,6},{8,9},{9,8},{10,11... | collective-permute-start | bytes 1572872 | tf_op jit(solution)/shard_map/ppermute | solution.py:70
  41.1 17.0 %collective-permute-start.4 = (bf16[4,512,128]{2,1,0:T(8,128)(2,1)S(1)}, bf16[4,512,128]{2,1,0:T(8,128)(2,1)S(1)}, u32[]{:S(2)}, u32[]{:S(2)}) collective-permute-start(bf16[4,512,128]{2,1,0:T(8,128)(2,1)S(1)} %add_convert_fusion.3), channel_id=1, source_target_pairs={{0,3},{1,2},{2,1},{3,0},{4,7},{5,6},{6,5},{7,4},{8,11},{9,10},{10,... | collective-permute-start | bytes 1572872 | tf_op jit(solution)/shard_map/ppermute | solution.py:70
  46.1 17.3 %collective-permute-start.21 = (bf16[4,512,128]{2,1,0:T(8,128)(2,1)S(1)}, bf16[4,512,128]{2,1,0:T(8,128)(2,1)S(1)}, u32[]{:S(2)}, u32[]{:S(2)}) collective-permute-start(bf16[4,512,128]{2,1,0:T(8,128)(2,1)S(1)} %add_convert_fusion), channel_id=1, source_target_pairs={{0,1},{1,0},{2,3},{3,2},{4,5},{5,4},{6,7},{7,6},{8,9},{9,8},{10,11... | collective-permute-start | bytes 1572872 | tf_op jit(solution)/shard_map/ppermute | solution.py:70
  52.3 11.3 %collective-permute-start.19 = (bf16[4,512,128]{2,1,0:T(8,128)(2,1)S(1)}, bf16[4,512,128]{2,1,0:T(8,128)(2,1)S(1)}, u32[]{:S(2)}, u32[]{:S(2)}) collective-permute-start(bf16[4,512,128]{2,1,0:T(8,128)(2,1)S(1)} %add_convert_fusion.1), channel_id=1, source_target_pairs={{0,3},{1,2},{2,1},{3,0},{4,7},{5,6},{6,5},{7,4},{8,11},{9,10},{10,... | collective-permute-start | bytes 1572872 | tf_op jit(solution)/shard_map/ppermute | solution.py:70
  58.4 10.5 %collective-permute-start.8 = (bf16[2,512,128]{2,1,0:T(8,128)(2,1)S(1)}, bf16[2,512,128]{2,1,0:T(8,128)(2,1)S(1)}, u32[]{:S(2)}, u32[]{:S(2)}) collective-permute-start(bf16[2,512,128]{2,1,0:T(8,128)(2,1)S(1)} %pad_maximum_fusion.6), channel_id=1, source_target_pairs={{0,12},{1,13},{2,14},{3,15},{4,8},{5,9},{6,10},{7,11},{8,4},{9,5},... | collective-permute-start | bytes 786440 | tf_op jit(solution)/shard_map/ppermute | solution.py:70
  58.7 10.2 %collective-permute-start.9 = (bf16[2,512,128]{2,1,0:T(8,128)(2,1)S(1)}, bf16[2,512,128]{2,1,0:T(8,128)(2,1)S(1)}, u32[]{:S(2)}, u32[]{:S(2)}) collective-permute-start(bf16[2,512,128]{2,1,0:T(8,128)(2,1)S(1)} %pad_maximum_fusion.7), channel_id=1, source_target_pairs={{0,8},{1,9},{2,10},{3,11},{4,12},{5,13},{6,14},{7,15},{8,0},{9,1},... | collective-permute-start | bytes 786440 | tf_op jit(solution)/shard_map/ppermute | solution.py:70
  60.3 9.2 %collective-permute-start.7 = (bf16[2,512,128]{2,1,0:T(8,128)(2,1)S(1)}, bf16[2,512,128]{2,1,0:T(8,128)(2,1)S(1)}, u32[]{:S(2)}, u32[]{:S(2)}) collective-permute-start(bf16[2,512,128]{2,1,0:T(8,128)(2,1)S(1)} %pad_maximum_fusion.5), channel_id=1, source_target_pairs={{0,4},{1,5},{2,6},{3,7},{4,0},{5,1},{6,2},{7,3},{8,12},{9,13},{10,... | collective-permute-start | bytes 786440 | tf_op jit(solution)/shard_map/ppermute | solution.py:70
  64.0 10.5 %collective-permute-start.23 = (bf16[2,512,128]{2,1,0:T(8,128)(2,1)S(1)}, bf16[2,512,128]{2,1,0:T(8,128)(2,1)S(1)}, u32[]{:S(2)}, u32[]{:S(2)}) collective-permute-start(bf16[2,512,128]{2,1,0:T(8,128)(2,1)S(1)} %pad_maximum_fusion.10), channel_id=1, source_target_pairs={{0,12},{1,13},{2,14},{3,15},{4,8},{5,9},{6,10},{7,11},{8,4},{9,5},... | collective-permute-start | bytes 786440 | tf_op jit(solution)/shard_map/ppermute | solution.py:70
  64.3 10.2 %collective-permute-start.24 = (bf16[2,512,128]{2,1,0:T(8,128)(2,1)S(1)}, bf16[2,512,128]{2,1,0:T(8,128)(2,1)S(1)}, u32[]{:S(2)}, u32[]{:S(2)}) collective-permute-start(bf16[2,512,128]{2,1,0:T(8,128)(2,1)S(1)} %pad_maximum_fusion.11), channel_id=1, source_target_pairs={{0,8},{1,9},{2,10},{3,11},{4,12},{5,13},{6,14},{7,15},{8,0},{9,1},... | collective-permute-start | bytes 786440 | tf_op jit(solution)/shard_map/ppermute | solution.py:70
  69.8 11.5 %collective-permute-start.12 = (bf16[2,512,128]{2,1,0:T(8,128)(2,1)S(1)}, bf16[2,512,128]{2,1,0:T(8,128)(2,1)S(1)}, u32[]{:S(2)}, u32[]{:S(2)}) collective-permute-start(bf16[2,512,128]{2,1,0:T(8,128)(2,1)S(1)} %get-tuple-element.26), channel_id=1, source_target_pairs={{0,12},{1,13},{2,14},{3,15},{4,8},{5,9},{6,10},{7,11},{8,4},{9,5},... | collective-permute-start | bytes 786440 | tf_op jit(solution)/shard_map/ppermute | solution.py:70
  70.3 10.8 %collective-permute-start.11 = (bf16[2,512,128]{2,1,0:T(8,128)(2,1)S(1)}, bf16[2,512,128]{2,1,0:T(8,128)(2,1)S(1)}, u32[]{:S(2)}, u32[]{:S(2)}) collective-permute-start(bf16[2,512,128]{2,1,0:T(8,128)(2,1)S(1)} %get-tuple-element.26), channel_id=1, source_target_pairs={{0,8},{1,9},{2,10},{3,11},{4,12},{5,13},{6,14},{7,15},{8,0},{9,1},... | collective-permute-start | bytes 786440 | tf_op jit(solution)/shard_map/ppermute | solution.py:70
  74.5 6.2 %collective-permute-start.10 = (bf16[2,512,128]{2,1,0:T(8,128)(2,1)S(1)}, bf16[2,512,128]{2,1,0:T(8,128)(2,1)S(1)}, u32[]{:S(2)}, u32[]{:S(2)}) collective-permute-start(bf16[2,512,128]{2,1,0:T(8,128)(2,1)S(1)} %get-tuple-element.26), channel_id=1, source_target_pairs={{0,4},{1,5},{2,6},{3,7},{4,0},{5,1},{6,2},{7,3},{8,12},{9,13},{10,... | collective-permute-start | bytes 786440 | tf_op jit(solution)/shard_map/ppermute | solution.py:70
  75.4 10.3 %collective-permute-start.27 = (bf16[2,512,128]{2,1,0:T(8,128)(2,1)S(1)}, bf16[2,512,128]{2,1,0:T(8,128)(2,1)S(1)}, u32[]{:S(2)}, u32[]{:S(2)}) collective-permute-start(bf16[2,512,128]{2,1,0:T(8,128)(2,1)S(1)} %fusion.11), channel_id=1, source_target_pairs={{0,12},{1,13},{2,14},{3,15},{4,8},{5,9},{6,10},{7,11},{8,4},{9,5},... | collective-permute-start | bytes 786440 | tf_op jit(solution)/shard_map/ppermute | solution.py:70
  76.0 9.8 %collective-permute-start.26 = (bf16[2,512,128]{2,1,0:T(8,128)(2,1)S(1)}, bf16[2,512,128]{2,1,0:T(8,128)(2,1)S(1)}, u32[]{:S(2)}, u32[]{:S(2)}) collective-permute-start(bf16[2,512,128]{2,1,0:T(8,128)(2,1)S(1)} %fusion.11), channel_id=1, source_target_pairs={{0,8},{1,9},{2,10},{3,11},{4,12},{5,13},{6,14},{7,15},{8,0},{9,1},... | collective-permute-start | bytes 786440 | tf_op jit(solution)/shard_map/ppermute | solution.py:70
  81.4 15.9 %collective-permute-start.13 = (bf16[4,512,128]{2,1,0:T(8,128)(2,1)S(1)}, bf16[4,512,128]{2,1,0:T(8,128)(2,1)S(1)}, u32[]{:S(2)}, u32[]{:S(2)}) collective-permute-start(bf16[4,512,128]{2,1,0:T(8,128)(2,1)S(1)} %pad_maximum_fusion), channel_id=1, source_target_pairs={{0,3},{1,2},{2,1},{3,0},{4,7},{5,6},{6,5},{7,4},{8,11},{9,10},{10,... | collective-permute-start | bytes 1572872 | tf_op jit(solution)/shard_map/ppermute | solution.py:70
  84.3 11.9 %collective-permute-start.29 = (bf16[4,512,128]{2,1,0:T(8,128)(2,1)S(1)}, bf16[4,512,128]{2,1,0:T(8,128)(2,1)S(1)}, u32[]{:S(2)}, u32[]{:S(2)}) collective-permute-start(bf16[4,512,128]{2,1,0:T(8,128)(2,1)S(1)} %pad_maximum_fusion.3), channel_id=1, source_target_pairs={{0,1},{1,0},{2,3},{3,2},{4,5},{5,4},{6,7},{7,6},{8,9},{9,8},{10,11... | collective-permute-start | bytes 1572872 | tf_op jit(solution)/shard_map/ppermute | solution.py:70
  96.3 8.4 %collective-permute-start.30 = (bf16[4,512,128]{2,1,0:T(8,128)(2,1)S(1)}, bf16[4,512,128]{2,1,0:T(8,128)(2,1)S(1)}, u32[]{:S(2)}, u32[]{:S(2)}) collective-permute-start(bf16[4,512,128]{2,1,0:T(8,128)(2,1)S(1)} %pad_maximum_fusion.2), channel_id=1, source_target_pairs={{0,1},{1,0},{2,3},{3,2},{4,5},{5,4},{6,7},{7,6},{8,9},{9,8},{10,11... | collective-permute-start | bytes 1572872 | tf_op jit(solution)/shard_map/ppermute | solution.py:70
  97.4 9.6 %collective-permute-start.28 = (bf16[4,512,128]{2,1,0:T(8,128)(2,1)S(1)}, bf16[4,512,128]{2,1,0:T(8,128)(2,1)S(1)}, u32[]{:S(2)}, u32[]{:S(2)}) collective-permute-start(bf16[4,512,128]{2,1,0:T(8,128)(2,1)S(1)} %pad_maximum_fusion.1), channel_id=1, source_target_pairs={{0,3},{1,2},{2,1},{3,0},{4,7},{5,6},{6,5},{7,4},{8,11},{9,10},{10,... | collective-permute-start | bytes 1572872 | tf_op jit(solution)/shard_map/ppermute | solution.py:70
  98.3 19.9 %collective-permute-start.31 = (bf16[8,512,128]{2,1,0:T(8,128)(2,1)S(1)}, bf16[8,512,128]{2,1,0:T(8,128)(2,1)S(1)}, u32[]{:S(2)}, u32[]{:S(2)}) collective-permute-start(bf16[8,512,128]{2,1,0:T(8,128)(2,1)S(1)} %constant_dynamic-update-slice_fusion.18.b_ref), channel_id=1, source_target_pairs={{0,3},{1,2},{2,1},{3,0},{4,7},{5,6},{6,5},{7,4},{8,11},{9,10},{10,... | collective-permute-start | bytes 3145736 | tf_op jit(solution)/shard_map/ppermute | solution.py:70
  100.1 15.8 %collective-permute-start.14 = (bf16[8,512,128]{2,1,0:T(8,128)(2,1)S(1)}, bf16[8,512,128]{2,1,0:T(8,128)(2,1)S(1)}, u32[]{:S(2)}, u32[]{:S(2)}) collective-permute-start(bf16[8,512,128]{2,1,0:T(8,128)(2,1)S(1)} %constant_dynamic-update-slice_fusion.7.a_ref), channel_id=1, source_target_pairs={{0,1},{1,0},{2,3},{3,2},{4,5},{5,4},{6,7},{7,6},{8,9},{9,8},{10,11... | collective-permute-start | bytes 3145736 | tf_op jit(solution)/shard_map/ppermute | solution.py:70
  107.1 20.1 %collective-permute-start.32 = (bf16[8,512,128]{2,1,0:T(8,128)(2,1)S(1)}, bf16[8,512,128]{2,1,0:T(8,128)(2,1)S(1)}, u32[]{:S(2)}, u32[]{:S(2)}) collective-permute-start(bf16[8,512,128]{2,1,0:T(8,128)(2,1)S(1)} %constant_dynamic-update-slice_fusion.16.a_ref), channel_id=1, source_target_pairs={{0,1},{1,0},{2,3},{3,2},{4,5},{5,4},{6,7},{7,6},{8,9},{9,8},{10,11... | collective-permute-start | bytes 3145736 | tf_op jit(solution)/shard_map/ppermute | solution.py:70
  107.2 22.3 %collective-permute-start.33 = (bf16[8,512,128]{2,1,0:T(8,128)(2,1)S(1)}, bf16[8,512,128]{2,1,0:T(8,128)(2,1)S(1)}, u32[]{:S(2)}, u32[]{:S(2)}) collective-permute-start(bf16[8,512,128]{2,1,0:T(8,128)(2,1)S(1)} %constant_dynamic-update-slice_fusion.23.b_ref), channel_id=1, source_target_pairs={{0,3},{1,2},{2,1},{3,0},{4,7},{5,6},{6,5},{7,4},{8,11},{9,10},{10,... | collective-permute-start | bytes 3145736 | tf_op jit(solution)/shard_map/ppermute | solution.py:70
  134.5 7.2 %collective-permute-start.36 = (bf16[2,64,512]{2,1,0:T(8,128)(2,1)S(1)}, bf16[2,64,512]{2,1,0:T(8,128)(2,1)S(1)}, u32[]{:S(2)}, u32[]{:S(2)}) collective-permute-start(bf16[2,64,512]{2,1,0:T(8,128)(2,1)S(1)} %pad_maximum_fusion.15), channel_id=1, source_target_pairs={{0,96},{1,97},{2,98},{3,99},{4,100},{5,101},{6,102},{7,103},{8,104... | collective-permute-start | bytes 393224 | tf_op jit(solution)/shard_map/ppermute | solution.py:70
  134.6 7.1 %collective-permute-start.37 = (bf16[2,64,512]{2,1,0:T(8,128)(2,1)S(1)}, bf16[2,64,512]{2,1,0:T(8,128)(2,1)S(1)}, u32[]{:S(2)}, u32[]{:S(2)}) collective-permute-start(bf16[2,64,512]{2,1,0:T(8,128)(2,1)S(1)} %pad_maximum_fusion.16), channel_id=1, source_target_pairs={{0,64},{1,65},{2,66},{3,67},{4,68},{5,69},{6,70},{7,71},{8,72},{9,... | collective-permute-start | bytes 393224 | tf_op jit(solution)/shard_map/ppermute | solution.py:70
  136.8 8.0 %collective-permute-start.35 = (bf16[2,64,512]{2,1,0:T(8,128)(2,1)S(1)}, bf16[2,64,512]{2,1,0:T(8,128)(2,1)S(1)}, u32[]{:S(2)}, u32[]{:S(2)}) collective-permute-start(bf16[2,64,512]{2,1,0:T(8,128)(2,1)S(1)} %pad_maximum_fusion.14), channel_id=1, source_target_pairs={{0,32},{1,33},{2,34},{3,35},{4,36},{5,37},{6,38},{7,39},{8,40},{9,... | collective-permute-start | bytes 393224 | tf_op jit(solution)/shard_map/ppermute | solution.py:70
  (10 other events, 71.8 us)

commit v4 on v3

--- a/solution.py
+++ b/solution.py
@@ -330,7 +330,7 @@
     p_near = spread_second(p_four)
     d_four = spread_first(d_pre)
     p_far = spread_third(p_near)
-    d_near = spread_second([after(d_four[h], p_near[h]) for h in range(2)])
+    d_near = spread_second(d_four)
     total, grad = consume(p_near[0], p_near[1], w_out, cotangent, me, True, 0)
     d_far = spread_third([after(d_near[h], total) for h in range(2)])
     d_total, d_grad = consume(d_near[0], d_near[1], w_in, inputs, me, False, 0)

time: 146 us -> 145 us (level)
  waiting for transfers between devices: 57.9 us -> 49.5 us
  starting transfers between devices: 48.8 us -> 54.8 us
    ppermute x38, waiting for transfers between devices: 57.9 us -> 49.5 us  [send(): return lax.ppermute(block, BOTH, perm)]
    ppermute x38, starting transfers between devices: 48.8 us -> 54.8 us  [send(): return lax.ppermute(block, BOTH, perm)]
    unnamed x15 -> x13, local copies, waits for them, and re-layouts: 3.15 us -> 3.08 us
  transfers between devices with their start and end apart: 38 -> 38, of which waited for: 24 -> 20; matrix products, arithmetic and copies ran while one was open for 4% -> 5% of each run, Pallas kernels for 18% -> 18%
where the time goes in v4:
time: 145 us; the launch traced here: 143 us
  starting transfers between devices  54.8 us (38%)
  waiting for transfers between devices  49.5 us (34%)
  Pallas kernels  28.2 us (19%)
  other arithmetic  5.38 us (4%)
  local copies, waits for them, and re-layouts  4.36 us (3%)
    ppermute x38, starting transfers between devices, send(): return lax.ppermute(block, BOTH, perm)  54.8 us
    ppermute x38, waiting for transfers between devices, send(): return lax.ppermute(block, BOTH, perm)  49.5 us
    pallas_call x5, Pallas kernels, consume(): pl.pallas_call(functools.partial(consume_body, transposed, total is not N...  18 us
    pallas_call x6, Pallas kernels, produce(): pl.pallas_call(functools.partial(produce_body, transposed, parts), out_sh...  10.2 us
    unnamed x13, local copies, waits for them, and re-layouts  3.08 us
  transfers between devices with their start and end apart: 38, of which 20 were waited for; matrix products, arithmetic and copies ran while one was open for 5% of the time, Pallas kernels for 18%

profile of v4, /device:TPU:1, one launch (start us, length us, event | category | flops | bytes accessed | tf_op | source)
XLA Modules:
  0.0 143.3 jit_solution(10017227406310805729)
XLA Ops:
  0.6 4.7 %collective-permute-start = (bf16[64,512]{1,0:T(8,128)(2,1)}, bf16[64,512]{1,0:T(8,128)(2,1)S(1)}, u32[]{:S(2)}, u32[]{:S(2)}) collective-permute-start(bf16[64,512]{1,0:T(8,128)(2,1)} %param.4), channel_id=1, source_target_pairs={{0,32},{1,33},{2,34},{3,35},{4,36},{5,37},{6,38},{7,39},{8,40},{9,... | collective-permute-start | bytes 196616 | tf_op jit(solution)/shard_map/ppermute | solution.py:70
  9.0 2.9 %collective-permute-done.1 = bf16[128,512]{1,0:T(8,128)(2,1)S(1)} collective-permute-done((bf16[128,512]{1,0:T(8,128)(2,1)S(1)}, bf16[128,512]{1,0:T(8,128)(2,1)S(1)}, u32[]{:S(2)}, u32[]{:S(2)}) %collective-permute-start.1) | collective-permute-done | bytes 131104 | tf_op jit(solution)/shard_map/ppermute | solution.py:70
  12.0 2.8 %collective-permute-start.2 = (bf16[256,512]{1,0:T(8,128)(2,1)S(1)}, bf16[256,512]{1,0:T(8,128)(2,1)S(1)}, u32[]{:S(2)}, u32[]{:S(2)}) collective-permute-start(bf16[256,512]{1,0:T(8,128)(2,1)S(1)} %get-tuple-element.108), channel_id=1, source_target_pairs={{0,16},{1,17},{2,18},{3,19},{4,20},{5,21},{6,22},{7,23},{8,24},{9,... | collective-permute-start | bytes 786440 | tf_op jit(solution)/shard_map/ppermute | solution.py:70
  15.9 2.2 %copy-done.1 = bf16[512,4096]{1,0:T(8,128)(2,1)S(1)} copy-done((bf16[512,4096]{1,0:T(8,128)(2,1)S(1)}, bf16[512,4096]{1,0:T(8,128)(2,1)}, u32[]{:S(2)}) %copy-start.1) | copy-done | bytes 4194328
  19.4 2.8 %collective-permute-start.5 = (bf16[8,512,128]{2,1,0:T(8,128)(2,1)S(1)}, bf16[8,512,128]{2,1,0:T(8,128)(2,1)S(1)}, u32[]{:S(2)}, u32[]{:S(2)}) collective-permute-start(bf16[8,512,128]{2,1,0:T(8,128)(2,1)S(1)} %shard_map.77), channel_id=1, source_target_pairs={{0,3},{1,2},{2,1},{3,0},{4,7},{5,6},{6,5},{7,4},{8,11},{9,10},{10,... | collective-permute-start | bytes 3145736 | tf_op jit(solution)/shard_map/ppermute | solution.py:70
  22.3 3.3 %collective-permute-start.17 = (bf16[256,512]{1,0:T(8,128)(2,1)S(1)}, bf16[256,512]{1,0:T(8,128)(2,1)S(1)}, u32[]{:S(2)}, u32[]{:S(2)}) collective-permute-start(bf16[256,512]{1,0:T(8,128)(2,1)S(1)} %pad_maximum_fusion.8), channel_id=1, source_target_pairs={{0,16},{1,17},{2,18},{3,19},{4,20},{5,21},{6,22},{7,23},{8,24},{9,... | collective-permute-start | bytes 786440 | tf_op jit(solution)/shard_map/ppermute | solution.py:70
  29.7 2.0 %collective-permute-start.20 = (bf16[8,512,128]{2,1,0:T(8,128)(2,1)S(1)}, bf16[8,512,128]{2,1,0:T(8,128)(2,1)S(1)}, u32[]{:S(2)}, u32[]{:S(2)}) collective-permute-start(bf16[8,512,128]{2,1,0:T(8,128)(2,1)S(1)} %shard_map.80), channel_id=1, source_target_pairs={{0,3},{1,2},{2,1},{3,0},{4,7},{5,6},{6,5},{7,4},{8,11},{9,10},{10,... | collective-permute-start | bytes 3145736 | tf_op jit(solution)/shard_map/ppermute | solution.py:70
  33.5 2.5 %shard_map.75 = (bf16[8,512,128]{2,1,0:T(8,128)(2,1)S(1)}, bf16[8,512,128]{2,1,0:T(8,128)(2,1)S(1)}) custom-call(s32[2]{0:T(128)S(1)} %pad_add_fusion.me, bf16[512,512]{1,0:T(8,128)(2,1)S(1)} %constant_dynamic-update-slice_fusion.3.x_ref.rest_1_.rest_0_, bf16[512,4096]{1,0:T(8,128)(2,1)S(1)} %copy-done.1), custom_call_target="tpu_custom_call" | custom-call | flops 67108864 | bytes 262144 | tf_op jit(solution)/shard_map/pallas_call | solution.py:127
  36.0 2.4 %shard_map.78 = (bf16[8,512,128]{2,1,0:T(8,128)(2,1)S(1)}, bf16[8,512,128]{2,1,0:T(8,128)(2,1)S(1)}) custom-call(s32[2]{0:T(128)S(1)} %pad_add_fusion.me, bf16[512,512]{1,0:T(8,128)(2,1)S(1)} %constant_dynamic-update-slice_fusion.12.x_ref.rest_1_, bf16[4096,512]{1,0:T(8,128)(2,1)S(1)} %copy-done), custom_call_target="tpu_custom_call" | custom-call | flops 67108864 | bytes 262144 | tf_op jit(solution)/shard_map/pallas_call | solution.py:127
  41.1 2.8 %collective-permute-start.4 = (bf16[4,512,128]{2,1,0:T(8,128)(2,1)S(1)}, bf16[4,512,128]{2,1,0:T(8,128)(2,1)S(1)}, u32[]{:S(2)}, u32[]{:S(2)}) collective-permute-start(bf16[4,512,128]{2,1,0:T(8,128)(2,1)S(1)} %add_convert_fusion.3), channel_id=1, source_target_pairs={{0,3},{1,2},{2,1},{3,0},{4,7},{5,6},{6,5},{7,4},{8,11},{9,10},{10,... | collective-permute-start | bytes 1572872 | tf_op jit(solution)/shard_map/ppermute | solution.py:70
  43.9 2.1 %collective-permute-done.20 = bf16[8,512,128]{2,1,0:T(8,128)(2,1)S(1)} collective-permute-done((bf16[8,512,128]{2,1,0:T(8,128)(2,1)S(1)}, bf16[8,512,128]{2,1,0:T(8,128)(2,1)S(1)}, u32[]{:S(2)}, u32[]{:S(2)}) %collective-permute-start.20) | collective-permute-done | bytes 1048608 | tf_op jit(solution)/shard_map/ppermute | solution.py:70
  46.2 5.9 %collective-permute-done.18 = bf16[8,512,128]{2,1,0:T(8,128)(2,1)S(1)} collective-permute-done((bf16[8,512,128]{2,1,0:T(8,128)(2,1)S(1)}, bf16[8,512,128]{2,1,0:T(8,128)(2,1)S(1)}, u32[]{:S(2)}, u32[]{:S(2)}) %collective-permute-start.18) | collective-permute-done | bytes 1048608 | tf_op jit(solution)/shard_map/ppermute | solution.py:70
  52.3 2.8 %collective-permute-start.19 = (bf16[4,512,128]{2,1,0:T(8,128)(2,1)S(1)}, bf16[4,512,128]{2,1,0:T(8,128)(2,1)S(1)}, u32[]{:S(2)}, u32[]{:S(2)}) collective-permute-start(bf16[4,512,128]{2,1,0:T(8,128)(2,1)S(1)} %add_convert_fusion.1), channel_id=1, source_target_pairs={{0,3},{1,2},{2,1},{3,0},{4,7},{5,6},{6,5},{7,4},{8,11},{9,10},{10,... | collective-permute-start | bytes 1572872 | tf_op jit(solution)/shard_map/ppermute | solution.py:70
  55.1 2.7 %collective-permute-done.6 = bf16[4,512,128]{2,1,0:T(8,128)(2,1)S(1)} collective-permute-done((bf16[4,512,128]{2,1,0:T(8,128)(2,1)S(1)}, bf16[4,512,128]{2,1,0:T(8,128)(2,1)S(1)}, u32[]{:S(2)}, u32[]{:S(2)}) %collective-permute-start.6) | collective-permute-done | bytes 524320 | tf_op jit(solution)/shard_map/ppermute | solution.py:70
  65.9 2.9 %collective-permute-done.8 = bf16[2,512,128]{2,1,0:T(8,128)(2,1)S(1)} collective-permute-done((bf16[2,512,128]{2,1,0:T(8,128)(2,1)S(1)}, bf16[2,512,128]{2,1,0:T(8,128)(2,1)S(1)}, u32[]{:S(2)}, u32[]{:S(2)}) %collective-permute-start.8) | collective-permute-done | bytes 262176 | tf_op jit(solution)/shard_map/ppermute | solution.py:70
  70.3 2.4 %collective-permute-start.11 = (bf16[2,512,128]{2,1,0:T(8,128)(2,1)S(1)}, bf16[2,512,128]{2,1,0:T(8,128)(2,1)S(1)}, u32[]{:S(2)}, u32[]{:S(2)}) collective-permute-start(bf16[2,512,128]{2,1,0:T(8,128)(2,1)S(1)} %get-tuple-element.24), channel_id=1, source_target_pairs={{0,8},{1,9},{2,10},{3,11},{4,12},{5,13},{6,14},{7,15},{8,0},{9,1},... | collective-permute-start | bytes 786440 | tf_op jit(solution)/shard_map/ppermute | solution.py:70
  75.9 2.3 %collective-permute-start.26 = (bf16[2,512,128]{2,1,0:T(8,128)(2,1)S(1)}, bf16[2,512,128]{2,1,0:T(8,128)(2,1)S(1)}, u32[]{:S(2)}, u32[]{:S(2)}) collective-permute-start(bf16[2,512,128]{2,1,0:T(8,128)(2,1)S(1)} %fusion.11), channel_id=1, source_target_pairs={{0,8},{1,9},{2,10},{3,11},{4,12},{5,13},{6,14},{7,15},{8,0},{9,1},... | collective-permute-start | bytes 786440 | tf_op jit(solution)/shard_map/ppermute | solution.py:70
  78.3 2.4 %collective-permute-done.10 = bf16[2,512,128]{2,1,0:T(8,128)(2,1)S(1)} collective-permute-done((bf16[2,512,128]{2,1,0:T(8,128)(2,1)S(1)}, bf16[2,512,128]{2,1,0:T(8,128)(2,1)S(1)}, u32[]{:S(2)}, u32[]{:S(2)}) %collective-permute-start.10) | collective-permute-done | bytes 262176 | tf_op jit(solution)/shard_map/ppermute | solution.py:70
  81.4 2.8 %collective-permute-start.13 = (bf16[4,512,128]{2,1,0:T(8,128)(2,1)S(1)}, bf16[4,512,128]{2,1,0:T(8,128)(2,1)S(1)}, u32[]{:S(2)}, u32[]{:S(2)}) collective-permute-start(bf16[4,512,128]{2,1,0:T(8,128)(2,1)S(1)} %pad_maximum_fusion), channel_id=1, source_target_pairs={{0,3},{1,2},{2,1},{3,0},{4,7},{5,6},{6,5},{7,4},{8,11},{9,10},{10,... | collective-permute-start | bytes 1572872 | tf_op jit(solution)/shard_map/ppermute | solution.py:70
  84.4 1.9 %collective-permute-done.25 = bf16[2,512,128]{2,1,0:T(8,128)(2,1)S(1)} collective-permute-done((bf16[2,512,128]{2,1,0:T(8,128)(2,1)S(1)}, bf16[2,512,128]{2,1,0:T(8,128)(2,1)S(1)}, u32[]{:S(2)}, u32[]{:S(2)}) %collective-permute-start.25) | collective-permute-done | bytes 262176 | tf_op jit(solution)/shard_map/ppermute | solution.py:70
  88.2 2.0 %collective-permute-start.28 = (bf16[4,512,128]{2,1,0:T(8,128)(2,1)S(1)}, bf16[4,512,128]{2,1,0:T(8,128)(2,1)S(1)}, u32[]{:S(2)}, u32[]{:S(2)}) collective-permute-start(bf16[4,512,128]{2,1,0:T(8,128)(2,1)S(1)} %pad_maximum_fusion.1), channel_id=1, source_target_pairs={{0,3},{1,2},{2,1},{3,0},{4,7},{5,6},{6,5},{7,4},{8,11},{9,10},{10,... | collective-permute-start | bytes 1572872 | tf_op jit(solution)/shard_map/ppermute | solution.py:70
  90.1 6.0 %collective-permute-done.30 = bf16[4,512,128]{2,1,0:T(8,128)(2,1)S(1)} collective-permute-done((bf16[4,512,128]{2,1,0:T(8,128)(2,1)S(1)}, bf16[4,512,128]{2,1,0:T(8,128)(2,1)S(1)}, u32[]{:S(2)}, u32[]{:S(2)}) %collective-permute-start.30) | collective-permute-done | bytes 524320 | tf_op jit(solution)/shard_map/ppermute | solution.py:70
  98.3 4.2 %shard_map.82 = (f32[512,512]{1,0:T(8,128)S(1)}, bf16[4096,512]{1,0:T(8,128)(2,1)}) custom-call(s32[2]{0:T(128)S(1)} %pad_add_fusion.me, bf16[8,512,128]{2,1,0:T(8,128)(2,1)S(1)} %constant_dynamic-update-slice_fusion.7.a_ref, bf16[8,512,128]{2,1,0:T(8,128)(2,1)S(1)} %constant_dynamic-update-slice_fusion.26.b_ref, bf16[4096,512]{1,0:T(8,128)(2,1)S(1)} %copy-done, ...), custom_call_target="tpu_custom_call" | custom-call | flops 134217728 | bytes 262144 | tf_op jit(solution)/shard_map/pallas_call | solution.py:208
  105.0 4.3 %shard_map.81 = (f32[512,512]{1,0:T(8,128)S(1)}, bf16[512,4096]{1,0:T(8,128)(2,1)}) custom-call(s32[2]{0:T(128)S(1)} %pad_add_fusion.me, bf16[8,512,128]{2,1,0:T(8,128)(2,1)S(1)} %constant_dynamic-update-slice_fusion.16.a_ref, bf16[8,512,128]{2,1,0:T(8,128)(2,1)S(1)} %constant_dynamic-update-slice_fusion.21.b_ref, bf16[512,4096]{1,0:T(8,128)(2,1)S(1)} %copy-done.1, ...), custom_call_target="tpu_custom_call" | custom-call | flops 134217728 | bytes 262144 | tf_op jit(solution)/shard_map/pallas_call | solution.py:208
  109.3 3.7 %collective-permute-done.14.a_ref = bf16[8,512,128]{2,1,0:T(8,128)(2,1)S(1)} collective-permute-done((bf16[8,512,128]{2,1,0:T(8,128)(2,1)S(1)}, bf16[8,512,128]{2,1,0:T(8,128)(2,1)S(1)}, u32[]{:S(2)}, u32[]{:S(2)}) %collective-permute-start.14) | collective-permute-done | bytes 1048608 | tf_op jit(solution)/shard_map/ppermute | solution.py:70
  113.0 4.2 %shard_map.83 = (f32[512,512]{1,0:T(8,128)S(1)}, bf16[4096,512]{1,0:T(8,128)(2,1)}) custom-call(s32[2]{0:T(128)S(1)} %pad_add_fusion.me, bf16[8,512,128]{2,1,0:T(8,128)(2,1)S(1)} %collective-permute-done.14.a_ref, bf16[8,512,128]{2,1,0:T(8,128)(2,1)S(1)} %collective-permute-done.31.b_ref, ...), custom_call_target="tpu_custom_call", output_to_operand_aliasing={{0}: (5, {}), {1}: (6, {})} | custom-call | flops 134217728 | bytes 262144 | tf_op jit(solution)/shard_map/pallas_call | solution.py:208
  117.2 7.0 %collective-permute-done.32.a_ref = bf16[8,512,128]{2,1,0:T(8,128)(2,1)S(1)} collective-permute-done((bf16[8,512,128]{2,1,0:T(8,128)(2,1)S(1)}, bf16[8,512,128]{2,1,0:T(8,128)(2,1)S(1)}, u32[]{:S(2)}, u32[]{:S(2)}) %collective-permute-start.32) | collective-permute-done | bytes 1048608 | tf_op jit(solution)/shard_map/ppermute | solution.py:70
  124.3 2.3 %shard_map.84 = f32[512,512]{1,0:T(8,128)S(1)} custom-call(s32[2]{0:T(128)S(1)} %pad_add_fusion.me, bf16[8,512,128]{2,1,0:T(8,128)(2,1)S(1)} %collective-permute-done.32.a_ref, bf16[8,512,128]{2,1,0:T(8,128)(2,1)S(1)} %collective-permute-done.33.b_ref, bf16[512,4096]{1,0:T(8,128)(2,1)S(1)} %copy-done.2, ...), custom_call_target="tpu_custom_call", output_to_operand_aliasing={{}: (4, {})} | custom-call | flops 134217728 | bytes 262144 | tf_op jit(solution)/shard_map/pallas_call | solution.py:208
  126.7 4.0 %collective-permute-start.34 = (bf16[2,256,512]{2,1,0:T(8,128)(2,1)S(1)}, bf16[2,256,512]{2,1,0:T(8,128)(2,1)S(1)}, u32[]{:S(2)}, u32[]{:S(2)}) collective-permute-start(bf16[2,256,512]{2,1,0:T(8,128)(2,1)S(1)} %pad_maximum_fusion.4), channel_id=1, source_target_pairs={{0,16},{1,17},{2,18},{3,19},{4,20},{5,21},{6,22},{7,23},{8,24},{9,... | collective-permute-start | bytes 1572872 | tf_op jit(solution)/shard_map/ppermute | solution.py:70
  133.0 2.7 %collective-permute-start.37 = (bf16[2,64,512]{2,1,0:T(8,128)(2,1)S(1)}, bf16[2,64,512]{2,1,0:T(8,128)(2,1)S(1)}, u32[]{:S(2)}, u32[]{:S(2)}) collective-permute-start(bf16[2,64,512]{2,1,0:T(8,128)(2,1)S(1)} %pad_maximum_fusion.16), channel_id=1, source_target_pairs={{0,64},{1,65},{2,66},{3,67},{4,68},{5,69},{6,70},{7,71},{8,72},{9,... | collective-permute-start | bytes 393224 | tf_op jit(solution)/shard_map/ppermute | solution.py:70
  136.6 3.0 %shard_map.85 = bf16[512,4096]{1,0:T(8,128)(2,1)} custom-call(s32[2]{0:T(128)S(1)} %pad_add_fusion.me, bf16[8,512,128]{2,1,0:T(8,128)(2,1)S(1)} %collective-permute-done.32.a_ref, bf16[8,512,128]{2,1,0:T(8,128)(2,1)S(1)} %collective-permute-done.33.b_ref, ...), custom_call_target="tpu_custom_call", output_to_operand_aliasing={{}: (4, {})} | custom-call | flops 134217728 | bytes 262144 | tf_op jit(solution)/shard_map/pallas_call | solution.py:208
  140.4 2.3 %collective-permute-done.35 = bf16[2,64,512]{2,1,0:T(8,128)(2,1)S(1)} collective-permute-done((bf16[2,64,512]{2,1,0:T(8,128)(2,1)S(1)}, bf16[2,64,512]{2,1,0:T(8,128)(2,1)S(1)}, u32[]{:S(2)}, u32[]{:S(2)}) %collective-permute-start.35) | collective-permute-done | bytes 131104 | tf_op jit(solution)/shard_map/ppermute | solution.py:70
  (123 shorter events, 39.9 us)
Async XLA Ops:
  0.6 6.5 %collective-permute-start = (bf16[64,512]{1,0:T(8,128)(2,1)}, bf16[64,512]{1,0:T(8,128)(2,1)S(1)}, u32[]{:S(2)}, u32[]{:S(2)}) collective-permute-start(bf16[64,512]{1,0:T(8,128)(2,1)} %param.4), channel_id=1, source_target_pairs={{0,32},{1,33},{2,34},{3,35},{4,36},{5,37},{6,38},{7,39},{8,40},{9,... | collective-permute-start | bytes 196616 | tf_op jit(solution)/shard_map/ppermute | solution.py:70
  5.3 9.4 %collective-permute-start.15 = (bf16[64,512]{1,0:T(8,128)(2,1)}, bf16[64,512]{1,0:T(8,128)(2,1)S(1)}, u32[]{:S(2)}, u32[]{:S(2)}) collective-permute-start(bf16[64,512]{1,0:T(8,128)(2,1)} %param.7), channel_id=1, source_target_pairs={{0,32},{1,33},{2,34},{3,35},{4,36},{5,37},{6,38},{7,39},{8,40},{9,... | collective-permute-start | bytes 196616 | tf_op jit(solution)/shard_map/ppermute | solution.py:70
  15.6 6.7 %collective-permute-start.16 = (bf16[128,512]{1,0:T(8,128)(2,1)S(1)}, bf16[128,512]{1,0:T(8,128)(2,1)S(1)}, u32[]{:S(2)}, u32[]{:S(2)}) collective-permute-start(bf16[128,512]{1,0:T(8,128)(2,1)S(1)} %pad_maximum_fusion.13), channel_id=1, source_target_pairs={{0,96},{1,97},{2,98},{3,99},{4,100},{5,101},{6,102},{7,103},{8,104... | collective-permute-start | bytes 393224 | tf_op jit(solution)/shard_map/ppermute | solution.py:70
  19.4 18.9 %collective-permute-start.5 = (bf16[8,512,128]{2,1,0:T(8,128)(2,1)S(1)}, bf16[8,512,128]{2,1,0:T(8,128)(2,1)S(1)}, u32[]{:S(2)}, u32[]{:S(2)}) collective-permute-start(bf16[8,512,128]{2,1,0:T(8,128)(2,1)S(1)} %shard_map.77), channel_id=1, source_target_pairs={{0,3},{1,2},{2,1},{3,0},{4,7},{5,6},{6,5},{7,4},{8,11},{9,10},{10,... | collective-permute-start | bytes 3145736 | tf_op jit(solution)/shard_map/ppermute | solution.py:70
  26.9 14.0 %collective-permute-start.3 = (bf16[8,512,128]{2,1,0:T(8,128)(2,1)S(1)}, bf16[8,512,128]{2,1,0:T(8,128)(2,1)S(1)}, u32[]{:S(2)}, u32[]{:S(2)}) collective-permute-start(bf16[8,512,128]{2,1,0:T(8,128)(2,1)S(1)} %shard_map.76), channel_id=1, source_target_pairs={{0,1},{1,0},{2,3},{3,2},{4,5},{5,4},{6,7},{7,6},{8,9},{9,8},{10,11... | collective-permute-start | bytes 3145736 | tf_op jit(solution)/shard_map/ppermute | solution.py:70
  29.7 16.3 %collective-permute-start.20 = (bf16[8,512,128]{2,1,0:T(8,128)(2,1)S(1)}, bf16[8,512,128]{2,1,0:T(8,128)(2,1)S(1)}, u32[]{:S(2)}, u32[]{:S(2)}) collective-permute-start(bf16[8,512,128]{2,1,0:T(8,128)(2,1)S(1)} %shard_map.80), channel_id=1, source_target_pairs={{0,3},{1,2},{2,1},{3,0},{4,7},{5,6},{6,5},{7,4},{8,11},{9,10},{10,... | collective-permute-start | bytes 3145736 | tf_op jit(solution)/shard_map/ppermute | solution.py:70
  33.0 19.1 %collective-permute-start.18 = (bf16[8,512,128]{2,1,0:T(8,128)(2,1)S(1)}, bf16[8,512,128]{2,1,0:T(8,128)(2,1)S(1)}, u32[]{:S(2)}, u32[]{:S(2)}) collective-permute-start(bf16[8,512,128]{2,1,0:T(8,128)(2,1)S(1)} %shard_map.79), channel_id=1, source_target_pairs={{0,1},{1,0},{2,3},{3,2},{4,5},{5,4},{6,7},{7,6},{8,9},{9,8},{10,11... | collective-permute-start | bytes 3145736 | tf_op jit(solution)/shard_map/ppermute | solution.py:70
  38.5 19.2 %collective-permute-start.6 = (bf16[4,512,128]{2,1,0:T(8,128)(2,1)S(1)}, bf16[4,512,128]{2,1,0:T(8,128)(2,1)S(1)}, u32[]{:S(2)}, u32[]{:S(2)}) collective-permute-start(bf16[4,512,128]{2,1,0:T(8,128)(2,1)S(1)} %add_convert_fusion.2), channel_id=1, source_target_pairs={{0,1},{1,0},{2,3},{3,2},{4,5},{5,4},{6,7},{7,6},{8,9},{9,8},{10,11... | collective-permute-start | bytes 1572872 | tf_op jit(solution)/shard_map/ppermute | solution.py:70
  41.1 17.0 %collective-permute-start.4 = (bf16[4,512,128]{2,1,0:T(8,128)(2,1)S(1)}, bf16[4,512,128]{2,1,0:T(8,128)(2,1)S(1)}, u32[]{:S(2)}, u32[]{:S(2)}) collective-permute-start(bf16[4,512,128]{2,1,0:T(8,128)(2,1)S(1)} %add_convert_fusion.3), channel_id=1, source_target_pairs={{0,3},{1,2},{2,1},{3,0},{4,7},{5,6},{6,5},{7,4},{8,11},{9,10},{10,... | collective-permute-start | bytes 1572872 | tf_op jit(solution)/shard_map/ppermute | solution.py:70
  46.1 17.3 %collective-permute-start.21 = (bf16[4,512,128]{2,1,0:T(8,128)(2,1)S(1)}, bf16[4,512,128]{2,1,0:T(8,128)(2,1)S(1)}, u32[]{:S(2)}, u32[]{:S(2)}) collective-permute-start(bf16[4,512,128]{2,1,0:T(8,128)(2,1)S(1)} %add_convert_fusion), channel_id=1, source_target_pairs={{0,1},{1,0},{2,3},{3,2},{4,5},{5,4},{6,7},{7,6},{8,9},{9,8},{10,11... | collective-permute-start | bytes 1572872 | tf_op jit(solution)/shard_map/ppermute | solution.py:70
  52.3 11.3 %collective-permute-start.19 = (bf16[4,512,128]{2,1,0:T(8,128)(2,1)S(1)}, bf16[4,512,128]{2,1,0:T(8,128)(2,1)S(1)}, u32[]{:S(2)}, u32[]{:S(2)}) collective-permute-start(bf16[4,512,128]{2,1,0:T(8,128)(2,1)S(1)} %add_convert_fusion.1), channel_id=1, source_target_pairs={{0,3},{1,2},{2,1},{3,0},{4,7},{5,6},{6,5},{7,4},{8,11},{9,10},{10,... | collective-permute-start | bytes 1572872 | tf_op jit(solution)/shard_map/ppermute | solution.py:70
  58.4 10.5 %collective-permute-start.8 = (bf16[2,512,128]{2,1,0:T(8,128)(2,1)S(1)}, bf16[2,512,128]{2,1,0:T(8,128)(2,1)S(1)}, u32[]{:S(2)}, u32[]{:S(2)}) collective-permute-start(bf16[2,512,128]{2,1,0:T(8,128)(2,1)S(1)} %pad_maximum_fusion.6), channel_id=1, source_target_pairs={{0,12},{1,13},{2,14},{3,15},{4,8},{5,9},{6,10},{7,11},{8,4},{9,5},... | collective-permute-start | bytes 786440 | tf_op jit(solution)/shard_map/ppermute | solution.py:70
  58.7 10.2 %collective-permute-start.9 = (bf16[2,512,128]{2,1,0:T(8,128)(2,1)S(1)}, bf16[2,512,128]{2,1,0:T(8,128)(2,1)S(1)}, u32[]{:S(2)}, u32[]{:S(2)}) collective-permute-start(bf16[2,512,128]{2,1,0:T(8,128)(2,1)S(1)} %pad_maximum_fusion.7), channel_id=1, source_target_pairs={{0,8},{1,9},{2,10},{3,11},{4,12},{5,13},{6,14},{7,15},{8,0},{9,1},... | collective-permute-start | bytes 786440 | tf_op jit(solution)/shard_map/ppermute | solution.py:70
  60.3 9.2 %collective-permute-start.7 = (bf16[2,512,128]{2,1,0:T(8,128)(2,1)S(1)}, bf16[2,512,128]{2,1,0:T(8,128)(2,1)S(1)}, u32[]{:S(2)}, u32[]{:S(2)}) collective-permute-start(bf16[2,512,128]{2,1,0:T(8,128)(2,1)S(1)} %pad_maximum_fusion.5), channel_id=1, source_target_pairs={{0,4},{1,5},{2,6},{3,7},{4,0},{5,1},{6,2},{7,3},{8,12},{9,13},{10,... | collective-permute-start | bytes 786440 | tf_op jit(solution)/shard_map/ppermute | solution.py:70
  64.0 10.5 %collective-permute-start.23 = (bf16[2,512,128]{2,1,0:T(8,128)(2,1)S(1)}, bf16[2,512,128]{2,1,0:T(8,128)(2,1)S(1)}, u32[]{:S(2)}, u32[]{:S(2)}) collective-permute-start(bf16[2,512,128]{2,1,0:T(8,128)(2,1)S(1)} %pad_maximum_fusion.10), channel_id=1, source_target_pairs={{0,12},{1,13},{2,14},{3,15},{4,8},{5,9},{6,10},{7,11},{8,4},{9,5},... | collective-permute-start | bytes 786440 | tf_op jit(solution)/shard_map/ppermute | solution.py:70
  64.3 10.2 %collective-permute-start.24 = (bf16[2,512,128]{2,1,0:T(8,128)(2,1)S(1)}, bf16[2,512,128]{2,1,0:T(8,128)(2,1)S(1)}, u32[]{:S(2)}, u32[]{:S(2)}) collective-permute-start(bf16[2,512,128]{2,1,0:T(8,128)(2,1)S(1)} %pad_maximum_fusion.11), channel_id=1, source_target_pairs={{0,8},{1,9},{2,10},{3,11},{4,12},{5,13},{6,14},{7,15},{8,0},{9,1},... | collective-permute-start | bytes 786440 | tf_op jit(solution)/shard_map/ppermute | solution.py:70
  69.8 11.5 %collective-permute-start.12 = (bf16[2,512,128]{2,1,0:T(8,128)(2,1)S(1)}, bf16[2,512,128]{2,1,0:T(8,128)(2,1)S(1)}, u32[]{:S(2)}, u32[]{:S(2)}) collective-permute-start(bf16[2,512,128]{2,1,0:T(8,128)(2,1)S(1)} %get-tuple-element.24), channel_id=1, source_target_pairs={{0,12},{1,13},{2,14},{3,15},{4,8},{5,9},{6,10},{7,11},{8,4},{9,5},... | collective-permute-start | bytes 786440 | tf_op jit(solution)/shard_map/ppermute | solution.py:70
  70.3 10.8 %collective-permute-start.11 = (bf16[2,512,128]{2,1,0:T(8,128)(2,1)S(1)}, bf16[2,512,128]{2,1,0:T(8,128)(2,1)S(1)}, u32[]{:S(2)}, u32[]{:S(2)}) collective-permute-start(bf16[2,512,128]{2,1,0:T(8,128)(2,1)S(1)} %get-tuple-element.24), channel_id=1, source_target_pairs={{0,8},{1,9},{2,10},{3,11},{4,12},{5,13},{6,14},{7,15},{8,0},{9,1},... | collective-permute-start | bytes 786440 | tf_op jit(solution)/shard_map/ppermute | solution.py:70
  74.5 6.2 %collective-permute-start.10 = (bf16[2,512,128]{2,1,0:T(8,128)(2,1)S(1)}, bf16[2,512,128]{2,1,0:T(8,128)(2,1)S(1)}, u32[]{:S(2)}, u32[]{:S(2)}) collective-permute-start(bf16[2,512,128]{2,1,0:T(8,128)(2,1)S(1)} %get-tuple-element.24), channel_id=1, source_target_pairs={{0,4},{1,5},{2,6},{3,7},{4,0},{5,1},{6,2},{7,3},{8,12},{9,13},{10,... | collective-permute-start | bytes 786440 | tf_op jit(solution)/shard_map/ppermute | solution.py:70
  75.3 11.2 %collective-permute-start.27 = (bf16[2,512,128]{2,1,0:T(8,128)(2,1)S(1)}, bf16[2,512,128]{2,1,0:T(8,128)(2,1)S(1)}, u32[]{:S(2)}, u32[]{:S(2)}) collective-permute-start(bf16[2,512,128]{2,1,0:T(8,128)(2,1)S(1)} %fusion.11), channel_id=1, source_target_pairs={{0,12},{1,13},{2,14},{3,15},{4,8},{5,9},{6,10},{7,11},{8,4},{9,5},... | collective-permute-start | bytes 786440 | tf_op jit(solution)/shard_map/ppermute | solution.py:70
  75.9 10.5 %collective-permute-start.26 = (bf16[2,512,128]{2,1,0:T(8,128)(2,1)S(1)}, bf16[2,512,128]{2,1,0:T(8,128)(2,1)S(1)}, u32[]{:S(2)}, u32[]{:S(2)}) collective-permute-start(bf16[2,512,128]{2,1,0:T(8,128)(2,1)S(1)} %fusion.11), channel_id=1, source_target_pairs={{0,8},{1,9},{2,10},{3,11},{4,12},{5,13},{6,14},{7,15},{8,0},{9,1},... | collective-permute-start | bytes 786440 | tf_op jit(solution)/shard_map/ppermute | solution.py:70
  81.4 16.7 %collective-permute-start.13 = (bf16[4,512,128]{2,1,0:T(8,128)(2,1)S(1)}, bf16[4,512,128]{2,1,0:T(8,128)(2,1)S(1)}, u32[]{:S(2)}, u32[]{:S(2)}) collective-permute-start(bf16[4,512,128]{2,1,0:T(8,128)(2,1)S(1)} %pad_maximum_fusion), channel_id=1, source_target_pairs={{0,3},{1,2},{2,1},{3,0},{4,7},{5,6},{6,5},{7,4},{8,11},{9,10},{10,... | collective-permute-start | bytes 1572872 | tf_op jit(solution)/shard_map/ppermute | solution.py:70
  84.3 11.8 %collective-permute-start.30 = (bf16[4,512,128]{2,1,0:T(8,128)(2,1)S(1)}, bf16[4,512,128]{2,1,0:T(8,128)(2,1)S(1)}, u32[]{:S(2)}, u32[]{:S(2)}) collective-permute-start(bf16[4,512,128]{2,1,0:T(8,128)(2,1)S(1)} %pad_maximum_fusion.3), channel_id=1, source_target_pairs={{0,1},{1,0},{2,3},{3,2},{4,5},{5,4},{6,7},{7,6},{8,9},{9,8},{10,11... | collective-permute-start | bytes 1572872 | tf_op jit(solution)/shard_map/ppermute | solution.py:70
  86.7 15.8 %collective-permute-start.29 = (bf16[4,512,128]{2,1,0:T(8,128)(2,1)S(1)}, bf16[4,512,128]{2,1,0:T(8,128)(2,1)S(1)}, u32[]{:S(2)}, u32[]{:S(2)}) collective-permute-start(bf16[4,512,128]{2,1,0:T(8,128)(2,1)S(1)} %pad_maximum_fusion.2), channel_id=1, source_target_pairs={{0,1},{1,0},{2,3},{3,2},{4,5},{5,4},{6,7},{7,6},{8,9},{9,8},{10,11... | collective-permute-start | bytes 1572872 | tf_op jit(solution)/shard_map/ppermute | solution.py:70
  88.2 14.4 %collective-permute-start.28 = (bf16[4,512,128]{2,1,0:T(8,128)(2,1)S(1)}, bf16[4,512,128]{2,1,0:T(8,128)(2,1)S(1)}, u32[]{:S(2)}, u32[]{:S(2)}) collective-permute-start(bf16[4,512,128]{2,1,0:T(8,128)(2,1)S(1)} %pad_maximum_fusion.1), channel_id=1, source_target_pairs={{0,3},{1,2},{2,1},{3,0},{4,7},{5,6},{6,5},{7,4},{8,11},{9,10},{10,... | collective-permute-start | bytes 1572872 | tf_op jit(solution)/shard_map/ppermute | solution.py:70
  96.2 16.8 %collective-permute-start.31 = (bf16[8,512,128]{2,1,0:T(8,128)(2,1)S(1)}, bf16[8,512,128]{2,1,0:T(8,128)(2,1)S(1)}, u32[]{:S(2)}, u32[]{:S(2)}) collective-permute-start(bf16[8,512,128]{2,1,0:T(8,128)(2,1)S(1)} %constant_dynamic-update-slice_fusion.26.b_ref), channel_id=1, source_target_pairs={{0,3},{1,2},{2,1},{3,0},{4,7},{5,6},{6,5},{7,4},{8,11},{9,10},{10,... | collective-permute-start | bytes 3145736 | tf_op jit(solution)/shard_map/ppermute | solution.py:70
  98.2 14.8 %collective-permute-start.14 = (bf16[8,512,128]{2,1,0:T(8,128)(2,1)S(1)}, bf16[8,512,128]{2,1,0:T(8,128)(2,1)S(1)}, u32[]{:S(2)}, u32[]{:S(2)}) collective-permute-start(bf16[8,512,128]{2,1,0:T(8,128)(2,1)S(1)} %constant_dynamic-update-slice_fusion.7.a_ref), channel_id=1, source_target_pairs={{0,1},{1,0},{2,3},{3,2},{4,5},{5,4},{6,7},{7,6},{8,9},{9,8},{10,11... | collective-permute-start | bytes 3145736 | tf_op jit(solution)/shard_map/ppermute | solution.py:70
  102.6 21.6 %collective-permute-start.32 = (bf16[8,512,128]{2,1,0:T(8,128)(2,1)S(1)}, bf16[8,512,128]{2,1,0:T(8,128)(2,1)S(1)}, u32[]{:S(2)}, u32[]{:S(2)}) collective-permute-start(bf16[8,512,128]{2,1,0:T(8,128)(2,1)S(1)} %constant_dynamic-update-slice_fusion.16.a_ref), channel_id=1, source_target_pairs={{0,1},{1,0},{2,3},{3,2},{4,5},{5,4},{6,7},{7,6},{8,9},{9,8},{10,11... | collective-permute-start | bytes 3145736 | tf_op jit(solution)/shard_map/ppermute | solution.py:70
  104.2 20.1 %collective-permute-start.33 = (bf16[8,512,128]{2,1,0:T(8,128)(2,1)S(1)}, bf16[8,512,128]{2,1,0:T(8,128)(2,1)S(1)}, u32[]{:S(2)}, u32[]{:S(2)}) collective-permute-start(bf16[8,512,128]{2,1,0:T(8,128)(2,1)S(1)} %constant_dynamic-update-slice_fusion.21.b_ref), channel_id=1, source_target_pairs={{0,3},{1,2},{2,1},{3,0},{4,7},{5,6},{6,5},{7,4},{8,11},{9,10},{10,... | collective-permute-start | bytes 3145736 | tf_op jit(solution)/shard_map/ppermute | solution.py:70
  132.5 7.2 %collective-permute-start.36 = (bf16[2,64,512]{2,1,0:T(8,128)(2,1)S(1)}, bf16[2,64,512]{2,1,0:T(8,128)(2,1)S(1)}, u32[]{:S(2)}, u32[]{:S(2)}) collective-permute-start(bf16[2,64,512]{2,1,0:T(8,128)(2,1)S(1)} %pad_maximum_fusion.15), channel_id=1, source_target_pairs={{0,96},{1,97},{2,98},{3,99},{4,100},{5,101},{6,102},{7,103},{8,104... | collective-permute-start | bytes 393224 | tf_op jit(solution)/shard_map/ppermute | solution.py:70
  133.0 7.4 %collective-permute-start.37 = (bf16[2,64,512]{2,1,0:T(8,128)(2,1)S(1)}, bf16[2,64,512]{2,1,0:T(8,128)(2,1)S(1)}, u32[]{:S(2)}, u32[]{:S(2)}) collective-permute-start(bf16[2,64,512]{2,1,0:T(8,128)(2,1)S(1)} %pad_maximum_fusion.16), channel_id=1, source_target_pairs={{0,64},{1,65},{2,66},{3,67},{4,68},{5,69},{6,70},{7,71},{8,72},{9,... | collective-permute-start | bytes 393224 | tf_op jit(solution)/shard_map/ppermute | solution.py:70
  135.7 6.9 %collective-permute-start.35 = (bf16[2,64,512]{2,1,0:T(8,128)(2,1)S(1)}, bf16[2,64,512]{2,1,0:T(8,128)(2,1)S(1)}, u32[]{:S(2)}, u32[]{:S(2)}) collective-permute-start(bf16[2,64,512]{2,1,0:T(8,128)(2,1)S(1)} %pad_maximum_fusion.14), channel_id=1, source_target_pairs={{0,32},{1,33},{2,34},{3,35},{4,36},{5,37},{6,38},{7,39},{8,40},{9,... | collective-permute-start | bytes 393224 | tf_op jit(solution)/shard_map/ppermute | solution.py:70
  (10 other events, 75.0 us)

commit v5 on v4

--- a/solution.py
+++ b/solution.py
@@ -332,7 +332,7 @@
     p_far = spread_third(p_near)
     d_near = spread_second(d_four)
     total, grad = consume(p_near[0], p_near[1], w_out, cotangent, me, True, 0)
-    d_far = spread_third([after(d_near[h], total) for h in range(2)])
+    d_far = spread_third(d_near)
     d_total, d_grad = consume(d_near[0], d_near[1], w_in, inputs, me, False, 0)
     p_far[0] = after(p_far[0], d_total)
     total, grad_out = consume(p_far[0], p_far[1], w_out, cotangent, me, True, 1, total, grad)

time: 145 us -> 145 us (level)
  transfers between devices with their start and end apart: 38 -> 38, of which waited for: 20 -> 23; matrix products, arithmetic and copies ran while one was open for 5% -> 5% of each run, Pallas kernels for 18% -> 18%
where the time goes in v5:
time: 145 us; the launch traced here: 143 us
  starting transfers between devices  55 us (38%)
  waiting for transfers between devices  49.3 us (34%)
  Pallas kernels  28.2 us (19%)
  other arithmetic  5.38 us (4%)
  local copies, waits for them, and re-layouts  4.35 us (3%)
    ppermute x38, starting transfers between devices, send(): return lax.ppermute(block, BOTH, perm)  55 us
    ppermute x38, waiting for transfers between devices, send(): return lax.ppermute(block, BOTH, perm)  49.3 us
    pallas_call x5, Pallas kernels, consume(): pl.pallas_call(functools.partial(consume_body, transposed, total is not N...  18 us
    pallas_call x6, Pallas kernels, produce(): pl.pallas_call(functools.partial(produce_body, transposed, parts), out_sh...  10.2 us
    unnamed x13, local copies, waits for them, and re-layouts  3.08 us
  transfers between devices with their start and end apart: 38, of which 23 were waited for; matrix products, arithmetic and copies ran while one was open for 5% of the time, Pallas kernels for 18%

profile of v5, /device:TPU:1, one launch (start us, length us, event | category | flops | bytes accessed | tf_op | source)
XLA Modules:
  0.0 143.3 jit_solution(18193254023527398096)
XLA Ops:
  0.6 4.7 %collective-permute-start = (bf16[64,512]{1,0:T(8,128)(2,1)}, bf16[64,512]{1,0:T(8,128)(2,1)S(1)}, u32[]{:S(2)}, u32[]{:S(2)}) collective-permute-start(bf16[64,512]{1,0:T(8,128)(2,1)} %param.4), channel_id=1, source_target_pairs={{0,32},{1,33},{2,34},{3,35},{4,36},{5,37},{6,38},{7,39},{8,40},{9,... | collective-permute-start | bytes 196616 | tf_op jit(solution)/shard_map/ppermute | solution.py:70
  9.0 2.9 %collective-permute-done.1 = bf16[128,512]{1,0:T(8,128)(2,1)S(1)} collective-permute-done((bf16[128,512]{1,0:T(8,128)(2,1)S(1)}, bf16[128,512]{1,0:T(8,128)(2,1)S(1)}, u32[]{:S(2)}, u32[]{:S(2)}) %collective-permute-start.1) | collective-permute-done | bytes 131104 | tf_op jit(solution)/shard_map/ppermute | solution.py:70
  12.0 2.8 %collective-permute-start.2 = (bf16[256,512]{1,0:T(8,128)(2,1)S(1)}, bf16[256,512]{1,0:T(8,128)(2,1)S(1)}, u32[]{:S(2)}, u32[]{:S(2)}) collective-permute-start(bf16[256,512]{1,0:T(8,128)(2,1)S(1)} %get-tuple-element.104), channel_id=1, source_target_pairs={{0,16},{1,17},{2,18},{3,19},{4,20},{5,21},{6,22},{7,23},{8,24},{9,... | collective-permute-start | bytes 786440 | tf_op jit(solution)/shard_map/ppermute | solution.py:70
  15.9 2.2 %copy-done.1 = bf16[512,4096]{1,0:T(8,128)(2,1)S(1)} copy-done((bf16[512,4096]{1,0:T(8,128)(2,1)S(1)}, bf16[512,4096]{1,0:T(8,128)(2,1)}, u32[]{:S(2)}) %copy-start.1) | copy-done | bytes 4194328
  19.4 2.8 %collective-permute-start.5 = (bf16[8,512,128]{2,1,0:T(8,128)(2,1)S(1)}, bf16[8,512,128]{2,1,0:T(8,128)(2,1)S(1)}, u32[]{:S(2)}, u32[]{:S(2)}) collective-permute-start(bf16[8,512,128]{2,1,0:T(8,128)(2,1)S(1)} %shard_map.77), channel_id=1, source_target_pairs={{0,3},{1,2},{2,1},{3,0},{4,7},{5,6},{6,5},{7,4},{8,11},{9,10},{10,... | collective-permute-start | bytes 3145736 | tf_op jit(solution)/shard_map/ppermute | solution.py:70
  22.3 3.3 %collective-permute-start.17 = (bf16[256,512]{1,0:T(8,128)(2,1)S(1)}, bf16[256,512]{1,0:T(8,128)(2,1)S(1)}, u32[]{:S(2)}, u32[]{:S(2)}) collective-permute-start(bf16[256,512]{1,0:T(8,128)(2,1)S(1)} %pad_maximum_fusion.8), channel_id=1, source_target_pairs={{0,16},{1,17},{2,18},{3,19},{4,20},{5,21},{6,22},{7,23},{8,24},{9,... | collective-permute-start | bytes 786440 | tf_op jit(solution)/shard_map/ppermute | solution.py:70
  33.5 2.5 %shard_map.75 = (bf16[8,512,128]{2,1,0:T(8,128)(2,1)S(1)}, bf16[8,512,128]{2,1,0:T(8,128)(2,1)S(1)}) custom-call(s32[2]{0:T(128)S(1)} %pad_add_fusion.me, bf16[512,512]{1,0:T(8,128)(2,1)S(1)} %constant_dynamic-update-slice_fusion.3.x_ref.rest_1_.rest_0_, bf16[512,4096]{1,0:T(8,128)(2,1)S(1)} %copy-done.1), custom_call_target="tpu_custom_call" | custom-call | flops 67108864 | bytes 262144 | tf_op jit(solution)/shard_map/pallas_call | solution.py:127
  36.0 2.4 %shard_map.78 = (bf16[8,512,128]{2,1,0:T(8,128)(2,1)S(1)}, bf16[8,512,128]{2,1,0:T(8,128)(2,1)S(1)}) custom-call(s32[2]{0:T(128)S(1)} %pad_add_fusion.me, bf16[512,512]{1,0:T(8,128)(2,1)S(1)} %constant_dynamic-update-slice_fusion.12.x_ref.rest_1_, bf16[4096,512]{1,0:T(8,128)(2,1)S(1)} %copy-done), custom_call_target="tpu_custom_call" | custom-call | flops 67108864 | bytes 262144 | tf_op jit(solution)/shard_map/pallas_call | solution.py:127
  41.1 2.8 %collective-permute-start.4 = (bf16[4,512,128]{2,1,0:T(8,128)(2,1)S(1)}, bf16[4,512,128]{2,1,0:T(8,128)(2,1)S(1)}, u32[]{:S(2)}, u32[]{:S(2)}) collective-permute-start(bf16[4,512,128]{2,1,0:T(8,128)(2,1)S(1)} %add_convert_fusion.3), channel_id=1, source_target_pairs={{0,3},{1,2},{2,1},{3,0},{4,7},{5,6},{6,5},{7,4},{8,11},{9,10},{10,... | collective-permute-start | bytes 1572872 | tf_op jit(solution)/shard_map/ppermute | solution.py:70
  43.9 2.1 %collective-permute-done.20 = bf16[8,512,128]{2,1,0:T(8,128)(2,1)S(1)} collective-permute-done((bf16[8,512,128]{2,1,0:T(8,128)(2,1)S(1)}, bf16[8,512,128]{2,1,0:T(8,128)(2,1)S(1)}, u32[]{:S(2)}, u32[]{:S(2)}) %collective-permute-start.20) | collective-permute-done | bytes 1048608 | tf_op jit(solution)/shard_map/ppermute | solution.py:70
  46.2 5.9 %collective-permute-done.18 = bf16[8,512,128]{2,1,0:T(8,128)(2,1)S(1)} collective-permute-done((bf16[8,512,128]{2,1,0:T(8,128)(2,1)S(1)}, bf16[8,512,128]{2,1,0:T(8,128)(2,1)S(1)}, u32[]{:S(2)}, u32[]{:S(2)}) %collective-permute-start.18) | collective-permute-done | bytes 1048608 | tf_op jit(solution)/shard_map/ppermute | solution.py:70
  52.3 2.8 %collective-permute-start.19 = (bf16[4,512,128]{2,1,0:T(8,128)(2,1)S(1)}, bf16[4,512,128]{2,1,0:T(8,128)(2,1)S(1)}, u32[]{:S(2)}, u32[]{:S(2)}) collective-permute-start(bf16[4,512,128]{2,1,0:T(8,128)(2,1)S(1)} %add_convert_fusion.1), channel_id=1, source_target_pairs={{0,3},{1,2},{2,1},{3,0},{4,7},{5,6},{6,5},{7,4},{8,11},{9,10},{10,... | collective-permute-start | bytes 1572872 | tf_op jit(solution)/shard_map/ppermute | solution.py:70
  55.1 2.7 %collective-permute-done.6 = bf16[4,512,128]{2,1,0:T(8,128)(2,1)S(1)} collective-permute-done((bf16[4,512,128]{2,1,0:T(8,128)(2,1)S(1)}, bf16[4,512,128]{2,1,0:T(8,128)(2,1)S(1)}, u32[]{:S(2)}, u32[]{:S(2)}) %collective-permute-start.6) | collective-permute-done | bytes 524320 | tf_op jit(solution)/shard_map/ppermute | solution.py:70
  65.9 2.9 %collective-permute-done.8 = bf16[2,512,128]{2,1,0:T(8,128)(2,1)S(1)} collective-permute-done((bf16[2,512,128]{2,1,0:T(8,128)(2,1)S(1)}, bf16[2,512,128]{2,1,0:T(8,128)(2,1)S(1)}, u32[]{:S(2)}, u32[]{:S(2)}) %collective-permute-start.8) | collective-permute-done | bytes 262176 | tf_op jit(solution)/shard_map/ppermute | solution.py:70
  70.3 2.4 %collective-permute-start.11 = (bf16[2,512,128]{2,1,0:T(8,128)(2,1)S(1)}, bf16[2,512,128]{2,1,0:T(8,128)(2,1)S(1)}, u32[]{:S(2)}, u32[]{:S(2)}) collective-permute-start(bf16[2,512,128]{2,1,0:T(8,128)(2,1)S(1)} %get-tuple-element.22), channel_id=1, source_target_pairs={{0,8},{1,9},{2,10},{3,11},{4,12},{5,13},{6,14},{7,15},{8,0},{9,1},... | collective-permute-start | bytes 786440 | tf_op jit(solution)/shard_map/ppermute | solution.py:70
  75.9 2.3 %collective-permute-start.26 = (bf16[2,512,128]{2,1,0:T(8,128)(2,1)S(1)}, bf16[2,512,128]{2,1,0:T(8,128)(2,1)S(1)}, u32[]{:S(2)}, u32[]{:S(2)}) collective-permute-start(bf16[2,512,128]{2,1,0:T(8,128)(2,1)S(1)} %fusion.11), channel_id=1, source_target_pairs={{0,8},{1,9},{2,10},{3,11},{4,12},{5,13},{6,14},{7,15},{8,0},{9,1},... | collective-permute-start | bytes 786440 | tf_op jit(solution)/shard_map/ppermute | solution.py:70
  78.3 2.4 %collective-permute-done.10 = bf16[2,512,128]{2,1,0:T(8,128)(2,1)S(1)} collective-permute-done((bf16[2,512,128]{2,1,0:T(8,128)(2,1)S(1)}, bf16[2,512,128]{2,1,0:T(8,128)(2,1)S(1)}, u32[]{:S(2)}, u32[]{:S(2)}) %collective-permute-start.10) | collective-permute-done | bytes 262176 | tf_op jit(solution)/shard_map/ppermute | solution.py:70
  81.4 2.8 %collective-permute-start.13 = (bf16[4,512,128]{2,1,0:T(8,128)(2,1)S(1)}, bf16[4,512,128]{2,1,0:T(8,128)(2,1)S(1)}, u32[]{:S(2)}, u32[]{:S(2)}) collective-permute-start(bf16[4,512,128]{2,1,0:T(8,128)(2,1)S(1)} %pad_maximum_fusion), channel_id=1, source_target_pairs={{0,3},{1,2},{2,1},{3,0},{4,7},{5,6},{6,5},{7,4},{8,11},{9,10},{10,... | collective-permute-start | bytes 1572872 | tf_op jit(solution)/shard_map/ppermute | solution.py:70
  88.2 2.0 %collective-permute-start.28 = (bf16[4,512,128]{2,1,0:T(8,128)(2,1)S(1)}, bf16[4,512,128]{2,1,0:T(8,128)(2,1)S(1)}, u32[]{:S(2)}, u32[]{:S(2)}) collective-permute-start(bf16[4,512,128]{2,1,0:T(8,128)(2,1)S(1)} %pad_maximum_fusion.1), channel_id=1, source_target_pairs={{0,3},{1,2},{2,1},{3,0},{4,7},{5,6},{6,5},{7,4},{8,11},{9,10},{10,... | collective-permute-start | bytes 1572872 | tf_op jit(solution)/shard_map/ppermute | solution.py:70
  90.1 5.1 %collective-permute-done.13 = bf16[4,512,128]{2,1,0:T(8,128)(2,1)S(1)} collective-permute-done((bf16[4,512,128]{2,1,0:T(8,128)(2,1)S(1)}, bf16[4,512,128]{2,1,0:T(8,128)(2,1)S(1)}, u32[]{:S(2)}, u32[]{:S(2)}) %collective-permute-start.13) | collective-permute-done | bytes 524320 | tf_op jit(solution)/shard_map/ppermute | solution.py:70
  96.2 2.1 %collective-permute-start.31 = (bf16[8,512,128]{2,1,0:T(8,128)(2,1)S(1)}, bf16[8,512,128]{2,1,0:T(8,128)(2,1)S(1)}, u32[]{:S(2)}, u32[]{:S(2)}) collective-permute-start(bf16[8,512,128]{2,1,0:T(8,128)(2,1)S(1)} %constant_dynamic-update-slice_fusion.26.b_ref), channel_id=1, source_target_pairs={{0,3},{1,2},{2,1},{3,0},{4,7},{5,6},{6,5},{7,4},{8,11},{9,10},{10,... | collective-permute-start | bytes 3145736 | tf_op jit(solution)/shard_map/ppermute | solution.py:70
  98.3 3.5 %collective-permute-done.29 = bf16[4,512,128]{2,1,0:T(8,128)(2,1)S(1)} collective-permute-done((bf16[4,512,128]{2,1,0:T(8,128)(2,1)S(1)}, bf16[4,512,128]{2,1,0:T(8,128)(2,1)S(1)}, u32[]{:S(2)}, u32[]{:S(2)}) %collective-permute-start.29) | collective-permute-done | bytes 524320 | tf_op jit(solution)/shard_map/ppermute | solution.py:70
  101.9 2.3 %collective-permute-start.33 = (bf16[8,512,128]{2,1,0:T(8,128)(2,1)S(1)}, bf16[8,512,128]{2,1,0:T(8,128)(2,1)S(1)}, u32[]{:S(2)}, u32[]{:S(2)}) collective-permute-start(bf16[8,512,128]{2,1,0:T(8,128)(2,1)S(1)} %constant_dynamic-update-slice_fusion.21.b_ref), channel_id=1, source_target_pairs={{0,3},{1,2},{2,1},{3,0},{4,7},{5,6},{6,5},{7,4},{8,11},{9,10},{10,... | collective-permute-start | bytes 3145736 | tf_op jit(solution)/shard_map/ppermute | solution.py:70
  104.3 4.2 %shard_map.82 = (f32[512,512]{1,0:T(8,128)S(1)}, bf16[4096,512]{1,0:T(8,128)(2,1)}) custom-call(s32[2]{0:T(128)S(1)} %pad_add_fusion.me, bf16[8,512,128]{2,1,0:T(8,128)(2,1)S(1)} %constant_dynamic-update-slice_fusion.7.a_ref, bf16[8,512,128]{2,1,0:T(8,128)(2,1)S(1)} %constant_dynamic-update-slice_fusion.26.b_ref, bf16[4096,512]{1,0:T(8,128)(2,1)S(1)} %copy-done, ...), custom_call_target="tpu_custom_call" | custom-call | flops 134217728 | bytes 262144 | tf_op jit(solution)/shard_map/pallas_call | solution.py:208
  108.5 4.3 %shard_map.81 = (f32[512,512]{1,0:T(8,128)S(1)}, bf16[512,4096]{1,0:T(8,128)(2,1)}) custom-call(s32[2]{0:T(128)S(1)} %pad_add_fusion.me, bf16[8,512,128]{2,1,0:T(8,128)(2,1)S(1)} %constant_dynamic-update-slice_fusion.16.a_ref, bf16[8,512,128]{2,1,0:T(8,128)(2,1)S(1)} %constant_dynamic-update-slice_fusion.21.b_ref, bf16[512,4096]{1,0:T(8,128)(2,1)S(1)} %copy-done.1, ...), custom_call_target="tpu_custom_call" | custom-call | flops 134217728 | bytes 262144 | tf_op jit(solution)/shard_map/pallas_call | solution.py:208
  113.0 4.2 %shard_map.83 = (f32[512,512]{1,0:T(8,128)S(1)}, bf16[4096,512]{1,0:T(8,128)(2,1)}) custom-call(s32[2]{0:T(128)S(1)} %pad_add_fusion.me, bf16[8,512,128]{2,1,0:T(8,128)(2,1)S(1)} %collective-permute-done.14.a_ref, bf16[8,512,128]{2,1,0:T(8,128)(2,1)S(1)} %collective-permute-done.31.b_ref, ...), custom_call_target="tpu_custom_call", output_to_operand_aliasing={{0}: (5, {}), {1}: (6, {})} | custom-call | flops 134217728 | bytes 262144 | tf_op jit(solution)/shard_map/pallas_call | solution.py:208
  117.2 6.1 %collective-permute-done.33.b_ref = bf16[8,512,128]{2,1,0:T(8,128)(2,1)S(1)} collective-permute-done((bf16[8,512,128]{2,1,0:T(8,128)(2,1)S(1)}, bf16[8,512,128]{2,1,0:T(8,128)(2,1)S(1)}, u32[]{:S(2)}, u32[]{:S(2)}) %collective-permute-start.33) | collective-permute-done | bytes 1048608 | tf_op jit(solution)/shard_map/ppermute | solution.py:70
  124.3 2.3 %shard_map.84 = f32[512,512]{1,0:T(8,128)S(1)} custom-call(s32[2]{0:T(128)S(1)} %pad_add_fusion.me, bf16[8,512,128]{2,1,0:T(8,128)(2,1)S(1)} %collective-permute-done.32.a_ref, bf16[8,512,128]{2,1,0:T(8,128)(2,1)S(1)} %collective-permute-done.33.b_ref, bf16[512,4096]{1,0:T(8,128)(2,1)S(1)} %copy-done.2, ...), custom_call_target="tpu_custom_call", output_to_operand_aliasing={{}: (4, {})} | custom-call | flops 134217728 | bytes 262144 | tf_op jit(solution)/shard_map/pallas_call | solution.py:208
  126.7 4.0 %collective-permute-start.34 = (bf16[2,256,512]{2,1,0:T(8,128)(2,1)S(1)}, bf16[2,256,512]{2,1,0:T(8,128)(2,1)S(1)}, u32[]{:S(2)}, u32[]{:S(2)}) collective-permute-start(bf16[2,256,512]{2,1,0:T(8,128)(2,1)S(1)} %pad_maximum_fusion.4), channel_id=1, source_target_pairs={{0,16},{1,17},{2,18},{3,19},{4,20},{5,21},{6,22},{7,23},{8,24},{9,... | collective-permute-start | bytes 1572872 | tf_op jit(solution)/shard_map/ppermute | solution.py:70
  133.0 2.7 %collective-permute-start.37 = (bf16[2,64,512]{2,1,0:T(8,128)(2,1)S(1)}, bf16[2,64,512]{2,1,0:T(8,128)(2,1)S(1)}, u32[]{:S(2)}, u32[]{:S(2)}) collective-permute-start(bf16[2,64,512]{2,1,0:T(8,128)(2,1)S(1)} %pad_maximum_fusion.16), channel_id=1, source_target_pairs={{0,64},{1,65},{2,66},{3,67},{4,68},{5,69},{6,70},{7,71},{8,72},{9,... | collective-permute-start | bytes 393224 | tf_op jit(solution)/shard_map/ppermute | solution.py:70
  136.6 3.0 %shard_map.85 = bf16[512,4096]{1,0:T(8,128)(2,1)} custom-call(s32[2]{0:T(128)S(1)} %pad_add_fusion.me, bf16[8,512,128]{2,1,0:T(8,128)(2,1)S(1)} %collective-permute-done.32.a_ref, bf16[8,512,128]{2,1,0:T(8,128)(2,1)S(1)} %collective-permute-done.33.b_ref, ...), custom_call_target="tpu_custom_call", output_to_operand_aliasing={{}: (4, {})} | custom-call | flops 134217728 | bytes 262144 | tf_op jit(solution)/shard_map/pallas_call | solution.py:208
  140.4 2.3 %collective-permute-done.35 = bf16[2,64,512]{2,1,0:T(8,128)(2,1)S(1)} collective-permute-done((bf16[2,64,512]{2,1,0:T(8,128)(2,1)S(1)}, bf16[2,64,512]{2,1,0:T(8,128)(2,1)S(1)}, u32[]{:S(2)}, u32[]{:S(2)}) %collective-permute-start.35) | collective-permute-done | bytes 131104 | tf_op jit(solution)/shard_map/ppermute | solution.py:70
  (123 shorter events, 41.6 us)
Async XLA Ops:
  0.6 6.5 %collective-permute-start = (bf16[64,512]{1,0:T(8,128)(2,1)}, bf16[64,512]{1,0:T(8,128)(2,1)S(1)}, u32[]{:S(2)}, u32[]{:S(2)}) collective-permute-start(bf16[64,512]{1,0:T(8,128)(2,1)} %param.4), channel_id=1, source_target_pairs={{0,32},{1,33},{2,34},{3,35},{4,36},{5,37},{6,38},{7,39},{8,40},{9,... | collective-permute-start | bytes 196616 | tf_op jit(solution)/shard_map/ppermute | solution.py:70
  5.3 9.4 %collective-permute-start.15 = (bf16[64,512]{1,0:T(8,128)(2,1)}, bf16[64,512]{1,0:T(8,128)(2,1)S(1)}, u32[]{:S(2)}, u32[]{:S(2)}) collective-permute-start(bf16[64,512]{1,0:T(8,128)(2,1)} %param.7), channel_id=1, source_target_pairs={{0,32},{1,33},{2,34},{3,35},{4,36},{5,37},{6,38},{7,39},{8,40},{9,... | collective-permute-start | bytes 196616 | tf_op jit(solution)/shard_map/ppermute | solution.py:70
  15.6 6.7 %collective-permute-start.16 = (bf16[128,512]{1,0:T(8,128)(2,1)S(1)}, bf16[128,512]{1,0:T(8,128)(2,1)S(1)}, u32[]{:S(2)}, u32[]{:S(2)}) collective-permute-start(bf16[128,512]{1,0:T(8,128)(2,1)S(1)} %pad_maximum_fusion.13), channel_id=1, source_target_pairs={{0,96},{1,97},{2,98},{3,99},{4,100},{5,101},{6,102},{7,103},{8,104... | collective-permute-start | bytes 393224 | tf_op jit(solution)/shard_map/ppermute | solution.py:70
  19.4 18.9 %collective-permute-start.5 = (bf16[8,512,128]{2,1,0:T(8,128)(2,1)S(1)}, bf16[8,512,128]{2,1,0:T(8,128)(2,1)S(1)}, u32[]{:S(2)}, u32[]{:S(2)}) collective-permute-start(bf16[8,512,128]{2,1,0:T(8,128)(2,1)S(1)} %shard_map.77), channel_id=1, source_target_pairs={{0,3},{1,2},{2,1},{3,0},{4,7},{5,6},{6,5},{7,4},{8,11},{9,10},{10,... | collective-permute-start | bytes 3145736 | tf_op jit(solution)/shard_map/ppermute | solution.py:70
  26.9 14.0 %collective-permute-start.3 = (bf16[8,512,128]{2,1,0:T(8,128)(2,1)S(1)}, bf16[8,512,128]{2,1,0:T(8,128)(2,1)S(1)}, u32[]{:S(2)}, u32[]{:S(2)}) collective-permute-start(bf16[8,512,128]{2,1,0:T(8,128)(2,1)S(1)} %shard_map.76), channel_id=1, source_target_pairs={{0,1},{1,0},{2,3},{3,2},{4,5},{5,4},{6,7},{7,6},{8,9},{9,8},{10,11... | collective-permute-start | bytes 3145736 | tf_op jit(solution)/shard_map/ppermute | solution.py:70
  29.7 16.3 %collective-permute-start.20 = (bf16[8,512,128]{2,1,0:T(8,128)(2,1)S(1)}, bf16[8,512,128]{2,1,0:T(8,128)(2,1)S(1)}, u32[]{:S(2)}, u32[]{:S(2)}) collective-permute-start(bf16[8,512,128]{2,1,0:T(8,128)(2,1)S(1)} %shard_map.80), channel_id=1, source_target_pairs={{0,3},{1,2},{2,1},{3,0},{4,7},{5,6},{6,5},{7,4},{8,11},{9,10},{10,... | collective-permute-start | bytes 3145736 | tf_op jit(solution)/shard_map/ppermute | solution.py:70
  33.0 19.1 %collective-permute-start.18 = (bf16[8,512,128]{2,1,0:T(8,128)(2,1)S(1)}, bf16[8,512,128]{2,1,0:T(8,128)(2,1)S(1)}, u32[]{:S(2)}, u32[]{:S(2)}) collective-permute-start(bf16[8,512,128]{2,1,0:T(8,128)(2,1)S(1)} %shard_map.79), channel_id=1, source_target_pairs={{0,1},{1,0},{2,3},{3,2},{4,5},{5,4},{6,7},{7,6},{8,9},{9,8},{10,11... | collective-permute-start | bytes 3145736 | tf_op jit(solution)/shard_map/ppermute | solution.py:70
  38.5 19.2 %collective-permute-start.6 = (bf16[4,512,128]{2,1,0:T(8,128)(2,1)S(1)}, bf16[4,512,128]{2,1,0:T(8,128)(2,1)S(1)}, u32[]{:S(2)}, u32[]{:S(2)}) collective-permute-start(bf16[4,512,128]{2,1,0:T(8,128)(2,1)S(1)} %add_convert_fusion.2), channel_id=1, source_target_pairs={{0,1},{1,0},{2,3},{3,2},{4,5},{5,4},{6,7},{7,6},{8,9},{9,8},{10,11... | collective-permute-start | bytes 1572872 | tf_op jit(solution)/shard_map/ppermute | solution.py:70
  41.1 17.0 %collective-permute-start.4 = (bf16[4,512,128]{2,1,0:T(8,128)(2,1)S(1)}, bf16[4,512,128]{2,1,0:T(8,128)(2,1)S(1)}, u32[]{:S(2)}, u32[]{:S(2)}) collective-permute-start(bf16[4,512,128]{2,1,0:T(8,128)(2,1)S(1)} %add_convert_fusion.3), channel_id=1, source_target_pairs={{0,3},{1,2},{2,1},{3,0},{4,7},{5,6},{6,5},{7,4},{8,11},{9,10},{10,... | collective-permute-start | bytes 1572872 | tf_op jit(solution)/shard_map/ppermute | solution.py:70
  46.1 17.3 %collective-permute-start.21 = (bf16[4,512,128]{2,1,0:T(8,128)(2,1)S(1)}, bf16[4,512,128]{2,1,0:T(8,128)(2,1)S(1)}, u32[]{:S(2)}, u32[]{:S(2)}) collective-permute-start(bf16[4,512,128]{2,1,0:T(8,128)(2,1)S(1)} %add_convert_fusion), channel_id=1, source_target_pairs={{0,1},{1,0},{2,3},{3,2},{4,5},{5,4},{6,7},{7,6},{8,9},{9,8},{10,11... | collective-permute-start | bytes 1572872 | tf_op jit(solution)/shard_map/ppermute | solution.py:70
  52.3 11.3 %collective-permute-start.19 = (bf16[4,512,128]{2,1,0:T(8,128)(2,1)S(1)}, bf16[4,512,128]{2,1,0:T(8,128)(2,1)S(1)}, u32[]{:S(2)}, u32[]{:S(2)}) collective-permute-start(bf16[4,512,128]{2,1,0:T(8,128)(2,1)S(1)} %add_convert_fusion.1), channel_id=1, source_target_pairs={{0,3},{1,2},{2,1},{3,0},{4,7},{5,6},{6,5},{7,4},{8,11},{9,10},{10,... | collective-permute-start | bytes 1572872 | tf_op jit(solution)/shard_map/ppermute | solution.py:70
  58.4 10.5 %collective-permute-start.8 = (bf16[2,512,128]{2,1,0:T(8,128)(2,1)S(1)}, bf16[2,512,128]{2,1,0:T(8,128)(2,1)S(1)}, u32[]{:S(2)}, u32[]{:S(2)}) collective-permute-start(bf16[2,512,128]{2,1,0:T(8,128)(2,1)S(1)} %pad_maximum_fusion.6), channel_id=1, source_target_pairs={{0,12},{1,13},{2,14},{3,15},{4,8},{5,9},{6,10},{7,11},{8,4},{9,5},... | collective-permute-start | bytes 786440 | tf_op jit(solution)/shard_map/ppermute | solution.py:70
  58.7 10.2 %collective-permute-start.9 = (bf16[2,512,128]{2,1,0:T(8,128)(2,1)S(1)}, bf16[2,512,128]{2,1,0:T(8,128)(2,1)S(1)}, u32[]{:S(2)}, u32[]{:S(2)}) collective-permute-start(bf16[2,512,128]{2,1,0:T(8,128)(2,1)S(1)} %pad_maximum_fusion.7), channel_id=1, source_target_pairs={{0,8},{1,9},{2,10},{3,11},{4,12},{5,13},{6,14},{7,15},{8,0},{9,1},... | collective-permute-start | bytes 786440 | tf_op jit(solution)/shard_map/ppermute | solution.py:70
  60.3 9.2 %collective-permute-start.7 = (bf16[2,512,128]{2,1,0:T(8,128)(2,1)S(1)}, bf16[2,512,128]{2,1,0:T(8,128)(2,1)S(1)}, u32[]{:S(2)}, u32[]{:S(2)}) collective-permute-start(bf16[2,512,128]{2,1,0:T(8,128)(2,1)S(1)} %pad_maximum_fusion.5), channel_id=1, source_target_pairs={{0,4},{1,5},{2,6},{3,7},{4,0},{5,1},{6,2},{7,3},{8,12},{9,13},{10,... | collective-permute-start | bytes 786440 | tf_op jit(solution)/shard_map/ppermute | solution.py:70
  64.0 10.5 %collective-permute-start.23 = (bf16[2,512,128]{2,1,0:T(8,128)(2,1)S(1)}, bf16[2,512,128]{2,1,0:T(8,128)(2,1)S(1)}, u32[]{:S(2)}, u32[]{:S(2)}) collective-permute-start(bf16[2,512,128]{2,1,0:T(8,128)(2,1)S(1)} %pad_maximum_fusion.10), channel_id=1, source_target_pairs={{0,12},{1,13},{2,14},{3,15},{4,8},{5,9},{6,10},{7,11},{8,4},{9,5},... | collective-permute-start | bytes 786440 | tf_op jit(solution)/shard_map/ppermute | solution.py:70
  64.3 10.2 %collective-permute-start.24 = (bf16[2,512,128]{2,1,0:T(8,128)(2,1)S(1)}, bf16[2,512,128]{2,1,0:T(8,128)(2,1)S(1)}, u32[]{:S(2)}, u32[]{:S(2)}) collective-permute-start(bf16[2,512,128]{2,1,0:T(8,128)(2,1)S(1)} %pad_maximum_fusion.11), channel_id=1, source_target_pairs={{0,8},{1,9},{2,10},{3,11},{4,12},{5,13},{6,14},{7,15},{8,0},{9,1},... | collective-permute-start | bytes 786440 | tf_op jit(solution)/shard_map/ppermute | solution.py:70
  69.8 11.5 %collective-permute-start.12 = (bf16[2,512,128]{2,1,0:T(8,128)(2,1)S(1)}, bf16[2,512,128]{2,1,0:T(8,128)(2,1)S(1)}, u32[]{:S(2)}, u32[]{:S(2)}) collective-permute-start(bf16[2,512,128]{2,1,0:T(8,128)(2,1)S(1)} %get-tuple-element.22), channel_id=1, source_target_pairs={{0,12},{1,13},{2,14},{3,15},{4,8},{5,9},{6,10},{7,11},{8,4},{9,5},... | collective-permute-start | bytes 786440 | tf_op jit(solution)/shard_map/ppermute | solution.py:70
  70.3 10.8 %collective-permute-start.11 = (bf16[2,512,128]{2,1,0:T(8,128)(2,1)S(1)}, bf16[2,512,128]{2,1,0:T(8,128)(2,1)S(1)}, u32[]{:S(2)}, u32[]{:S(2)}) collective-permute-start(bf16[2,512,128]{2,1,0:T(8,128)(2,1)S(1)} %get-tuple-element.22), channel_id=1, source_target_pairs={{0,8},{1,9},{2,10},{3,11},{4,12},{5,13},{6,14},{7,15},{8,0},{9,1},... | collective-permute-start | bytes 786440 | tf_op jit(solution)/shard_map/ppermute | solution.py:70
  74.5 6.2 %collective-permute-start.10 = (bf16[2,512,128]{2,1,0:T(8,128)(2,1)S(1)}, bf16[2,512,128]{2,1,0:T(8,128)(2,1)S(1)}, u32[]{:S(2)}, u32[]{:S(2)}) collective-permute-start(bf16[2,512,128]{2,1,0:T(8,128)(2,1)S(1)} %get-tuple-element.22), channel_id=1, source_target_pairs={{0,4},{1,5},{2,6},{3,7},{4,0},{5,1},{6,2},{7,3},{8,12},{9,13},{10,... | collective-permute-start | bytes 786440 | tf_op jit(solution)/shard_map/ppermute | solution.py:70
  75.3 11.2 %collective-permute-start.27 = (bf16[2,512,128]{2,1,0:T(8,128)(2,1)S(1)}, bf16[2,512,128]{2,1,0:T(8,128)(2,1)S(1)}, u32[]{:S(2)}, u32[]{:S(2)}) collective-permute-start(bf16[2,512,128]{2,1,0:T(8,128)(2,1)S(1)} %fusion.11), channel_id=1, source_target_pairs={{0,12},{1,13},{2,14},{3,15},{4,8},{5,9},{6,10},{7,11},{8,4},{9,5},... | collective-permute-start | bytes 786440 | tf_op jit(solution)/shard_map/ppermute | solution.py:70
  75.9 10.5 %collective-permute-start.26 = (bf16[2,512,128]{2,1,0:T(8,128)(2,1)S(1)}, bf16[2,512,128]{2,1,0:T(8,128)(2,1)S(1)}, u32[]{:S(2)}, u32[]{:S(2)}) collective-permute-start(bf16[2,512,128]{2,1,0:T(8,128)(2,1)S(1)} %fusion.11), channel_id=1, source_target_pairs={{0,8},{1,9},{2,10},{3,11},{4,12},{5,13},{6,14},{7,15},{8,0},{9,1},... | collective-permute-start | bytes 786440 | tf_op jit(solution)/shard_map/ppermute | solution.py:70
  81.4 13.8 %collective-permute-start.13 = (bf16[4,512,128]{2,1,0:T(8,128)(2,1)S(1)}, bf16[4,512,128]{2,1,0:T(8,128)(2,1)S(1)}, u32[]{:S(2)}, u32[]{:S(2)}) collective-permute-start(bf16[4,512,128]{2,1,0:T(8,128)(2,1)S(1)} %pad_maximum_fusion), channel_id=1, source_target_pairs={{0,3},{1,2},{2,1},{3,0},{4,7},{5,6},{6,5},{7,4},{8,11},{9,10},{10,... | collective-permute-start | bytes 1572872 | tf_op jit(solution)/shard_map/ppermute | solution.py:70
  84.3 11.8 %collective-permute-start.30 = (bf16[4,512,128]{2,1,0:T(8,128)(2,1)S(1)}, bf16[4,512,128]{2,1,0:T(8,128)(2,1)S(1)}, u32[]{:S(2)}, u32[]{:S(2)}) collective-permute-start(bf16[4,512,128]{2,1,0:T(8,128)(2,1)S(1)} %pad_maximum_fusion.3), channel_id=1, source_target_pairs={{0,1},{1,0},{2,3},{3,2},{4,5},{5,4},{6,7},{7,6},{8,9},{9,8},{10,11... | collective-permute-start | bytes 1572872 | tf_op jit(solution)/shard_map/ppermute | solution.py:70
  86.7 15.1 %collective-permute-start.29 = (bf16[4,512,128]{2,1,0:T(8,128)(2,1)S(1)}, bf16[4,512,128]{2,1,0:T(8,128)(2,1)S(1)}, u32[]{:S(2)}, u32[]{:S(2)}) collective-permute-start(bf16[4,512,128]{2,1,0:T(8,128)(2,1)S(1)} %pad_maximum_fusion.2), channel_id=1, source_target_pairs={{0,1},{1,0},{2,3},{3,2},{4,5},{5,4},{6,7},{7,6},{8,9},{9,8},{10,11... | collective-permute-start | bytes 1572872 | tf_op jit(solution)/shard_map/ppermute | solution.py:70
  88.2 16.0 %collective-permute-start.28 = (bf16[4,512,128]{2,1,0:T(8,128)(2,1)S(1)}, bf16[4,512,128]{2,1,0:T(8,128)(2,1)S(1)}, u32[]{:S(2)}, u32[]{:S(2)}) collective-permute-start(bf16[4,512,128]{2,1,0:T(8,128)(2,1)S(1)} %pad_maximum_fusion.1), channel_id=1, source_target_pairs={{0,3},{1,2},{2,1},{3,0},{4,7},{5,6},{6,5},{7,4},{8,11},{9,10},{10,... | collective-permute-start | bytes 1572872 | tf_op jit(solution)/shard_map/ppermute | solution.py:70
  95.3 17.7 %collective-permute-start.14 = (bf16[8,512,128]{2,1,0:T(8,128)(2,1)S(1)}, bf16[8,512,128]{2,1,0:T(8,128)(2,1)S(1)}, u32[]{:S(2)}, u32[]{:S(2)}) collective-permute-start(bf16[8,512,128]{2,1,0:T(8,128)(2,1)S(1)} %constant_dynamic-update-slice_fusion.7.a_ref), channel_id=1, source_target_pairs={{0,1},{1,0},{2,3},{3,2},{4,5},{5,4},{6,7},{7,6},{8,9},{9,8},{10,11... | collective-permute-start | bytes 3145736 | tf_op jit(solution)/shard_map/ppermute | solution.py:70
  96.2 16.8 %collective-permute-start.31 = (bf16[8,512,128]{2,1,0:T(8,128)(2,1)S(1)}, bf16[8,512,128]{2,1,0:T(8,128)(2,1)S(1)}, u32[]{:S(2)}, u32[]{:S(2)}) collective-permute-start(bf16[8,512,128]{2,1,0:T(8,128)(2,1)S(1)} %constant_dynamic-update-slice_fusion.26.b_ref), channel_id=1, source_target_pairs={{0,3},{1,2},{2,1},{3,0},{4,7},{5,6},{6,5},{7,4},{8,11},{9,10},{10,... | collective-permute-start | bytes 3145736 | tf_op jit(solution)/shard_map/ppermute | solution.py:70
  101.9 21.5 %collective-permute-start.33 = (bf16[8,512,128]{2,1,0:T(8,128)(2,1)S(1)}, bf16[8,512,128]{2,1,0:T(8,128)(2,1)S(1)}, u32[]{:S(2)}, u32[]{:S(2)}) collective-permute-start(bf16[8,512,128]{2,1,0:T(8,128)(2,1)S(1)} %constant_dynamic-update-slice_fusion.21.b_ref), channel_id=1, source_target_pairs={{0,3},{1,2},{2,1},{3,0},{4,7},{5,6},{6,5},{7,4},{8,11},{9,10},{10,... | collective-permute-start | bytes 3145736 | tf_op jit(solution)/shard_map/ppermute | solution.py:70
  104.2 20.0 %collective-permute-start.32 = (bf16[8,512,128]{2,1,0:T(8,128)(2,1)S(1)}, bf16[8,512,128]{2,1,0:T(8,128)(2,1)S(1)}, u32[]{:S(2)}, u32[]{:S(2)}) collective-permute-start(bf16[8,512,128]{2,1,0:T(8,128)(2,1)S(1)} %constant_dynamic-update-slice_fusion.16.a_ref), channel_id=1, source_target_pairs={{0,1},{1,0},{2,3},{3,2},{4,5},{5,4},{6,7},{7,6},{8,9},{9,8},{10,11... | collective-permute-start | bytes 3145736 | tf_op jit(solution)/shard_map/ppermute | solution.py:70
  132.5 7.2 %collective-permute-start.36 = (bf16[2,64,512]{2,1,0:T(8,128)(2,1)S(1)}, bf16[2,64,512]{2,1,0:T(8,128)(2,1)S(1)}, u32[]{:S(2)}, u32[]{:S(2)}) collective-permute-start(bf16[2,64,512]{2,1,0:T(8,128)(2,1)S(1)} %pad_maximum_fusion.15), channel_id=1, source_target_pairs={{0,96},{1,97},{2,98},{3,99},{4,100},{5,101},{6,102},{7,103},{8,104... | collective-permute-start | bytes 393224 | tf_op jit(solution)/shard_map/ppermute | solution.py:70
  133.0 7.4 %collective-permute-start.37 = (bf16[2,64,512]{2,1,0:T(8,128)(2,1)S(1)}, bf16[2,64,512]{2,1,0:T(8,128)(2,1)S(1)}, u32[]{:S(2)}, u32[]{:S(2)}) collective-permute-start(bf16[2,64,512]{2,1,0:T(8,128)(2,1)S(1)} %pad_maximum_fusion.16), channel_id=1, source_target_pairs={{0,64},{1,65},{2,66},{3,67},{4,68},{5,69},{6,70},{7,71},{8,72},{9,... | collective-permute-start | bytes 393224 | tf_op jit(solution)/shard_map/ppermute | solution.py:70
  135.7 6.9 %collective-permute-start.35 = (bf16[2,64,512]{2,1,0:T(8,128)(2,1)S(1)}, bf16[2,64,512]{2,1,0:T(8,128)(2,1)S(1)}, u32[]{:S(2)}, u32[]{:S(2)}) collective-permute-start(bf16[2,64,512]{2,1,0:T(8,128)(2,1)S(1)} %pad_maximum_fusion.14), channel_id=1, source_target_pairs={{0,32},{1,33},{2,34},{3,35},{4,36},{5,37},{6,38},{7,39},{8,40},{9,... | collective-permute-start | bytes 393224 | tf_op jit(solution)/shard_map/ppermute | solution.py:70
  (10 other events, 75.0 us)
